TPU v7x, 256 devices: a whole 4x4x8 slice. The times are simulated.
256 devices in a mesh: rep: 16 (over x_lo, y, core), et: 16 (over z, x_hi).
Axes of the slice: x: 4 (x_hi: 2, x_lo: 2; x = x_hi * 2 + x_lo), y: 4, z: 8, core: 2. Of those that a mesh axis runs over, the one named last changes fastest.
Arguments:
- tokens: bfloat16 [32768, 2048], P(('rep', 'et')), parts along dimension 0, may hold values from -6 to 6
- expert_ids: int32 [32768, 2], P(('rep', 'et')), parts along dimension 0, may hold values from 0 to 7, as said below
- route_logits: float32 [32768, 2], P(('rep', 'et')), parts along dimension 0, may hold values from -3 to 3
- w_gate: bfloat16 [2, 7168, 2048], P(None, 'et'), may hold values from -0.125 to 0.125
- w_up: bfloat16 [2, 7168, 2048], P(None, 'et'), may hold values from -0.125 to 0.125
- w_down: bfloat16 [2, 7168, 2048], P(None, 'et'), may hold values from -0.0625 to 0.0625
Outputs:
- mixed: bfloat16 [32768, 2048], P(('rep', 'et')), parts along dimension 0
There are 16 independent parts, one for each index of `rep`. A program takes and returns all parts, laid end to end along the dimension named above; an argument that names none is the same for every part. Nothing has to cross between parts.
Inputs may be any that keep to these rules, and one draw needn't show every extreme that they name: `expert_ids`: each row names two different experts. Within each aligned block of 128 rows (the rows of one device), no expert is named by more than 48 rows, and experts 0 and 1 are each named by exactly 48 rows.
All inputs are finite; a program needn't handle non-finite values.
Results may differ from a plain program's by a relative error of at most 0.015.
Values may be sent and summed in bfloat16 or wider, within the bound.
No kernel may reach another device: no remote copies, remote signals or barrier semaphores. Data moves between devices by JAX's collectives and lax.ppermute only.
A program may use at most 128 MiB of HBM per device.

v0:
```python
import jax
import jax.numpy as jnp
from jax import lax
from jax.sharding import PartitionSpec as P

EXP_WIN = 2
CAP = 48


def slot_onehot(routed, capacity):
    ranking = jnp.cumsum(routed.astype(jnp.int32), axis=0) - 1
    slot_of = jnp.where(routed, ranking, capacity)
    numbers = jnp.arange(capacity, dtype=jnp.int32)
    return (slot_of.T[:, None, :] == numbers[None, :, None]).astype(jnp.bfloat16)


def experts_apply(token_rows, weights, w_gate, w_up, w_down):
    gate_act = jnp.einsum("erd,efd->erf", token_rows, w_gate, preferred_element_type=jnp.float32)
    up_act = jnp.einsum("erd,efd->erf", token_rows, w_up, preferred_element_type=jnp.float32)
    hidden = (jax.nn.silu(gate_act) * up_act).astype(jnp.bfloat16)
    expert_out = jnp.einsum("erf,efd->erd", hidden, w_down, preferred_element_type=jnp.float32)
    return (expert_out * weights.astype(jnp.float32)[..., None]).astype(jnp.bfloat16)


def body(tokens, expert_ids, route_logits, w_gate, w_up, w_down):
    tok_rows = tokens.shape[0]
    width = tokens.shape[1]
    groups = lax.axis_size("et")
    route_probs = jax.nn.softmax(route_logits, axis=-1).astype(jnp.bfloat16)
    probs_wide = route_probs.astype(jnp.float32)
    numbers = jnp.arange(EXP_WIN, dtype=jnp.int32)
    chosen = expert_ids[:, :, None] == numbers[None, None, :]
    combine = jnp.sum(jnp.where(chosen, probs_wide[:, :, None], jnp.float32(0.0)), axis=1).astype(
        jnp.bfloat16
    )
    gathered, combine_all = (
        lax.all_gather(tokens, "et", axis=0, tiled=True),
        lax.all_gather(combine, "et", axis=0, tiled=True),
    )
    routed = (combine_all > 0).reshape(groups, tok_rows, EXP_WIN)
    selector = jax.vmap(lambda block: slot_onehot(block, CAP))(routed)
    rows_grouped = gathered.reshape(groups, tok_rows, width)
    token_rows = jnp.einsum(
        "gesr,grd->egsd", selector, rows_grouped, preferred_element_type=jnp.float32
    )
    token_rows = token_rows.astype(jnp.bfloat16).reshape(EXP_WIN, groups * CAP, width)
    combine_grouped = combine_all.astype(jnp.float32).reshape(groups, tok_rows, EXP_WIN)
    weights = jnp.einsum("gesr,gre->egs", selector.astype(jnp.float32), combine_grouped)
    weights = weights.astype(jnp.bfloat16).reshape(EXP_WIN, groups * CAP)
    partial_value = experts_apply(token_rows, weights, w_gate, w_up, w_down)
    partial_grouped = partial_value.reshape(EXP_WIN, groups, CAP, width)
    placed = jnp.einsum(
        "gesr,egsd->egrd", selector, partial_grouped, preferred_element_type=jnp.float32
    )
    placed = placed.astype(jnp.bfloat16).reshape(EXP_WIN, groups * tok_rows, width)
    own_sums = lax.psum_scatter(placed, "et", scatter_dimension=1, tiled=True).astype(jnp.float32)
    return jnp.sum(own_sums, axis=0).astype(jnp.bfloat16)


def solution(mesh):
    in_specs = (
        P(("rep", "et"), None),
        P(("rep", "et"), None),
        P(("rep", "et"), None),
        P(None, "et", None),
        P(None, "et", None),
        P(None, "et", None),
    )
    out_specs = P(("rep", "et"), None)
    return jax.shard_map(body, mesh=mesh, in_specs=in_specs, out_specs=out_specs, check_vma=False)
```

profile of v0, /device:TPU:30, one launch (start us, length us, event | category | flops | bytes accessed | tf_op | source)
XLA Modules:
  0.0 479.2 jit_solution(10208628982744986797)
XLA Ops:
  6.5 0.0 all-gather.2.cloned.1.call-start
  6.5 0.7 all-gather.2.cloned.1.call-update
  7.3 0.0 reduce-scatter.2.cloned.1.call-start
  7.3 0.7 reduce_max.9
  8.0 0.7 fusion.6
  8.7 0.7 fusion.7
  9.4 0.7 fusion.5
  10.1 39.9 %all_gather.6 = bf16[2048,2]{0,1:T(2,128)(2,1)S(1)} all-gather(bf16[128,2]{0,1:T(2,128)(2,1)S(1)} %fusion.5), channel_id=1, replica_groups=mesh['rep'=16,'et'=16] {'et'}, dimensions={0}, use_global_device_ids=true | all-gather | bytes 8704 | tf_op jit(solution)/shard_map/all_gather | solution.py:38
  50.0 0.6 copy.19
  50.6 0.5 copy.18
  51.2 23.6 %select_bitcast_fusion = s32[16,2,128]{1,0,2:T(8,128)S(1)} fusion(pred[16,128,2]{2,0,1:T(8,128)(4,1)S(1)} %copy.19, s32[16,128,2]{2,0,1:T(8,128)S(1)} %copy.18), kind=kOutput, calls=%fused_computation.5 | output fusion | flops 528384 | bytes 36864 | tf_op jit(solution)/shard_map/vmap(jit(cumsum))/reduce_window_sum | solution.py:11
  74.8 0.4 copy.20
  75.2 0.3 fusion.2
  75.5 0.1 reshape.37
  75.6 71.4 %all-gather.2.cloned.1.call-done = bf16[2048,2048]{1,0:T(8,128)(2,1)} async-done(((bf16[128,2048]{1,0:T(8,128)(2,1)}), bf16[2048,2048]{1,0:T(8,128)(2,1)}) %all-gather.2.cloned.1.call-update) | async-done | bytes 8388624 | tf_op jit(solution)/shard_map/all_gather | solution.py:37
  147.0 5.2 %convert_bitcast_fusion = bf16[2,16,48,2048]{3,2,0,1:T(8,128)(2,1)S(1)} fusion(bf16[16,128,2048,1]{2,1,3,0:T(8,128)(2,1)} %bitcast.33, s32[16,2,128]{2,0,1:T(8,128)S(1)} %copy.20), kind=kOutput, calls=%fused_computation.2 | convolution fusion | flops 808648704 | bytes 14696448 | tf_op jit(solution)/shard_map/gesr,grd->egsd/dot_general | solution.py:43
  152.1 1.1 copy.22
  153.2 0.0 copy-start
  153.3 2.7 copy-done
  155.9 5.1 %fusion.10 = f32[2,768,448]{1,2,0:T(8,128)S(1)} fusion(bf16[2,768,2048]{2,1,0:T(8,128)(2,1)S(1)} %bitcast.34, bf16[2,448,2048]{2,1,0:T(8,128)(2,1)} %param.9), kind=kOutput, calls=%fused_computation.22 | convolution fusion | flops 2818572288 | bytes 12713984 | tf_op jit(solution)/shard_map/erd,efd->erf/dot_general | solution.py:18
  161.0 13.4 %multiply_convert_fusion = bf16[2,768,2048]{2,1,0:T(8,128)(2,1)} fusion(f32[2,768]{1,0:T(2,128)S(1)} %reshape.37, bf16[2,448,2048]{2,1,0:T(8,128)(2,1)} %param.11, f32[2,768,448]{1,2,0:T(8,128)S(1)} %fusion.10, bf16[2,768,2048]{2,1,0:T(8,128)(2,1)} %bitcast.35, bf16[2,448,2048]{2,1,0:T(8,128)(2,1)} %param.10), kind=kOutput, calls=%fused_computation | convolution fusion | flops 5647564800 | bytes 22681600 | tf_op jit(solution)/shard_map/erf,efd->erd/dot_general | solution.py:21
  174.4 13.0 %convolution_convert_fusion = bf16[2,16,128,2048]{3,2,1,0:T(8,128)(2,1)} fusion(bf16[2,16,48,2048]{3,2,1,0:T(8,128)(2,1)} %bitcast.36, s32[16,2,128]{2,0,1:T(8,128)S(1)} %copy.20), kind=kOutput, calls=%fused_computation.1 | convolution fusion | flops 813891584 | bytes 23085056 | tf_op jit(solution)/shard_map/gesr,egsd->egrd/dot_general | solution.py:52
  187.4 0.0 reduce-scatter.2.cloned.1.call-update
  187.5 282.6 %reduce-scatter.2.cloned.1.call-done = bf16[2,128,2048]{2,1,0:T(8,128)(2,1)} async-done(((bf16[2,2048,2048]{2,1,0:T(8,128)(2,1)}), bf16[2,128,2048]{2,1,0:T(8,128)(2,1)}) %reduce-scatter.2.cloned.1.call-update) | async-done | bytes 1048592 | tf_op jit(solution)/shard_map/reduce_scatter | solution.py:56
  470.0 2.4 reduce_sum.32
  (4 shorter events, 0.0 us)
Async XLA Ops:
  6.5 140.4 %all-gather.2.cloned.1.call-start = ((), (), s32[]{:S(2)}) async-start(), calls=%async_computation.1 | async-start | bytes 8912896 | tf_op jit(solution)/shard_map/all_gather | solution.py:37
  7.3 462.8 %reduce-scatter.2.cloned.1.call-start = ((), (), s32[]{:S(2)}) async-start(), calls=%async_computation.2 | async-start | bytes 17825792 | tf_op jit(solution)/shard_map/reduce_scatter | solution.py:56
  153.2 2.7 copy-start
Sparse Core Ops, SparseCore 0:
  9.9 136.9 all-gather.1
  187.6 282.3 reduce-scatter.1
where the time goes:
time: 482 us; the launch traced here: 479 us
  waiting for transfers between devices  355 us (74%)
  blocking collectives  39.9 us (8%)
  matrix products  37 us (8%)
  other arithmetic  28.7 us (6%)
  between operations  13.5 us (3%)
  local copies, waits for them, and re-layouts  5.43 us (1%)
    reduce_scatter x1, waiting for transfers between devices, body(): lax.psum_scatter(placed, 'et', scatter_dimension=1, tiled=True)  283 us
    all_gather x1, waiting for transfers between devices, body(): lax.all_gather(tokens, 'et', axis=0, tiled=True)  71.4 us
    all_gather x1, blocking collectives, body(): lax.all_gather(combine, 'et', axis=0, tiled=True)  39.9 us
    another operation x1, other arithmetic, slot_onehot(): ranking = jnp.cumsum(routed.astype(jnp.int32), axis=0) - 1  23.6 us
    dot_general x1, matrix products, experts_apply(): jnp.einsum('erf,efd->erd', hidden, w_down, preferred_element_type=jnp.flo...  13.4 us
    dot_general x1, matrix products, body(): jnp.einsum('gesr,egsd->egrd', selector, partial_grouped, preferred_elemen...  13 us
  transfers between devices with their start and end apart: 2, of which 2 were waited for; matrix products, arithmetic and copies ran while one was open for 6% of the time, Pallas kernels for 0%

commit v1 on v0

v1 whole, which is shorter than its diff:
```python
import jax
import jax.numpy as jnp
from jax import lax
from jax.experimental import pallas as pl
from jax.experimental.pallas import tpu as pltpu
from jax.sharding import Mesh
from jax.sharding import PartitionSpec as P

EXPERTS = 2
CAP = 48
PLANE = ("xl", "y", "xh")
VMEM = 50 * 1024 * 1024


def role_of(index):
    return (index // 2) % 2


def selector(ids, rows):
    chosen = [jnp.any(ids == e, axis=1, keepdims=True) for e in range(EXPERTS)]
    flags = jnp.concatenate([c.astype(jnp.float32) for c in chosen], axis=1)
    before = lax.broadcasted_iota(jnp.int32, (rows, rows), 1) < lax.broadcasted_iota(
        jnp.int32, (rows, rows), 0
    )
    rank = jnp.dot(before.astype(jnp.float32), flags, preferred_element_type=jnp.float32)
    slots = lax.broadcasted_iota(jnp.int32, (rows, CAP), 1).astype(jnp.float32)
    return [(rank[:, e : e + 1] == slots) & chosen[e] for e in range(EXPERTS)]


def pick_kernel(ids_ref, tokens_ref, out_ref):
    tokens = tokens_ref[...]
    marks = selector(ids_ref[...], tokens.shape[0])
    for e in range(EXPERTS):
        picked = lax.dot_general(
            marks[e].astype(jnp.bfloat16),
            tokens,
            (((0,), (0,)), ((), ())),
            preferred_element_type=jnp.float32,
        ).astype(jnp.bfloat16)
        for k in range(out_ref.shape[0]):
            if role_of(k) == e:
                out_ref[k] = picked


def pick(ids, tokens, chips):
    return pl.pallas_call(
        pick_kernel,
        out_shape=jax.ShapeDtypeStruct((chips, CAP, tokens.shape[1]), tokens.dtype),
        compiler_params=pltpu.CompilerParams(vmem_limit_bytes=VMEM),
        name="pick_rows",
    )(ids, tokens)


def pack_kernel(at_ref, gate_ref, up_ref, down_ref, out_ref, sems):
    _, rows, cols = out_ref.shape
    start = pl.multiple_of(at_ref[1] * rows, rows)
    left = pl.multiple_of(at_ref[2] * cols, cols)
    copies = [
        pltpu.make_async_copy(
            ref.at[at_ref[0], pl.ds(start, rows), pl.ds(left, cols)], out_ref.at[n], sems.at[n]
        )
        for n, ref in enumerate((gate_ref, up_ref, down_ref))
    ]
    for copy in copies:
        copy.start()
    for copy in copies:
        copy.wait()


def pack(at, w_gate, w_up, w_down, rows, cols):
    anywhere = pl.BlockSpec(memory_space=pl.ANY)
    return pl.pallas_call(
        pack_kernel,
        out_shape=jax.ShapeDtypeStruct((3, rows, cols), w_gate.dtype),
        in_specs=[pl.BlockSpec(memory_space=pltpu.SMEM)] + [anywhere] * 3,
        out_specs=anywhere,
        scratch_shapes=[pltpu.SemaphoreType.DMA((3,))],
        name="pack_weights",
    )(at, w_gate, w_up, w_down)


def ffn_kernel(
    core_ref,
    x_own,
    x_other,
    gate_own,
    gate_other,
    up_own,
    up_other,
    down_own,
    down_other,
    out_ref,
    hidden,
):
    step = pl.program_id(0)
    chunks = hidden.shape[0]

    def flat(ref, first, count):
        rows, cols = ref.shape[2:]
        return ref[first : first + count, 0].reshape(count * rows, cols)

    def project(own, other):
        dims = (((1,), (1,)), ((), ()))
        count = own.shape[0]
        return lax.dot_general(
            x_own[...], flat(own, 0, count), dims, preferred_element_type=jnp.float32
        ) + lax.dot_general(
            x_other[...], flat(other, 0, count), dims, preferred_element_type=jnp.float32
        )

    def expand(down_ref):
        count = down_ref.shape[0] // chunks
        total = None
        for c in range(chunks):
            part = jnp.dot(
                hidden[c], flat(down_ref, c * count, count), preferred_element_type=jnp.float32
            )
            total = part if total is None else total + part
        out_ref[...] = total.astype(out_ref.dtype)

    @pl.when(step < chunks)
    def _():
        gate = project(gate_own, gate_other)
        up = project(up_own, up_other)
        hidden[step] = (gate / (1.0 + jnp.exp(-gate)) * up).astype(hidden.dtype)

    last_own = chunks + (pl.num_programs(0) - chunks) // 2

    @pl.when((step >= chunks) & (step < last_own))
    def _():
        expand(down_own)

    @pl.when(step >= last_own)
    def _():
        expand(down_other)


def ffn(core, rows, own, other):
    count, width = rows.shape
    depth, _, share, half = own.shape
    chunks = 4
    tiles = 2
    each = depth // chunks

    def side(s, c):
        return jnp.where(s < chunks + tiles, c[0], 1 - c[0])

    def chunk(kind):
        return pl.BlockSpec(
            (each, 1, share, half), lambda s, c: (jnp.minimum(s, chunks - 1), kind, 0, 0)
        )

    def columns(first):
        return pl.BlockSpec(
            (depth, 1, share, half // tiles),
            lambda s, c: (0, 2, 0, jnp.clip(s - first, 0, tiles - 1)),
        )

    return pl.pallas_call(
        ffn_kernel,
        grid_spec=pltpu.PrefetchScalarGridSpec(
            num_scalar_prefetch=1,
            grid=(chunks + 2 * tiles,),
            in_specs=[
                pl.BlockSpec((count, half), lambda s, c: (0, c[0])),
                pl.BlockSpec((count, half), lambda s, c: (0, 1 - c[0])),
                chunk(0),
                chunk(0),
                chunk(1),
                chunk(1),
                columns(chunks),
                columns(chunks + tiles),
            ],
            out_specs=pl.BlockSpec(
                (count, half // tiles),
                lambda s, c: (0, side(s, c) * tiles + jnp.maximum(s - chunks, 0) % tiles),
            ),
            scratch_shapes=[pltpu.VMEM((chunks, count, each * share), rows.dtype)],
        ),
        out_shape=jax.ShapeDtypeStruct((count, width), rows.dtype),
        compiler_params=pltpu.CompilerParams(vmem_limit_bytes=VMEM),
        name="expert_ffn",
    )(core, rows, rows, own, other, own, other, own, other)


def body(tokens, expert_ids, route_logits, w_gate, w_up, w_down):
    width = tokens.shape[1]
    chips = lax.axis_size(PLANE)
    share = w_gate.shape[1] // 4
    half = width // 2
    xl, y, core = lax.axis_index("xl"), lax.axis_index("y"), lax.axis_index("c")
    at = jnp.stack([y % 2, xl * 2 + y // 2, core]).astype(jnp.int32)

    own = lax.all_gather(pack(at, w_gate, w_up, w_down, share, half), "z", axis=0, tiled=False)
    rows = lax.all_to_all(pick(expert_ids, tokens, chips), PLANE, 0, 0)
    rows = rows.reshape(chips * CAP, width)
    own, rows = lax.optimization_barrier((own, rows))
    other = lax.ppermute(own, "c", [(0, 1), (1, 0)])
    partial = ffn(core.astype(jnp.int32).reshape(1), rows, own, other)
    back = lax.all_to_all(partial.reshape(chips, CAP, width), PLANE, 0, 0)
    return mix(expert_ids, route_logits, back)


def mix_kernel(ids_ref, logits_ref, back_ref, out_ref):
    logits = logits_ref[...]
    top = jnp.max(logits, axis=1, keepdims=True)
    powers = jnp.exp(logits - top)
    probs = (powers / jnp.sum(powers, axis=1, keepdims=True)).astype(jnp.bfloat16)
    probs = probs.astype(jnp.float32)
    ids = ids_ref[...]
    marks = selector(ids, logits.shape[0])
    total = None
    for e in range(EXPERTS):
        combine = jnp.sum(jnp.where(ids == e, probs, 0.0), axis=1, keepdims=True)
        place = jnp.where(marks[e], combine, 0.0).astype(jnp.bfloat16)
        value = None
        for k in range(back_ref.shape[0]):
            if role_of(k) == e:
                term = back_ref[k].astype(jnp.float32)
                value = term if value is None else value + term
        high = value.astype(jnp.bfloat16)
        low = (value - high.astype(jnp.float32)).astype(jnp.bfloat16)
        part = jnp.dot(place, high, preferred_element_type=jnp.float32) + jnp.dot(
            place, low, preferred_element_type=jnp.float32
        )
        total = part if total is None else total + part
    out_ref[...] = total.astype(out_ref.dtype)


def mix(ids, logits, back):
    rows = ids.shape[0]
    chips, cap, width = back.shape
    tile = 512
    return pl.pallas_call(
        mix_kernel,
        grid=(width // tile,),
        in_specs=[
            pl.BlockSpec((rows, 2), lambda i: (0, 0)),
            pl.BlockSpec((rows, 2), lambda i: (0, 0)),
            pl.BlockSpec((chips, cap, tile), lambda i: (0, 0, i)),
        ],
        out_specs=pl.BlockSpec((rows, tile), lambda i: (0, i)),
        out_shape=jax.ShapeDtypeStruct((rows, width), back.dtype),
        compiler_params=pltpu.CompilerParams(vmem_limit_bytes=VMEM),
        name="mix_terms",
    )(ids, logits, back)


def solution(mesh):
    fine = Mesh(mesh.devices.reshape(2, 4, 2, 8, 2), ("xl", "y", "c", "z", "xh"))
    tokens = P(("xl", "y", "c", "z", "xh"), None)
    weights = P(None, ("z", "xh"), None)
    return jax.shard_map(
        body,
        mesh=fine,
        in_specs=(tokens,) * 3 + (weights,) * 3,
        out_specs=tokens,
        check_vma=False,
    )
```

time: 482 us -> 199 us (0.41)
  waiting for transfers between devices: 355 us -> 86.7 us
  Pallas kernels: 0 us -> 43.5 us
  matrix products: 37 us -> 0 us
  other arithmetic: 28.7 us -> 0.64 us
  starting transfers between devices: 0.04 us -> 7.35 us
    reduce_scatter x1 -> x0, waiting for transfers between devices: 283 us -> none  [body(): lax.psum_scatter(placed, 'et', scatter_dimension=1, tiled=True)]
    all_to_all x0 -> x1, waiting for transfers between devices: none -> 51.5 us  [body(): back = lax.all_to_all(partial.reshape(chips, CAP, width), PLANE, 0, 0)]
    all_gather x1, waiting for transfers between devices: 71.4 us -> 26 us  [body(): lax.all_gather(pack(at, w_gate, w_up, w_down, share, half), 'z', axis=0,...]
    pallas_call x0 -> x4, Pallas kernels: none -> 43.5 us  [the longest x1 22.8 us: pack(): pl.pallas_call(pack_kernel, out_shape=jax.ShapeDtypeStruct((3, rows, cols...]
    all_to_all x0 -> x1, blocking collectives: none -> 43 us  [body(): rows = lax.all_to_all(pick(expert_ids, tokens, chips), PLANE, 0, 0)]
    all_gather x1 -> x0, blocking collectives: 39.9 us -> none  [body(): lax.all_gather(combine, 'et', axis=0, tiled=True)]
    dot_general x5 -> x0, matrix products: 37 us -> none  [the longest x1 13.4 us: experts_apply(): jnp.einsum('erf,efd->erd', hidden, w_down, preferred_element_type=jnp.flo...]
    another operation x1, other arithmetic: 23.6 us -> 0.64 us  [body(): at = jnp.stack([y % 2, xl * 2 + y // 2, core]).astype(jnp.int32)]
  transfers between devices with their start and end apart: 2 -> 3, of which waited for: 2 -> 3; matrix products, arithmetic and copies ran while one was open for 6% -> 0% of each run, Pallas kernels for 0% -> 0%
where the time goes in v1:
time: 199 us; the launch traced here: 197 us
  waiting for transfers between devices  86.7 us (44%)
  Pallas kernels  43.5 us (22%)
  blocking collectives  43 us (22%)
  between operations  13.4 us (7%)
  starting transfers between devices  7.35 us (4%)
  local copies, waits for them, and re-layouts  2.71 us (1%)
    all_to_all x1, waiting for transfers between devices, body(): back = lax.all_to_all(partial.reshape(chips, CAP, width), PLANE, 0, 0)  51.5 us
    all_to_all x1, blocking collectives, body(): rows = lax.all_to_all(pick(expert_ids, tokens, chips), PLANE, 0, 0)  43 us
    all_gather x1, waiting for transfers between devices, body(): lax.all_gather(pack(at, w_gate, w_up, w_down, share, half), 'z', axis=0,...  26 us
    pallas_call x1, Pallas kernels, pack(): pl.pallas_call(pack_kernel, out_shape=jax.ShapeDtypeStruct((3, rows, cols...  22.8 us
    pallas_call x1, Pallas kernels, ffn(): pl.pallas_call(ffn_kernel, grid_spec=pltpu.PrefetchScalarGridSpec(num_sca...  16.4 us
    ppermute x1, waiting for transfers between devices, body(): other = lax.ppermute(own, 'c', [(0, 1), (1, 0)])  9.24 us
    all_to_all x1, starting transfers between devices, body(): back = lax.all_to_all(partial.reshape(chips, CAP, width), PLANE, 0, 0)  7.35 us
  transfers between devices with their start and end apart: 3, of which 3 were waited for; matrix products, arithmetic and copies ran while one was open for 0% of the time, Pallas kernels for 0%

profile of v1, /device:TPU:30, one launch (start us, length us, event | category | flops | bytes accessed | tf_op | source)
XLA Modules:
  0.0 197.3 jit_solution(16850043858122867413)
XLA Ops:
  6.5 0.0 all-gather.3.cloned.1.call-start
  6.5 0.6 pad_add_fusion.at_ref
  7.2 0.0 copy-start.2
  7.2 0.0 copy-start
  7.2 22.8 %pack_weights.1 = bf16[3,112,1024]{2,1,0:T(8,128)(2,1)} custom-call(s32[3]{0:T(128)} %pad_add_fusion.at_ref, bf16[2,448,2048]{2,1,0:T(8,128)(2,1)} %gate_ref.1, bf16[2,448,2048]{2,1,0:T(8,128)(2,1)} %up_ref.1, bf16[2,448,2048]{2,1,0:T(8,128)(2,1)} %down_ref.1), custom_call_target="tpu_custom_call" | custom-call | tf_op jit(solution)/shard_map/pack_weights/pallas_call | solution.py:72
  30.0 0.0 all-gather.3.cloned.1.call-update
  30.0 0.0 copy-done.2
  30.0 0.1 copy.11.ids_ref
  30.1 0.0 copy-done
  30.1 0.8 pick_rows.1
  30.9 43.0 %all_to_all.10 = bf16[16,48,2048]{2,1,0:T(8,128)(2,1)} all-to-all(bf16[16,48,2048]{2,1,0:T(8,128)(2,1)S(1)} %pick_rows.1), channel_id=1, replica_groups=mesh['xl'=2,'y'=4,'c'=2,'z'=8,'xh'=2] {'xl','y','xh'}, dimensions={0} | all-to-all | bytes 6291456 | tf_op jit(solution)/shard_map/all_to_all | solution.py:195
  73.9 26.0 %all-gather.3.cloned.1.call-done = bf16[24,112,1024]{2,1,0:T(8,128)(2,1)} async-done(((bf16[3,112,1024]{2,1,0:T(8,128)(2,1)}), bf16[24,112,1024]{2,1,0:T(8,128)(2,1)}) %all-gather.3.cloned.1.call-update) | async-done | bytes 5505040 | tf_op jit(solution)/shard_map/all_gather | solution.py:194
  99.9 0.0 collective-permute-start
  99.9 9.2 %collective-permute-done.gate_other.up_other.down_other = bf16[8,3,112,1024]{3,2,1,0:T(8,128)(2,1)S(1)} collective-permute-done((bf16[8,3,112,1024]{3,2,1,0:T(8,128)(2,1)}, bf16[8,3,112,1024]{3,2,1,0:T(8,128)(2,1)S(1)}, u32[]{:S(2)}, u32[]{:S(2)}) %collective-permute-start) | collective-permute-done | bytes 5505056 | tf_op jit(solution)/shard_map/ppermute | solution.py:198
  109.1 0.0 copy-start.1
  109.1 2.5 %copy-done.1 = bf16[8,3,112,1024]{3,2,1,0:T(8,128)(2,1)} copy-done((bf16[8,3,112,1024]{3,2,1,0:T(8,128)(2,1)}, bf16[8,3,112,1024]{3,2,1,0:T(8,128)(2,1)S(1)}, u32[]{:S(2)}) %copy-start.1) | copy-done | bytes 5505048
  111.6 16.4 %expert_ffn.1 = bf16[768,2048]{1,0:T(8,128)(2,1)} custom-call(s32[1]{0:T(128)} %bitcast.core_ref, bf16[768,2048]{1,0:T(8,128)(2,1)} %bitcast.10, bf16[768,2048]{1,0:T(8,128)(2,1)} %bitcast.11, bf16[8,3,112,1024]{3,2,1,0:T(8,128)(2,1)} %bitcast.7, bf16[8,3,112,1024]{3,2,1,0:T(8,128)(2,1)} %copy-done.1, bf16[8,3,112,1024]{3,2,1,0:T(8,128)(2,1)} %bitcast.8, ...), custom_call_target="tpu_custom_call" | custom-call | tf_op jit(solution)/shard_map/expert_ffn/pallas_call | solution.py:159
  128.0 0.0 copy-start.3
  128.0 7.3 %all-to-all-start.1 = ((bf16[16,48,2048]{2,1,0:T(8,128)(2,1)}), bf16[16,48,2048]{2,1,0:T(8,128)(2,1)S(1)}, u32[]{:S(2)}, u32[]{:S(2)}) async-start(bf16[16,48,2048]{2,1,0:T(8,128)(2,1)} %bitcast.5), calls=%async_computation.1 | async-start | bytes 6291456 | tf_op jit(solution)/shard_map/all_to_all | solution.py:200
  135.4 0.0 copy-done.3
  135.4 0.1 copy.12.logits_ref
  135.5 51.5 %all-to-all-done.1.back_ref = bf16[16,48,2048]{2,1,0:T(8,128)(2,1)S(1)} async-done(((bf16[16,48,2048]{2,1,0:T(8,128)(2,1)}), bf16[16,48,2048]{2,1,0:T(8,128)(2,1)S(1)}, u32[]{:S(2)}, u32[]{:S(2)}) %all-to-all-start.1) | async-done | bytes 3145760 | tf_op jit(solution)/shard_map/all_to_all | solution.py:200
  187.0 3.5 %mix_terms.1 = bf16[128,2048]{1,0:T(8,128)(2,1)} custom-call(s32[128,2]{1,0:T(8,128)S(1)} %copy.11.ids_ref, f32[128,2]{1,0:T(8,128)S(1)} %copy.12.logits_ref, bf16[16,48,2048]{2,1,0:T(8,128)(2,1)S(1)} %all-to-all-done.1.back_ref), custom_call_target="tpu_custom_call" | custom-call | tf_op jit(solution)/shard_map/mix_terms/pallas_call | solution.py:234
Async XLA Ops:
  6.5 93.3 %all-gather.3.cloned.1.call-start = ((), (), s32[]{:S(2)}) async-start(), calls=%async_computation.2 | async-start | bytes 6193152 | tf_op jit(solution)/shard_map/all_gather | solution.py:194
  7.2 22.8 %copy-start.2 = (s32[128,2]{0,1:T(2,128)S(1)}, s32[128,2]{0,1:T(2,128)}, u32[]{:S(2)}) copy-start(s32[128,2]{0,1:T(2,128)} %param.7) | copy-start | bytes 3076
  7.2 22.9 %copy-start = (bf16[128,2048]{1,0:T(8,128)(2,1)S(1)}, bf16[128,2048]{1,0:T(8,128)(2,1)}, u32[]{:S(2)}) copy-start(bf16[128,2048]{1,0:T(8,128)(2,1)} %tokens_ref.1) | copy-start | bytes 1572868
  99.9 9.2 %collective-permute-start = (bf16[8,3,112,1024]{3,2,1,0:T(8,128)(2,1)}, bf16[8,3,112,1024]{3,2,1,0:T(8,128)(2,1)S(1)}, u32[]{:S(2)}, u32[]{:S(2)}) collective-permute-start(bf16[8,3,112,1024]{3,2,1,0:T(8,128)(2,1)} %bitcast.6), channel_id=1, source_target_pairs={{0,16},{16,0},{1,17},{17,1},{2,18},{18,2},{3,19},{19,3},{4,20},{20... | collective-permute-start | bytes 16515080 | tf_op jit(solution)/shard_map/ppermute | solution.py:198
  109.1 2.5 %copy-start.1 = (bf16[8,3,112,1024]{3,2,1,0:T(8,128)(2,1)}, bf16[8,3,112,1024]{3,2,1,0:T(8,128)(2,1)S(1)}, u32[]{:S(2)}) copy-start(bf16[8,3,112,1024]{3,2,1,0:T(8,128)(2,1)S(1)} %collective-permute-done.gate_other.up_other.down_other) | copy-start | bytes 16515076
  128.0 7.4 %copy-start.3 = (f32[128,2]{0,1:T(2,128)S(1)}, f32[128,2]{0,1:T(2,128)}, u32[]{:S(2)}) copy-start(f32[128,2]{0,1:T(2,128)} %param.8) | copy-start | bytes 3076
  128.0 59.0 %all-to-all-start.1 = ((bf16[16,48,2048]{2,1,0:T(8,128)(2,1)}), bf16[16,48,2048]{2,1,0:T(8,128)(2,1)S(1)}, u32[]{:S(2)}, u32[]{:S(2)}) async-start(bf16[16,48,2048]{2,1,0:T(8,128)(2,1)} %bitcast.5), calls=%async_computation.1 | async-start | bytes 6291456 | tf_op jit(solution)/shard_map/all_to_all | solution.py:200
Sparse Core Ops, SparseCore 0:
  30.1 69.7 all-gather.2

commit v2 on v1

--- a/solution.py
+++ b/solution.py
@@ -9,7 +9,7 @@
 EXPERTS = 2
 CAP = 48
 PLANE = ("xl", "y", "xh")
-VMEM = 50 * 1024 * 1024
+VMEM = 60 * 1024 * 1024
 
 
 def role_of(index):
@@ -27,10 +27,18 @@
     return [(rank[:, e : e + 1] == slots) & chosen[e] for e in range(EXPERTS)]
 
 
-def pick_kernel(ids_ref, tokens_ref, out_ref):
+def pick_kernel(ids_ref, logits_ref, tokens_ref, out_ref, place_ref):
     tokens = tokens_ref[...]
-    marks = selector(ids_ref[...], tokens.shape[0])
+    ids = ids_ref[...]
+    logits = logits_ref[...]
+    top = jnp.max(logits, axis=1, keepdims=True)
+    powers = jnp.exp(logits - top)
+    probs = (powers / jnp.sum(powers, axis=1, keepdims=True)).astype(jnp.bfloat16)
+    probs = probs.astype(jnp.float32)
+    marks = selector(ids, tokens.shape[0])
     for e in range(EXPERTS):
+        combine = jnp.sum(jnp.where(ids == e, probs, 0.0), axis=1, keepdims=True)
+        place_ref[e] = jnp.where(marks[e], combine, 0.0).astype(place_ref.dtype)
         picked = lax.dot_general(
             marks[e].astype(jnp.bfloat16),
             tokens,
@@ -42,13 +50,17 @@
                 out_ref[k] = picked
 
 
-def pick(ids, tokens, chips):
+def pick(ids, logits, tokens, chips):
+    count, width = tokens.shape
     return pl.pallas_call(
         pick_kernel,
-        out_shape=jax.ShapeDtypeStruct((chips, CAP, tokens.shape[1]), tokens.dtype),
+        out_shape=[
+            jax.ShapeDtypeStruct((chips, CAP, width), tokens.dtype),
+            jax.ShapeDtypeStruct((EXPERTS, count, CAP), tokens.dtype),
+        ],
         compiler_params=pltpu.CompilerParams(vmem_limit_bytes=VMEM),
         name="pick_rows",
-    )(ids, tokens)
+    )(ids, logits, tokens)
 
 
 def pack_kernel(at_ref, gate_ref, up_ref, down_ref, out_ref, sems):
@@ -73,7 +85,7 @@
         pack_kernel,
         out_shape=jax.ShapeDtypeStruct((3, rows, cols), w_gate.dtype),
         in_specs=[pl.BlockSpec(memory_space=pltpu.SMEM)] + [anywhere] * 3,
-        out_specs=anywhere,
+        out_specs=pl.BlockSpec(memory_space=pltpu.VMEM),
         scratch_shapes=[pltpu.SemaphoreType.DMA((3,))],
         name="pack_weights",
     )(at, w_gate, w_up, w_down)
@@ -192,27 +204,19 @@
     at = jnp.stack([y % 2, xl * 2 + y // 2, core]).astype(jnp.int32)
 
     own = lax.all_gather(pack(at, w_gate, w_up, w_down, share, half), "z", axis=0, tiled=False)
-    rows = lax.all_to_all(pick(expert_ids, tokens, chips), PLANE, 0, 0)
+    picked, place = pick(expert_ids, route_logits, tokens, chips)
+    rows = lax.all_to_all(picked, PLANE, 0, 0)
     rows = rows.reshape(chips * CAP, width)
     own, rows = lax.optimization_barrier((own, rows))
     other = lax.ppermute(own, "c", [(0, 1), (1, 0)])
     partial = ffn(core.astype(jnp.int32).reshape(1), rows, own, other)
     back = lax.all_to_all(partial.reshape(chips, CAP, width), PLANE, 0, 0)
-    return mix(expert_ids, route_logits, back)
-
-
-def mix_kernel(ids_ref, logits_ref, back_ref, out_ref):
-    logits = logits_ref[...]
-    top = jnp.max(logits, axis=1, keepdims=True)
-    powers = jnp.exp(logits - top)
-    probs = (powers / jnp.sum(powers, axis=1, keepdims=True)).astype(jnp.bfloat16)
-    probs = probs.astype(jnp.float32)
-    ids = ids_ref[...]
-    marks = selector(ids, logits.shape[0])
+    return mix(place, back)
+
+
+def mix_kernel(place_ref, back_ref, out_ref):
     total = None
     for e in range(EXPERTS):
-        combine = jnp.sum(jnp.where(ids == e, probs, 0.0), axis=1, keepdims=True)
-        place = jnp.where(marks[e], combine, 0.0).astype(jnp.bfloat16)
         value = None
         for k in range(back_ref.shape[0]):
             if role_of(k) == e:
@@ -220,30 +224,29 @@
                 value = term if value is None else value + term
         high = value.astype(jnp.bfloat16)
         low = (value - high.astype(jnp.float32)).astype(jnp.bfloat16)
-        part = jnp.dot(place, high, preferred_element_type=jnp.float32) + jnp.dot(
-            place, low, preferred_element_type=jnp.float32
+        part = jnp.dot(place_ref[e], high, preferred_element_type=jnp.float32) + jnp.dot(
+            place_ref[e], low, preferred_element_type=jnp.float32
         )
         total = part if total is None else total + part
     out_ref[...] = total.astype(out_ref.dtype)
 
 
-def mix(ids, logits, back):
-    rows = ids.shape[0]
+def mix(place, back):
     chips, cap, width = back.shape
+    rows = place.shape[1]
     tile = 512
     return pl.pallas_call(
         mix_kernel,
         grid=(width // tile,),
         in_specs=[
-            pl.BlockSpec((rows, 2), lambda i: (0, 0)),
-            pl.BlockSpec((rows, 2), lambda i: (0, 0)),
+            pl.BlockSpec(place.shape, lambda i: (0, 0, 0)),
             pl.BlockSpec((chips, cap, tile), lambda i: (0, 0, i)),
         ],
         out_specs=pl.BlockSpec((rows, tile), lambda i: (0, i)),
         out_shape=jax.ShapeDtypeStruct((rows, width), back.dtype),
         compiler_params=pltpu.CompilerParams(vmem_limit_bytes=VMEM),
         name="mix_terms",
-    )(ids, logits, back)
+    )(place, back)
 
 
 def solution(mesh):

time: 199 us -> 163 us (0.82)
  waiting for transfers between devices: 86.7 us -> 31 us
  blocking collectives: 43 us -> 86.9 us
  Pallas kernels: 43.5 us -> 27.2 us
  starting transfers between devices: 7.35 us -> 0.01 us
    all_to_all x1 -> x0, waiting for transfers between devices: 51.5 us -> none  [body(): back = lax.all_to_all(partial.reshape(chips, CAP, width), PLANE, 0, 0)]
    all_to_all x1 -> x2, blocking collectives: 43 us -> 86.9 us  [the longest x1 43.7 us: body(): back = lax.all_to_all(partial.reshape(chips, CAP, width), PLANE, 0, 0)]
    pallas_call x1, Pallas kernels: 22.8 us -> 2.91 us  [pack(): pl.pallas_call(pack_kernel, out_shape=jax.ShapeDtypeStruct((3, rows, cols...]
    all_to_all x1 -> x0, starting transfers between devices: 7.35 us -> none  [body(): back = lax.all_to_all(partial.reshape(chips, CAP, width), PLANE, 0, 0)]
    all_gather x1, waiting for transfers between devices: 26 us -> 21.6 us  [body(): lax.all_gather(pack(at, w_gate, w_up, w_down, share, half), 'z', axis=0,...]
    pallas_call x1, Pallas kernels: 0.78 us -> 3.62 us  [pick(): pl.pallas_call(pick_kernel, out_shape=[jax.ShapeDtypeStruct((chips, CAP,...]
  transfers between devices with their start and end apart: 3 -> 2, of which waited for: 3 -> 2; matrix products, arithmetic and copies ran while one was open for 0% -> 1% of each run, Pallas kernels for 0% -> 2%
where the time goes in v2:
time: 163 us; the launch traced here: 161 us
  blocking collectives  86.9 us (53%)
  waiting for transfers between devices  31 us (19%)
  Pallas kernels  27.2 us (17%)
  between operations  13.4 us (8%)
    all_to_all x1, blocking collectives, body(): back = lax.all_to_all(partial.reshape(chips, CAP, width), PLANE, 0, 0)  43.7 us
    all_to_all x1, blocking collectives, body(): rows = lax.all_to_all(picked, PLANE, 0, 0)  43.2 us
    all_gather x1, waiting for transfers between devices, body(): lax.all_gather(pack(at, w_gate, w_up, w_down, share, half), 'z', axis=0,...  21.6 us
    pallas_call x1, Pallas kernels, ffn(): pl.pallas_call(ffn_kernel, grid_spec=pltpu.PrefetchScalarGridSpec(num_sca...  16.4 us
    ppermute x1, waiting for transfers between devices, body(): other = lax.ppermute(own, 'c', [(0, 1), (1, 0)])  9.37 us
    pallas_call x1, Pallas kernels, mix(): pl.pallas_call(mix_kernel, grid=(width // tile,), in_specs=[pl.BlockSpec(...  4.31 us
    pallas_call x1, Pallas kernels, pick(): pl.pallas_call(pick_kernel, out_shape=[jax.ShapeDtypeStruct((chips, CAP,...  3.62 us
  transfers between devices with their start and end apart: 2, of which 2 were waited for; matrix products, arithmetic and copies ran while one was open for 1% of the time, Pallas kernels for 2%

profile of v2, /device:TPU:30, one launch (start us, length us, event | category | flops | bytes accessed | tf_op | source)
XLA Modules:
  0.0 160.7 jit_solution(13805923279760746225)
XLA Ops:
  6.5 0.0 all-gather.3.cloned.1.call-start
  6.5 0.7 pad_add_fusion.at_ref
  7.2 0.0 copy-start
  7.2 0.0 copy-start.1
  7.2 2.9 %pack_weights.1 = bf16[3,112,1024]{2,1,0:T(8,128)(2,1)} custom-call(s32[3]{0:T(128)} %pad_add_fusion.at_ref, bf16[2,448,2048]{2,1,0:T(8,128)(2,1)} %gate_ref.1, bf16[2,448,2048]{2,1,0:T(8,128)(2,1)} %up_ref.1, bf16[2,448,2048]{2,1,0:T(8,128)(2,1)} %down_ref.1), custom_call_target="tpu_custom_call" | custom-call | tf_op jit(solution)/shard_map/pack_weights/pallas_call | solution.py:84
  10.1 0.0 all-gather.3.cloned.1.call-update
  10.1 0.0 copy-done
  10.2 0.7 copy.9.ids_ref
  10.9 0.0 copy-done.1
  10.9 0.7 copy.10.logits_ref
  11.6 3.6 %pick_rows.1 = (bf16[16,48,2048]{2,1,0:T(8,128)(2,1)}, bf16[2,128,48]{2,1,0:T(8,128)(2,1)}) custom-call(s32[128,2]{1,0:T(8,128)} %copy.9.ids_ref, f32[128,2]{1,0:T(8,128)} %copy.10.logits_ref, bf16[128,2048]{1,0:T(8,128)(2,1)} %tokens_ref.1), custom_call_target="tpu_custom_call" | custom-call | tf_op jit(solution)/shard_map/pick_rows/pallas_call | solution.py:55
  15.3 43.2 %all_to_all.10 = bf16[16,48,2048]{2,1,0:T(8,128)(2,1)} all-to-all(bf16[16,48,2048]{2,1,0:T(8,128)(2,1)} %get-tuple-element.10), channel_id=1, replica_groups=mesh['xl'=2,'y'=4,'c'=2,'z'=8,'xh'=2] {'xl','y','xh'}, dimensions={0} | all-to-all | bytes 6291456 | tf_op jit(solution)/shard_map/all_to_all | solution.py:208
  58.5 21.6 %all-gather.3.cloned.1.call-done = bf16[24,112,1024]{2,1,0:T(8,128)(2,1)} async-done(((bf16[3,112,1024]{2,1,0:T(8,128)(2,1)}), bf16[24,112,1024]{2,1,0:T(8,128)(2,1)}) %all-gather.3.cloned.1.call-update) | async-done | bytes 5505040 | tf_op jit(solution)/shard_map/all_gather | solution.py:206
  80.0 0.0 collective-permute-start
  80.0 9.4 %collective-permute-done.gate_other.up_other.down_other = bf16[8,3,112,1024]{3,2,1,0:T(8,128)(2,1)} collective-permute-done((bf16[8,3,112,1024]{3,2,1,0:T(8,128)(2,1)}, bf16[8,3,112,1024]{3,2,1,0:T(8,128)(2,1)}, u32[]{:S(2)}, u32[]{:S(2)}) %collective-permute-start) | collective-permute-done | bytes 5505056 | tf_op jit(solution)/shard_map/ppermute | solution.py:211
  89.4 16.4 %expert_ffn.1 = bf16[768,2048]{1,0:T(8,128)(2,1)} custom-call(s32[1]{0:T(128)} %bitcast.core_ref, bf16[768,2048]{1,0:T(8,128)(2,1)} %bitcast.10, bf16[768,2048]{1,0:T(8,128)(2,1)} %bitcast.11, bf16[8,3,112,1024]{3,2,1,0:T(8,128)(2,1)} %bitcast.7, bf16[8,3,112,1024]{3,2,1,0:T(8,128)(2,1)} %collective-permute-done.gate_other.up_other.down_other, ...), custom_call_target="tpu_custom_call" | custom-call | tf_op jit(solution)/shard_map/expert_ffn/pallas_call | solution.py:171
  105.8 43.7 %all_to_all.11.back_ref = bf16[16,48,2048]{2,1,0:T(8,128)(2,1)} all-to-all(bf16[16,48,2048]{2,1,0:T(8,128)(2,1)} %bitcast.12), channel_id=1, replica_groups=mesh['xl'=2,'y'=4,'c'=2,'z'=8,'xh'=2] {'xl','y','xh'}, dimensions={0} | all-to-all | bytes 6291456 | tf_op jit(solution)/shard_map/all_to_all | solution.py:213
  149.5 4.3 %mix_terms.1 = bf16[128,2048]{1,0:T(8,128)(2,1)} custom-call(bf16[2,128,48]{2,1,0:T(8,128)(2,1)} %get-tuple-element.9.place_ref, bf16[16,48,2048]{2,1,0:T(8,128)(2,1)} %all_to_all.11.back_ref), custom_call_target="tpu_custom_call" | custom-call | tf_op jit(solution)/shard_map/mix_terms/pallas_call | solution.py:238
Async XLA Ops:
  6.5 73.5 %all-gather.3.cloned.1.call-start = ((), (), s32[]{:S(2)}) async-start(), calls=%async_computation.2 | async-start | bytes 6193152 | tf_op jit(solution)/shard_map/all_gather | solution.py:206
  7.2 3.0 %copy-start = (s32[128,2]{0,1:T(2,128)S(1)}, s32[128,2]{0,1:T(2,128)}, u32[]{:S(2)}) copy-start(s32[128,2]{0,1:T(2,128)} %param.7) | copy-start | bytes 3076
  7.2 3.7 %copy-start.1 = (f32[128,2]{0,1:T(2,128)S(1)}, f32[128,2]{0,1:T(2,128)}, u32[]{:S(2)}) copy-start(f32[128,2]{0,1:T(2,128)} %param.8) | copy-start | bytes 3076
  80.0 9.4 %collective-permute-start = (bf16[8,3,112,1024]{3,2,1,0:T(8,128)(2,1)}, bf16[8,3,112,1024]{3,2,1,0:T(8,128)(2,1)}, u32[]{:S(2)}, u32[]{:S(2)}) collective-permute-start(bf16[8,3,112,1024]{3,2,1,0:T(8,128)(2,1)} %bitcast.6), channel_id=1, source_target_pairs={{0,16},{16,0},{1,17},{17,1},{2,18},{18,2},{3,19},{19,3},{4,20},{20... | collective-permute-start | bytes 16515080 | tf_op jit(solution)/shard_map/ppermute | solution.py:211
Sparse Core Ops, SparseCore 0:
  10.3 69.7 all-gather.2

commit v3 on v2

v3 whole, which is shorter than its diff:
```python
import math

import jax
import jax.numpy as jnp
from jax import lax
from jax.experimental import pallas as pl
from jax.experimental.pallas import tpu as pltpu
from jax.sharding import Mesh
from jax.sharding import PartitionSpec as P

EXPERTS = 2
CAP = 48
PLANE = ("xl", "y", "xh")
VMEM = 20 * 1024 * 1024
GRANT = 30 * 1024 * 1024
LANES = 128
SIDE = 4
TILE = 256
Y_FIRST = 768


def role_of(index):
    return (index // 2) % 2


def selector(ids, rows):
    chosen = [jnp.any(ids == e, axis=1, keepdims=True) for e in range(EXPERTS)]
    flags = jnp.concatenate([c.astype(jnp.float32) for c in chosen], axis=1)
    before = lax.broadcasted_iota(jnp.int32, (rows, rows), 1) < lax.broadcasted_iota(
        jnp.int32, (rows, rows), 0
    )
    rank = jnp.dot(before.astype(jnp.float32), flags, preferred_element_type=jnp.float32)
    slots = lax.broadcasted_iota(jnp.int32, (rows, CAP), 1).astype(jnp.float32)
    return [(rank[:, e : e + 1] == slots) & chosen[e] for e in range(EXPERTS)]


def pick_kernel(ids_ref, logits_ref, tokens_ref, out_ref, place_ref):
    tokens = tokens_ref[...]
    ids = ids_ref[...]
    logits = logits_ref[...]
    top = jnp.max(logits, axis=1, keepdims=True)
    powers = jnp.exp(logits - top)
    probs = (powers / jnp.sum(powers, axis=1, keepdims=True)).astype(jnp.bfloat16)
    probs = probs.astype(jnp.float32)
    marks = selector(ids, tokens.shape[0])
    for e in range(EXPERTS):
        combine = jnp.sum(jnp.where(ids == e, probs, 0.0), axis=1, keepdims=True)
        place_ref[e] = jnp.where(marks[e], combine, 0.0).astype(place_ref.dtype)
        picked = lax.dot_general(
            marks[e].astype(jnp.bfloat16),
            tokens,
            (((0,), (0,)), ((), ())),
            preferred_element_type=jnp.float32,
        ).astype(jnp.bfloat16)
        for k in range(out_ref.shape[0]):
            if role_of(k) == e:
                out_ref[k] = picked


def pick(ids, logits, tokens, chips):
    count, width = tokens.shape
    return pl.pallas_call(
        pick_kernel,
        out_shape=[
            jax.ShapeDtypeStruct((chips, CAP, width), tokens.dtype),
            jax.ShapeDtypeStruct((EXPERTS, count, CAP), tokens.dtype),
        ],
        compiler_params=pltpu.CompilerParams(vmem_limit_bytes=VMEM),
        name="pick_rows",
    )(ids, logits, tokens)


def pack_kernel(at_ref, gate_ref, up_ref, down_ref, first_ref, last_ref, sems):
    rows = first_ref.shape[1]
    start = pl.multiple_of(at_ref[1] * rows, rows)
    spots = (first_ref.at[0], first_ref.at[1], last_ref.at[0])
    copies = [
        pltpu.make_async_copy(ref.at[at_ref[0], pl.ds(start, rows)], spots[n], sems.at[n])
        for n, ref in enumerate((gate_ref, up_ref, down_ref))
    ]
    for copy in copies:
        copy.start()
    for copy in copies:
        copy.wait()


def pack(at, w_gate, w_up, w_down, rows):
    anywhere = pl.BlockSpec(memory_space=pl.ANY)
    return pl.pallas_call(
        pack_kernel,
        out_shape=[
            jax.ShapeDtypeStruct((kinds, rows, w_gate.shape[2]), w_gate.dtype) for kinds in (2, 1)
        ],
        in_specs=[pl.BlockSpec(memory_space=pltpu.SMEM)] + [anywhere] * 3,
        out_specs=[pl.BlockSpec(memory_space=pltpu.VMEM)] * 2,
        scratch_shapes=[pltpu.SemaphoreType.DMA((3,))],
        name="pack_weights",
    )(at, w_gate, w_up, w_down)


def join_kernel(core_ref, own_ref, other_ref, out_ref):
    half = own_ref.shape[2]
    start = pl.multiple_of(core_ref[0] * half, half)
    out_ref[:, :, pl.ds(start, half)] = own_ref[...]
    out_ref[:, :, pl.ds(pl.multiple_of(half - start, half), half)] = other_ref[...]


def join(core, own, other):
    kinds, rows, half = own.shape
    whole = pl.BlockSpec(memory_space=pltpu.VMEM)
    return pl.pallas_call(
        join_kernel,
        in_specs=[pl.BlockSpec(memory_space=pltpu.SMEM), whole, whole],
        out_specs=whole,
        out_shape=jax.ShapeDtypeStruct((kinds, rows, 2 * half), own.dtype),
        compiler_params=pltpu.CompilerParams(vmem_limit_bytes=GRANT),
        name="join_halves",
    )(core, own, other)


def cost(flops, *arrays):
    return pl.CostEstimate(
        flops=flops,
        bytes_accessed=sum(math.prod(a.shape) * jnp.dtype(a.dtype).itemsize for a in arrays),
        transcendentals=0,
    )


def hidden_kernel(*refs):
    x_ref, pieces, (out_ref, held, sems) = refs[0], refs[1:-3], refs[-3:]
    _, share, width = held.shape[1:]
    copies = [
        pltpu.make_async_copy(piece, held.at[k], sems.at[k]) for k, piece in enumerate(pieces)
    ]
    for copy in copies:
        copy.start()
    x = x_ref[...]
    for k, copy in enumerate(copies):
        copy.wait()
        both = lax.dot_general(
            x,
            held[k].reshape(2 * share, width),
            (((1,), (1,)), ((), ())),
            preferred_element_type=jnp.float32,
        )
        gate, up = both[:, :share], both[:, share:]
        out_ref[k, :, :share] = (gate / (1.0 + jnp.exp(-gate)) * up).astype(out_ref.dtype)
        out_ref[k, :, share:] = jnp.zeros((x.shape[0], LANES - share), out_ref.dtype)


def hidden_units(rows, pieces):
    count, width = rows.shape
    shape = pieces[0].shape
    return pl.pallas_call(
        hidden_kernel,
        in_specs=[pl.BlockSpec(memory_space=pltpu.VMEM)]
        + [pl.BlockSpec(memory_space=pl.ANY)] * len(pieces),
        out_specs=pl.BlockSpec(memory_space=pltpu.VMEM),
        out_shape=jax.ShapeDtypeStruct((len(pieces), count, LANES), rows.dtype),
        scratch_shapes=[
            pltpu.VMEM((len(pieces),) + shape, rows.dtype),
            pltpu.SemaphoreType.DMA((len(pieces),)),
        ],
        compiler_params=pltpu.CompilerParams(vmem_limit_bytes=GRANT),
        cost_estimate=cost(4 * count * width * shape[1] * len(pieces), rows, *pieces),
        name="hidden_units",
    )(rows, *pieces)


def down_kernel(spots_ref, hidden_ref, last_ref, *refs):
    weights, out_ref = refs[:-1], refs[-1]
    share, tile = weights[0].shape[1:]
    blank = jnp.zeros((LANES - share, tile), out_ref.dtype)
    hidden = [hidden_ref[k] for k in range(hidden_ref.shape[0])]
    hidden += [last_ref[k] for k in range(last_ref.shape[0])]
    total = None
    for k in range(0, len(weights), 2):
        part = jnp.dot(
            jnp.concatenate(hidden[k : k + 2], axis=1),
            jnp.concatenate([weights[k][0], blank, weights[k + 1][0], blank], axis=0),
            preferred_element_type=jnp.float32,
        )
        total = part if total is None else total + part
    total = total.astype(out_ref.dtype)
    for k in range(SIDE * SIDE):
        out_ref[spots_ref[0, k], spots_ref[1, k]] = total[k * CAP : (k + 1) * CAP]


def down(spots, hidden, last, pieces, first, width, name):
    count = hidden.shape[1]
    share = pieces[0].shape[1]
    out_shape = jax.ShapeDtypeStruct((SIDE, SIDE, CAP, width), hidden.dtype)
    return pl.pallas_call(
        down_kernel,
        grid_spec=pltpu.PrefetchScalarGridSpec(
            num_scalar_prefetch=1,
            grid=(width // TILE,),
            in_specs=[
                pl.BlockSpec(hidden.shape, lambda s, spots: (0, 0, 0)),
                pl.BlockSpec(last.shape, lambda s, spots: (0, 0, 0)),
            ]
            + [pl.BlockSpec((1, share, TILE), lambda s, spots: (0, 0, first // TILE + s))]
            * len(pieces),
            out_specs=pl.BlockSpec((SIDE, SIDE, CAP, TILE), lambda s, spots: (0, 0, 0, s)),
        ),
        out_shape=out_shape,
        compiler_params=pltpu.CompilerParams(vmem_limit_bytes=GRANT),
        cost_estimate=cost(2 * count * width * share * len(pieces), out_shape, out_shape),
        name=name,
    )(spots, hidden, last, *pieces)


def along_z(value, depth):
    pairs = [(z, (z + 1) % depth) for z in range(depth)]
    pairs += [(depth + z, depth + (z - 1) % depth) for z in range(depth)]
    return lax.ppermute(value, ("c", "z"), pairs)


def swapped(value):
    return lax.ppermute(value, "c", [(0, 1), (1, 0)])


def along_x(value, step):
    places = [(x % 2) * 2 + x // 2 for x in range(SIDE)]
    return lax.ppermute(
        value, ("xl", "xh"), [(places[x], places[(x + step) % SIDE]) for x in range(SIDE)]
    )


def along_y(value, step):
    return lax.ppermute(value, "y", [(y, (y + step) % SIDE) for y in range(SIDE)])


def both(first, second):
    return jnp.concatenate([first, second], axis=0)


def body(tokens, expert_ids, route_logits, w_gate, w_up, w_down):
    width = tokens.shape[1]
    chips = lax.axis_size(PLANE)
    depth = lax.axis_size("z")
    share = w_gate.shape[1] // 4
    half = width // 2
    xl, xh, y = lax.axis_index("xl"), lax.axis_index("xh"), lax.axis_index("y")
    core = lax.axis_index("c").astype(jnp.int32)
    at = jnp.stack([y % 2, xl * 2 + y // 2]).astype(jnp.int32)
    sources = jnp.arange(chips, dtype=jnp.int32)
    across = (sources % 2 * 2 + sources // 8 - (xh * 2 + xl)) % SIDE
    along = (sources // 2 % SIDE - y) % SIDE
    x_spots, y_spots = jnp.stack([across, along]), jnp.stack([along, across])

    gate_up, below = pack(at, w_gate, w_up, w_down, share)
    picked, place = pick(expert_ids, route_logits, tokens, chips)
    rows = lax.all_to_all(picked, PLANE, 0, 0).reshape(chips * CAP, width)

    firsts, lasts = [gate_up], [below]
    for _ in range(depth // 2 - 1):
        gate_up, below = along_z(gate_up, depth), along_z(below, depth)
        firsts += [gate_up, swapped(gate_up)]
        lasts += [below, swapped(below)]

    def far(value):
        part = lax.dynamic_slice(value, (0, 0, core * half), value.shape[:2] + (half,))
        return along_z(part, depth)

    gate_up, below = far(gate_up), far(below)
    gate_up, below, rows = lax.optimization_barrier((gate_up, below, rows))
    hidden = hidden_units(rows, firsts)
    lasts.append(join(core.reshape(1), below, swapped(below)))
    last = hidden_units(rows, [join(core.reshape(1), gate_up, swapped(gate_up))])
    first = down(y_spots, hidden, last, lasts, 0, Y_FIRST, "down_y_first")
    first, hidden = lax.optimization_barrier((first, hidden))
    rest = down(x_spots, hidden, last, lasts, Y_FIRST, width - Y_FIRST, "down_x_first")
    return mix(at, place, home_y_first(first), home_x_first(rest))


def home_x_first(terms):
    right, left = along_x(terms[2, :2], 1), along_x(terms[2, 2:], -1)
    right = along_x(both(terms[1, :2] + right, terms[1, 2:]), 1)
    left = along_x(both(terms[3, :2], terms[3, 2:] + left), -1)
    mine = terms[0] + right + left
    return [mine[0], along_y(mine[2], 2), along_y(mine[1], 1), along_y(mine[3], -1)]


def home_y_first(terms):
    over, up, down = along_y(terms[2], 2), along_y(terms[1], 1), along_y(terms[3], -1)
    same, crossed = terms[0] + over, up + down
    pairs = [jnp.stack([same[k], crossed[k]]) for k in range(SIDE)]
    return [pairs[0]] + [along_x(pairs[k], k) for k in range(1, SIDE)]


def both(first, second):
    return jnp.concatenate([first, second], axis=0)


def mix_kernel(at_ref, place_ref, *refs):
    near, far, out_ref = refs[:SIDE], refs[SIDE:-1], refs[-1]
    role = at_ref[0]
    places = [place_ref[role], place_ref[1 - role]]

    def spread(values):
        total = None
        for place, value in zip(places, values):
            high = value.astype(jnp.bfloat16)
            low = (value - high.astype(jnp.float32)).astype(jnp.bfloat16)
            part = jnp.dot(place, high, preferred_element_type=jnp.float32) + jnp.dot(
                place, low, preferred_element_type=jnp.float32
            )
            total = part if total is None else total + part
        return total.astype(out_ref.dtype)

    def wide(value):
        return value.astype(jnp.float32)

    cut = near[0].shape[2]
    out_ref[:, :cut] = spread([sum(wide(ref[e]) for ref in near) for e in range(EXPERTS)])
    out_ref[:, cut:] = spread(
        [wide(far[2 * e][...]) + wide(far[2 * e + 1][...]) for e in range(EXPERTS)]
    )


def mix(at, place, near, far):
    rows = place.shape[1]
    width = near[0].shape[-1] + far[0].shape[-1]
    return pl.pallas_call(
        mix_kernel,
        in_specs=[pl.BlockSpec(memory_space=pltpu.SMEM)]
        + [pl.BlockSpec(memory_space=pltpu.VMEM)] * (1 + len(near) + len(far)),
        out_specs=pl.BlockSpec(memory_space=pltpu.VMEM),
        out_shape=jax.ShapeDtypeStruct((rows, width), jnp.bfloat16),
        compiler_params=pltpu.CompilerParams(vmem_limit_bytes=GRANT),
        name="mix_terms",
    )(at, place, *near, *far)


def solution(mesh):
    fine = Mesh(mesh.devices.reshape(2, 4, 2, 8, 2), ("xl", "y", "c", "z", "xh"))
    tokens = P(("xl", "y", "c", "z", "xh"), None)
    weights = P(None, ("z", "xh"), None)
    return jax.shard_map(
        body,
        mesh=fine,
        in_specs=(tokens,) * 3 + (weights,) * 3,
        out_specs=tokens,
        check_vma=False,
    )
```

time: 163 us -> 142 us (0.87); the launches traced: 161 us -> 141 us
  blocking collectives: 86.9 us -> 0 us
  waiting for transfers between devices: 31 us -> 73.4 us
  starting transfers between devices: 0.01 us -> 29.9 us
  between operations: 13.4 us -> 0.31 us
  local copies, waits for them, and re-layouts: 1.48 us -> 5.66 us
  Pallas kernels: 27.2 us -> 31.2 us
    all_to_all x2 -> x0, blocking collectives: 86.9 us -> none  [the longest x1 43.7 us: body(): back = lax.all_to_all(partial.reshape(chips, CAP, width), PLANE, 0, 0)]
    ppermute x1 -> x29, waiting for transfers between devices: 9.37 us -> 73.4 us  [the longest x8 54 us: along_z(): return lax.ppermute(value, ('c', 'z'), pairs)]
    ppermute x1 -> x29, starting transfers between devices: 0.01 us -> 22.8 us  [the longest x6 9.41 us: along_y(): lax.ppermute(value, 'y', [(y, (y + step) % SIDE) for y in range(SIDE)])]
    all_gather x1 -> x0, waiting for transfers between devices: 21.6 us -> none  [body(): lax.all_gather(pack(at, w_gate, w_up, w_down, share, half), 'z', axis=0,...]
    all_to_all x0 -> x1, starting transfers between devices: none -> 7.08 us  [body(): rows = lax.all_to_all(picked, PLANE, 0, 0).reshape(chips * CAP, width)]
    pallas_call x3 -> x8, Pallas kernels: 23.6 us -> 30.4 us  [the longest x2 14.3 us: hidden_units(): pl.pallas_call(hidden_kernel, in_specs=[pl.BlockSpec(memory_space=pltpu.V...]
    dynamic_slice x0 -> x2, local copies, waits for them, and re-layouts: none -> 2.78 us  [far(): lax.dynamic_slice(value, (0, 0, core * half), value.shape[:2] + (half,))]
    pallas_call x1, Pallas kernels: 3.62 us -> 0.85 us  [pick(): pl.pallas_call(pick_kernel, out_shape=[jax.ShapeDtypeStruct((chips, CAP,...]
  transfers between devices with their start and end apart: 2 -> 30, of which waited for: 2 -> 16; matrix products, arithmetic and copies ran while one was open for 1% -> 3% of each run, Pallas kernels for 2% -> 12%
where the time goes in v3:
time: 142 us; the launch traced here: 141 us
  waiting for transfers between devices  73.4 us (52%)
  Pallas kernels  31.2 us (22%)
  starting transfers between devices  29.9 us (21%)
  local copies, waits for them, and re-layouts  5.66 us (4%)
    ppermute x8, waiting for transfers between devices, along_z(): return lax.ppermute(value, ('c', 'z'), pairs)  54 us
    pallas_call x2, Pallas kernels, hidden_units(): pl.pallas_call(hidden_kernel, in_specs=[pl.BlockSpec(memory_space=pltpu.V...  14.3 us
    ppermute x6, waiting for transfers between devices, along_y(): lax.ppermute(value, 'y', [(y, (y + step) % SIDE) for y in range(SIDE)])  12 us
    ppermute x6, starting transfers between devices, along_y(): lax.ppermute(value, 'y', [(y, (y + step) % SIDE) for y in range(SIDE)])  9.41 us
    pallas_call x2, Pallas kernels, down(): pl.pallas_call(down_kernel, grid_spec=pltpu.PrefetchScalarGridSpec(num_sc...  8.66 us
    ppermute x7, starting transfers between devices, along_x(): lax.ppermute(value, ('xl', 'xh'), [(places[x], places[(x + step) % SIDE])...  8.56 us
    all_to_all x1, starting transfers between devices, body(): rows = lax.all_to_all(picked, PLANE, 0, 0).reshape(chips * CAP, width)  7.08 us
    ppermute x7, waiting for transfers between devices, along_x(): lax.ppermute(value, ('xl', 'xh'), [(places[x], places[(x + step) % SIDE])...  5.7 us
  transfers between devices with their start and end apart: 30, of which 16 were waited for; matrix products, arithmetic and copies ran while one was open for 3% of the time, Pallas kernels for 12%

profile of v3, /device:TPU:30, one launch (start us, length us, event | category | flops | bytes accessed | tf_op | source)
XLA Modules:
  0.0 141.4 jit_solution(11623870741731405308)
XLA Ops:
  0.0 0.6 pad_add_fusion.2.at_ref
  0.6 3.2 %pack_weights.1 = (bf16[2,112,2048]{2,1,0:T(8,128)(2,1)}, bf16[1,112,2048]{2,1,0:T(8,128)(2,1)}) custom-call(s32[2]{0:T(128)} %pad_add_fusion.2.at_ref, bf16[2,448,2048]{2,1,0:T(8,128)(2,1)} %gate_ref.1, bf16[2,448,2048]{2,1,0:T(8,128)(2,1)} %up_ref.1, bf16[2,448,2048]{2,1,0:T(8,128)(2,1)} %down_ref.1), custom_call_target="tpu_custom_call" | custom-call | tf_op jit(solution)/shard_map/pack_weights/pallas_call | solution.py:89
  3.8 2.0 %collective-permute-start = (bf16[2,112,2048]{2,1,0:T(8,128)(2,1)}, bf16[2,112,2048]{2,1,0:T(8,128)(2,1)}, u32[]{:S(2)}, u32[]{:S(2)}) collective-permute-start(bf16[2,112,2048]{2,1,0:T(8,128)(2,1)} %get-tuple-element.15.refs_1_), channel_id=1, source_target_pairs={{0,2},{2,4},{4,6},{6,8},{8,10},{10,12},{12,14},{14,0},{16,30},{18,... | collective-permute-start | bytes 2752520 | tf_op jit(solution)/shard_map/ppermute | solution.py:216
  5.8 0.1 copy.7.ids_ref
  5.9 0.1 copy.8.logits_ref
  6.0 0.8 pick_rows.1
  6.9 1.6 %copy-done = bf16[16,48,2048]{2,1,0:T(8,128)(2,1)} copy-done((bf16[16,48,2048]{2,1,0:T(8,128)(2,1)}, bf16[16,48,2048]{2,1,0:T(8,128)(2,1)S(1)}, u32[]{:S(2)}) %copy-start) | copy-done | bytes 3145752
  8.5 7.1 %all-to-all-start = ((bf16[16,48,2048]{2,1,0:T(8,128)(2,1)}), bf16[16,48,2048]{2,1,0:T(8,128)(2,1)S(1)}, u32[]{:S(2)}, u32[]{:S(2)}) async-start(bf16[16,48,2048]{2,1,0:T(8,128)(2,1)} %copy-done), calls=%async_computation | async-start | bytes 6291456 | tf_op jit(solution)/shard_map/all_to_all | solution.py:254
  15.6 5.8 %collective-permute-done.refs_2_ = bf16[2,112,2048]{2,1,0:T(8,128)(2,1)} collective-permute-done((bf16[2,112,2048]{2,1,0:T(8,128)(2,1)}, bf16[2,112,2048]{2,1,0:T(8,128)(2,1)}, u32[]{:S(2)}, u32[]{:S(2)}) %collective-permute-start) | collective-permute-done | bytes 917536 | tf_op jit(solution)/shard_map/ppermute | solution.py:216
  21.4 0.0 collective-permute-start.1
  21.4 0.0 collective-permute-start.4
  21.4 14.9 %collective-permute-done.1.refs_4_ = bf16[2,112,2048]{2,1,0:T(8,128)(2,1)} collective-permute-done((bf16[2,112,2048]{2,1,0:T(8,128)(2,1)}, bf16[2,112,2048]{2,1,0:T(8,128)(2,1)}, u32[]{:S(2)}, u32[]{:S(2)}) %collective-permute-start.1) | collective-permute-done | bytes 917536 | tf_op jit(solution)/shard_map/ppermute | solution.py:216
  36.3 0.0 collective-permute-start.2
  36.3 4.8 %collective-permute-done.4.refs_1_ = bf16[1,112,2048]{2,1,0:T(8,128)(2,1)S(1)} collective-permute-done((bf16[1,112,2048]{2,1,0:T(8,128)(2,1)}, bf16[1,112,2048]{2,1,0:T(8,128)(2,1)S(1)}, u32[]{:S(2)}, u32[]{:S(2)}) %collective-permute-start.4) | collective-permute-done | bytes 458784 | tf_op jit(solution)/shard_map/ppermute | solution.py:216
  41.1 0.8 copy-done.2
  41.9 14.2 %collective-permute-done.5.refs_3_ = bf16[1,112,2048]{2,1,0:T(8,128)(2,1)} collective-permute-done((bf16[1,112,2048]{2,1,0:T(8,128)(2,1)S(1)}, bf16[1,112,2048]{2,1,0:T(8,128)(2,1)}, u32[]{:S(2)}, u32[]{:S(2)}) %collective-permute-start.5) | collective-permute-done | bytes 458784 | tf_op jit(solution)/shard_map/ppermute | solution.py:216
  56.1 1.8 %constant_dynamic-slice_fusion.1 = bf16[2,112,1024]{2,1,0:T(8,128)(2,1)} fusion(bf16[2,112,2048]{2,1,0:T(8,128)(2,1)} %collective-permute-done.2.refs_6_, s32[]{:T(128)S(6)} %select_n.91), kind=kLoop, calls=%fused_computation.53 | loop fusion | bytes 917508 | tf_op jit(solution)/shard_map/dynamic_slice | solution.py:263
  58.0 0.7 collective-permute-start.8
  58.7 0.5 collective-permute-start.10
  59.2 7.0 %collective-permute-done.6.refs_5_ = bf16[1,112,2048]{2,1,0:T(8,128)(2,1)} collective-permute-done((bf16[1,112,2048]{2,1,0:T(8,128)(2,1)}, bf16[1,112,2048]{2,1,0:T(8,128)(2,1)}, u32[]{:S(2)}, u32[]{:S(2)}) %collective-permute-start.6) | collective-permute-done | bytes 458784 | tf_op jit(solution)/shard_map/ppermute | solution.py:216
  66.1 1.0 constant_dynamic-slice_fusion
  67.1 0.1 collective-permute-start.7
  67.2 7.2 %collective-permute-done.7.own_ref = bf16[1,112,1024]{2,1,0:T(8,128)(2,1)S(1)} collective-permute-done((bf16[1,112,1024]{2,1,0:T(8,128)(2,1)S(1)}, bf16[1,112,1024]{2,1,0:T(8,128)(2,1)S(1)}, u32[]{:S(2)}, u32[]{:S(2)}) %collective-permute-start.7) | collective-permute-done | bytes 229408 | tf_op jit(solution)/shard_map/ppermute | solution.py:216
  74.4 0.5 collective-permute-start.15
  75.0 1.7 %collective-permute-done.15.other_ref = bf16[1,112,1024]{2,1,0:T(8,128)(2,1)} collective-permute-done((bf16[1,112,1024]{2,1,0:T(8,128)(2,1)S(1)}, bf16[1,112,1024]{2,1,0:T(8,128)(2,1)}, u32[]{:S(2)}, u32[]{:S(2)}) %collective-permute-start.15) | collective-permute-done | bytes 229408 | tf_op jit(solution)/shard_map/ppermute | solution.py:220
  76.7 0.1 collective-permute-start.12
  76.8 1.0 join_halves.3.refs_7_
  77.8 0.6 collective-permute-start.13
  78.5 1.2 join_halves.2.refs_1_
  79.7 1.5 %hidden_units.3.last_ref = bf16[1,768,128]{2,1,0:T(8,128)(2,1)S(1)} custom-call(bf16[768,2048]{1,0:T(8,128)(2,1)S(1)} %bitcast.42, bf16[2,112,2048]{2,1,0:T(8,128)(2,1)S(1)} %join_halves.2.refs_1_), custom_call_target="tpu_custom_call" | custom-call | flops 704643072 | bytes 4063232 | tf_op jit(solution)/shard_map/hidden_units/pallas_call | solution.py:154
  81.2 0.0 copy-start.1
  81.2 0.2 collective-permute-start.14
  81.5 12.8 %hidden_units.2.hidden_ref = bf16[7,768,128]{2,1,0:T(8,128)(2,1)S(1)} custom-call(bf16[768,2048]{1,0:T(8,128)(2,1)S(1)} %bitcast.43, bf16[2,112,2048]{2,1,0:T(8,128)(2,1)S(1)} %copy-done.6, bf16[2,112,2048]{2,1,0:T(8,128)(2,1)} %collective-permute-done.refs_2_, bf16[2,112,2048]{2,1,0:T(8,128)(2,1)} %collective-permute-done.8.refs_3_, ...), custom_call_target="tpu_custom_call" | custom-call | flops 4932501504 | bytes 9568256 | tf_op jit(solution)/shard_map/hidden_units/pallas_call | solution.py:154
  94.3 3.6 %down_y_first.1 = bf16[4,4,48,768]{3,2,1,0:T(8,128)(2,1)S(1)} custom-call(s32[2,16]{1,0:T(2,128)S(1)} %get-tuple-element.45.spots_ref, bf16[7,768,128]{2,1,0:T(8,128)(2,1)S(1)} %hidden_units.2.hidden_ref, bf16[1,768,128]{2,1,0:T(8,128)(2,1)S(1)} %hidden_units.3.last_ref, bf16[1,112,2048]{2,1,0:T(8,128)(2,1)S(1)} %copy-done.1, ...), custom_call_target="tpu_custom_call" | custom-call | flops 1056964608 | bytes 2359296 | tf_op jit(solution)/shard_map/down_y_first/pallas_call | solution.py:193
  97.9 5.1 %down_x_first.1 = bf16[4,4,48,1280]{3,2,1,0:T(8,128)(2,1)S(1)} custom-call(s32[2,16]{1,0:T(2,128)S(1)} %get-tuple-element.44.spots_ref, bf16[7,768,128]{2,1,0:T(8,128)(2,1)S(1)} %hidden_units.2.hidden_ref, bf16[1,768,128]{2,1,0:T(8,128)(2,1)S(1)} %hidden_units.3.last_ref, bf16[1,112,2048]{2,1,0:T(8,128)(2,1)S(1)} %copy-done.1, ...), custom_call_target="tpu_custom_call" | custom-call | flops 1761607680 | bytes 3932160 | tf_op jit(solution)/shard_map/down_x_first/pallas_call | solution.py:193
  103.0 0.1 slice_bitcast_fusion.8
  103.1 0.5 collective-permute-start.22
  103.6 1.6 %collective-permute-start.24 = (bf16[2,48,1280]{2,1,0:T(8,128)(2,1)S(1)}, bf16[2,48,1280]{2,1,0:T(8,128)(2,1)S(1)}, u32[]{:S(2)}, u32[]{:S(2)}) collective-permute-start(bf16[2,48,1280]{2,1,0:T(8,128)(2,1)S(1)} %get-tuple-element.26), channel_id=1, source_target_pairs={{0,129},{128,0},{1,128},{129,1},{2,131},{130,2},{3,130},{131,3},{4... | collective-permute-start | bytes 737288 | tf_op jit(solution)/shard_map/ppermute | solution.py:225
  105.2 0.1 slice_bitcast_fusion.3
  105.3 1.3 collective-permute-start.16
  106.5 2.2 %collective-permute-start.17 = (bf16[4,48,768]{2,1,0:T(8,128)(2,1)S(1)}, bf16[4,48,768]{2,1,0:T(8,128)(2,1)S(1)}, u32[]{:S(2)}, u32[]{:S(2)}) collective-permute-start(bf16[4,48,768]{2,1,0:T(8,128)(2,1)S(1)} %get-tuple-element.31), channel_id=1, source_target_pairs={{0,32},{32,64},{64,96},{96,0},{1,33},{33,65},{65,97},{97,1},{2,34}... | collective-permute-start | bytes 884744 | tf_op jit(solution)/shard_map/ppermute | solution.py:231
  108.7 0.0 collective-permute-start.18
  108.7 2.6 %collective-permute-done.22 = bf16[2,48,1280]{2,1,0:T(8,128)(2,1)S(1)} collective-permute-done((bf16[2,48,1280]{2,1,0:T(8,128)(2,1)S(1)}, bf16[2,48,1280]{2,1,0:T(8,128)(2,1)S(1)}, u32[]{:S(2)}, u32[]{:S(2)}) %collective-permute-start.22) | collective-permute-done | bytes 245792 | tf_op jit(solution)/shard_map/ppermute | solution.py:225
  111.4 1.4 collective-permute-done.24
  112.8 0.1 fusion.3
  112.9 0.4 collective-permute-start.23
  113.3 1.8 %collective-permute-start.25 = (bf16[4,48,1280]{2,1,0:T(8,128)(2,1)S(1)}, bf16[4,48,1280]{2,1,0:T(8,128)(2,1)S(1)}, u32[]{:S(2)}, u32[]{:S(2)}) collective-permute-start(bf16[4,48,1280]{2,1,0:T(8,128)(2,1)S(1)} %pad_maximum_fusion.1), channel_id=1, source_target_pairs={{0,129},{128,0},{1,128},{129,1},{2,131},{130,2},{3,130},{131,3},{4... | collective-permute-start | bytes 1474568 | tf_op jit(solution)/shard_map/ppermute | solution.py:225
  115.1 1.7 %collective-permute-done.16 = bf16[4,48,768]{2,1,0:T(8,128)(2,1)S(1)} collective-permute-done((bf16[4,48,768]{2,1,0:T(8,128)(2,1)S(1)}, bf16[4,48,768]{2,1,0:T(8,128)(2,1)S(1)}, u32[]{:S(2)}, u32[]{:S(2)}) %collective-permute-start.16) | collective-permute-done | bytes 294944 | tf_op jit(solution)/shard_map/ppermute | solution.py:231
  116.9 2.6 %collective-permute-done.17 = bf16[4,48,768]{2,1,0:T(8,128)(2,1)S(1)} collective-permute-done((bf16[4,48,768]{2,1,0:T(8,128)(2,1)S(1)}, bf16[4,48,768]{2,1,0:T(8,128)(2,1)S(1)}, u32[]{:S(2)}, u32[]{:S(2)}) %collective-permute-start.17) | collective-permute-done | bytes 294944 | tf_op jit(solution)/shard_map/ppermute | solution.py:231
  119.4 2.4 %collective-permute-done.18 = bf16[4,48,768]{2,1,0:T(8,128)(2,1)S(1)} collective-permute-done((bf16[4,48,768]{2,1,0:T(8,128)(2,1)S(1)}, bf16[4,48,768]{2,1,0:T(8,128)(2,1)S(1)}, u32[]{:S(2)}, u32[]{:S(2)}) %collective-permute-start.18) | collective-permute-done | bytes 294944 | tf_op jit(solution)/shard_map/ppermute | solution.py:231
  121.9 0.1 add.115
  122.0 0.9 collective-permute-start.21
  122.9 2.4 %collective-permute-start.20 = (bf16[2,48,768]{2,1,0:T(8,128)(2,1)S(1)}, bf16[2,48,768]{2,1,0:T(8,128)(2,1)S(1)}, u32[]{:S(2)}, u32[]{:S(2)}) collective-permute-start(bf16[2,48,768]{2,1,0:T(8,128)(2,1)S(1)} %pad_maximum_fusion.4), channel_id=1, source_target_pairs={{0,1},{128,129},{1,0},{129,128},{2,3},{130,131},{3,2},{131,130},{4... | collective-permute-start | bytes 442376 | tf_op jit(solution)/shard_map/ppermute | solution.py:225
  125.3 1.0 collective-permute-start.19
  126.3 1.6 %collective-permute-done.25 = bf16[4,48,1280]{2,1,0:T(8,128)(2,1)S(1)} collective-permute-done((bf16[4,48,1280]{2,1,0:T(8,128)(2,1)S(1)}, bf16[4,48,1280]{2,1,0:T(8,128)(2,1)S(1)}, u32[]{:S(2)}, u32[]{:S(2)}) %collective-permute-start.25) | collective-permute-done | bytes 491552 | tf_op jit(solution)/shard_map/ppermute | solution.py:225
  128.0 0.1 fusion.1
  128.1 1.3 collective-permute-start.26
  129.4 3.8 %collective-permute-start.27 = (bf16[48,1280]{1,0:T(8,128)(2,1)S(1)}, bf16[48,1280]{1,0:T(8,128)(2,1)S(1)}, u32[]{:S(2)}, u32[]{:S(2)}) collective-permute-start(bf16[48,1280]{1,0:T(8,128)(2,1)S(1)} %get-tuple-element.33), channel_id=1, source_target_pairs={{0,32},{32,64},{64,96},{96,0},{1,33},{33,65},{65,97},{97,1},{2,34}... | collective-permute-start | bytes 368648 | tf_op jit(solution)/shard_map/ppermute | solution.py:231
  133.2 0.0 collective-permute-done.21.refs_3_
  133.3 0.7 collective-permute-start.28
  134.1 0.6 collective-permute-done.26.refs_5_
  134.6 1.0 collective-permute-done.27.refs_6_
  135.7 3.7 %collective-permute-done.28.refs_7_ = bf16[48,1280]{1,0:T(8,128)(2,1)S(1)} collective-permute-done((bf16[48,1280]{1,0:T(8,128)(2,1)S(1)}, bf16[48,1280]{1,0:T(8,128)(2,1)S(1)}, u32[]{:S(2)}, u32[]{:S(2)}) %collective-permute-start.28) | collective-permute-done | bytes 122912 | tf_op jit(solution)/shard_map/ppermute | solution.py:231
  139.4 2.0 %mix_terms.1 = bf16[128,2048]{1,0:T(8,128)(2,1)} custom-call(s32[2]{0:T(128)S(1)} %copy-done.5, bf16[2,128,48]{2,1,0:T(8,128)(2,1)S(1)} %get-tuple-element.14.place_ref, bf16[2,48,768]{2,1,0:T(8,128)(2,1)S(1)} %pad_maximum_fusion.2.refs_0_, bf16[2,48,768]{2,1,0:T(8,128)(2,1)S(1)} %collective-permute-done.19.refs_1_, ...), custom_call_target="tpu_custom_call" | custom-call | tf_op jit(solution)/shard_map/mix_terms/pallas_call | solution.py:325
  (45 shorter events, 0.4 us)
Async XLA Ops:
  0.6 5.2 %copy-start.7 = (s32[128,2]{0,1:T(2,128)S(1)}, s32[128,2]{0,1:T(2,128)}, u32[]{:S(2)}) copy-start(s32[128,2]{0,1:T(2,128)} %param.7) | copy-start | bytes 3076
  0.6 5.3 %copy-start.8 = (f32[128,2]{0,1:T(2,128)S(1)}, f32[128,2]{0,1:T(2,128)}, u32[]{:S(2)}) copy-start(f32[128,2]{0,1:T(2,128)} %param.8) | copy-start | bytes 3076
  0.6 5.4 %copy-start.4 = (bf16[128,2048]{1,0:T(8,128)(2,1)S(1)}, bf16[128,2048]{1,0:T(8,128)(2,1)}, u32[]{:S(2)}) copy-start(bf16[128,2048]{1,0:T(8,128)(2,1)} %tokens_ref.1) | copy-start | bytes 1572868
  3.8 17.6 %collective-permute-start = (bf16[2,112,2048]{2,1,0:T(8,128)(2,1)}, bf16[2,112,2048]{2,1,0:T(8,128)(2,1)}, u32[]{:S(2)}, u32[]{:S(2)}) collective-permute-start(bf16[2,112,2048]{2,1,0:T(8,128)(2,1)} %get-tuple-element.15.refs_1_), channel_id=1, source_target_pairs={{0,2},{2,4},{4,6},{6,8},{8,10},{10,12},{12,14},{14,0},{16,30},{18,... | collective-permute-start | bytes 2752520 | tf_op jit(solution)/shard_map/ppermute | solution.py:216
  6.8 1.6 %copy-start = (bf16[16,48,2048]{2,1,0:T(8,128)(2,1)}, bf16[16,48,2048]{2,1,0:T(8,128)(2,1)S(1)}, u32[]{:S(2)}) copy-start(bf16[16,48,2048]{2,1,0:T(8,128)(2,1)S(1)} %get-tuple-element.17) | copy-start | bytes 9437188
  8.5 65.9 %all-to-all-start = ((bf16[16,48,2048]{2,1,0:T(8,128)(2,1)}), bf16[16,48,2048]{2,1,0:T(8,128)(2,1)S(1)}, u32[]{:S(2)}, u32[]{:S(2)}) async-start(bf16[16,48,2048]{2,1,0:T(8,128)(2,1)} %copy-done), calls=%async_computation | async-start | bytes 6291456 | tf_op jit(solution)/shard_map/all_to_all | solution.py:254
  21.4 14.9 %collective-permute-start.1 = (bf16[2,112,2048]{2,1,0:T(8,128)(2,1)}, bf16[2,112,2048]{2,1,0:T(8,128)(2,1)}, u32[]{:S(2)}, u32[]{:S(2)}) collective-permute-start(bf16[2,112,2048]{2,1,0:T(8,128)(2,1)} %collective-permute-done.refs_2_), channel_id=1, source_target_pairs={{0,2},{2,4},{4,6},{6,8},{8,10},{10,12},{12,14},{14,0},{16,30},{18,... | collective-permute-start | bytes 2752520 | tf_op jit(solution)/shard_map/ppermute | solution.py:216
  21.4 19.7 %collective-permute-start.4 = (bf16[1,112,2048]{2,1,0:T(8,128)(2,1)}, bf16[1,112,2048]{2,1,0:T(8,128)(2,1)S(1)}, u32[]{:S(2)}, u32[]{:S(2)}) collective-permute-start(bf16[1,112,2048]{2,1,0:T(8,128)(2,1)} %get-tuple-element.16.refs_0_), channel_id=1, source_target_pairs={{0,2},{2,4},{4,6},{6,8},{8,10},{10,12},{12,14},{14,0},{16,30},{18,... | collective-permute-start | bytes 1376264 | tf_op jit(solution)/shard_map/ppermute | solution.py:216
  36.3 19.8 %collective-permute-start.2 = (bf16[2,112,2048]{2,1,0:T(8,128)(2,1)}, bf16[2,112,2048]{2,1,0:T(8,128)(2,1)}, u32[]{:S(2)}, u32[]{:S(2)}) collective-permute-start(bf16[2,112,2048]{2,1,0:T(8,128)(2,1)} %collective-permute-done.1.refs_4_), channel_id=1, source_target_pairs={{0,2},{2,4},{4,6},{6,8},{8,10},{10,12},{12,14},{14,0},{16,30},{18,... | collective-permute-start | bytes 2752520 | tf_op jit(solution)/shard_map/ppermute | solution.py:216
  41.1 0.8 copy-start.2
  41.9 14.2 %collective-permute-start.5 = (bf16[1,112,2048]{2,1,0:T(8,128)(2,1)S(1)}, bf16[1,112,2048]{2,1,0:T(8,128)(2,1)}, u32[]{:S(2)}, u32[]{:S(2)}) collective-permute-start(bf16[1,112,2048]{2,1,0:T(8,128)(2,1)S(1)} %collective-permute-done.4.refs_1_), channel_id=1, source_target_pairs={{0,2},{2,4},{4,6},{6,8},{8,10},{10,12},{12,14},{14,0},{16,30},{18,... | collective-permute-start | bytes 1376264 | tf_op jit(solution)/shard_map/ppermute | solution.py:216
  56.1 10.0 %collective-permute-start.6 = (bf16[1,112,2048]{2,1,0:T(8,128)(2,1)}, bf16[1,112,2048]{2,1,0:T(8,128)(2,1)}, u32[]{:S(2)}, u32[]{:S(2)}) collective-permute-start(bf16[1,112,2048]{2,1,0:T(8,128)(2,1)} %collective-permute-done.5.refs_3_), channel_id=1, source_target_pairs={{0,2},{2,4},{4,6},{6,8},{8,10},{10,12},{12,14},{14,0},{16,30},{18,... | collective-permute-start | bytes 1376264 | tf_op jit(solution)/shard_map/ppermute | solution.py:216
  58.0 16.4 %collective-permute-start.3 = (bf16[2,112,1024]{2,1,0:T(8,128)(2,1)}, bf16[2,112,1024]{2,1,0:T(8,128)(2,1)}, u32[]{:S(2)}, u32[]{:S(2)}) collective-permute-start(bf16[2,112,1024]{2,1,0:T(8,128)(2,1)} %constant_dynamic-slice_fusion.1), channel_id=1, source_target_pairs={{0,2},{2,4},{4,6},{6,8},{8,10},{10,12},{12,14},{14,0},{16,30},{18,... | collective-permute-start | bytes 1376264 | tf_op jit(solution)/shard_map/ppermute | solution.py:216
  58.0 23.3 %collective-permute-start.8 = (bf16[2,112,2048]{2,1,0:T(8,128)(2,1)}, bf16[2,112,2048]{2,1,0:T(8,128)(2,1)}, u32[]{:S(2)}, u32[]{:S(2)}) collective-permute-start(bf16[2,112,2048]{2,1,0:T(8,128)(2,1)} %collective-permute-done.refs_2_), channel_id=1, source_target_pairs={{0,16},{16,0},{1,17},{17,1},{2,18},{18,2},{3,19},{19,3},{4,20},{20... | collective-permute-start | bytes 2752520 | tf_op jit(solution)/shard_map/ppermute | solution.py:220
  58.7 22.8 %collective-permute-start.9 = (bf16[2,112,2048]{2,1,0:T(8,128)(2,1)}, bf16[2,112,2048]{2,1,0:T(8,128)(2,1)}, u32[]{:S(2)}, u32[]{:S(2)}) collective-permute-start(bf16[2,112,2048]{2,1,0:T(8,128)(2,1)} %collective-permute-done.1.refs_4_), channel_id=1, source_target_pairs={{0,16},{16,0},{1,17},{17,1},{2,18},{18,2},{3,19},{19,3},{4,20},{20... | collective-permute-start | bytes 2752520 | tf_op jit(solution)/shard_map/ppermute | solution.py:220
  58.7 22.8 %collective-permute-start.10 = (bf16[2,112,2048]{2,1,0:T(8,128)(2,1)}, bf16[2,112,2048]{2,1,0:T(8,128)(2,1)}, u32[]{:S(2)}, u32[]{:S(2)}) collective-permute-start(bf16[2,112,2048]{2,1,0:T(8,128)(2,1)} %collective-permute-done.2.refs_6_), channel_id=1, source_target_pairs={{0,16},{16,0},{1,17},{17,1},{2,18},{18,2},{3,19},{19,3},{4,20},{20... | collective-permute-start | bytes 2752520 | tf_op jit(solution)/shard_map/ppermute | solution.py:220
  67.1 7.3 %collective-permute-start.7 = (bf16[1,112,1024]{2,1,0:T(8,128)(2,1)S(1)}, bf16[1,112,1024]{2,1,0:T(8,128)(2,1)S(1)}, u32[]{:S(2)}, u32[]{:S(2)}) collective-permute-start(bf16[1,112,1024]{2,1,0:T(8,128)(2,1)S(1)} %constant_dynamic-slice_fusion), channel_id=1, source_target_pairs={{0,2},{2,4},{4,6},{6,8},{8,10},{10,12},{12,14},{14,0},{16,30},{18,... | collective-permute-start | bytes 688136 | tf_op jit(solution)/shard_map/ppermute | solution.py:216
  74.4 3.4 %collective-permute-start.11 = (bf16[2,112,1024]{2,1,0:T(8,128)(2,1)}, bf16[2,112,1024]{2,1,0:T(8,128)(2,1)}, u32[]{:S(2)}, u32[]{:S(2)}) collective-permute-start(bf16[2,112,1024]{2,1,0:T(8,128)(2,1)} %collective-permute-done.3.own_ref), channel_id=1, source_target_pairs={{0,16},{16,0},{1,17},{17,1},{2,18},{18,2},{3,19},{19,3},{4,20},{20... | collective-permute-start | bytes 1376264 | tf_op jit(solution)/shard_map/ppermute | solution.py:220
  74.4 2.3 %collective-permute-start.15 = (bf16[1,112,1024]{2,1,0:T(8,128)(2,1)S(1)}, bf16[1,112,1024]{2,1,0:T(8,128)(2,1)}, u32[]{:S(2)}, u32[]{:S(2)}) collective-permute-start(bf16[1,112,1024]{2,1,0:T(8,128)(2,1)S(1)} %collective-permute-done.7.own_ref), channel_id=1, source_target_pairs={{0,16},{16,0},{1,17},{17,1},{2,18},{18,2},{3,19},{19,3},{4,20},{20... | collective-permute-start | bytes 688136 | tf_op jit(solution)/shard_map/ppermute | solution.py:220
  76.7 17.6 %collective-permute-start.12 = (bf16[1,112,2048]{2,1,0:T(8,128)(2,1)}, bf16[1,112,2048]{2,1,0:T(8,128)(2,1)S(1)}, u32[]{:S(2)}, u32[]{:S(2)}) collective-permute-start(bf16[1,112,2048]{2,1,0:T(8,128)(2,1)} %copy-done.2), channel_id=1, source_target_pairs={{0,16},{16,0},{1,17},{17,1},{2,18},{18,2},{3,19},{19,3},{4,20},{20... | collective-permute-start | bytes 1376264 | tf_op jit(solution)/shard_map/ppermute | solution.py:220
  77.8 16.5 %collective-permute-start.13 = (bf16[1,112,2048]{2,1,0:T(8,128)(2,1)}, bf16[1,112,2048]{2,1,0:T(8,128)(2,1)S(1)}, u32[]{:S(2)}, u32[]{:S(2)}) collective-permute-start(bf16[1,112,2048]{2,1,0:T(8,128)(2,1)} %collective-permute-done.5.refs_3_), channel_id=1, source_target_pairs={{0,16},{16,0},{1,17},{17,1},{2,18},{18,2},{3,19},{19,3},{4,20},{20... | collective-permute-start | bytes 1376264 | tf_op jit(solution)/shard_map/ppermute | solution.py:220
  79.7 1.8 %copy-start.6 = (bf16[2,112,2048]{2,1,0:T(8,128)(2,1)S(1)}, bf16[2,112,2048]{2,1,0:T(8,128)(2,1)}, u32[]{:S(2)}) copy-start(bf16[2,112,2048]{2,1,0:T(8,128)(2,1)} %get-tuple-element.15.refs_1_) | copy-start | bytes 2752516
  81.2 13.1 %copy-start.1 = (bf16[1,112,2048]{2,1,0:T(8,128)(2,1)S(1)}, bf16[1,112,2048]{2,1,0:T(8,128)(2,1)}, u32[]{:S(2)}) copy-start(bf16[1,112,2048]{2,1,0:T(8,128)(2,1)} %get-tuple-element.16.refs_0_) | copy-start | bytes 1376260
  81.2 13.1 %copy-start.3 = (bf16[1,112,2048]{2,1,0:T(8,128)(2,1)S(1)}, bf16[1,112,2048]{2,1,0:T(8,128)(2,1)}, u32[]{:S(2)}) copy-start(bf16[1,112,2048]{2,1,0:T(8,128)(2,1)} %copy-done.2) | copy-start | bytes 1376260
  81.2 13.1 %collective-permute-start.14 = (bf16[1,112,2048]{2,1,0:T(8,128)(2,1)}, bf16[1,112,2048]{2,1,0:T(8,128)(2,1)S(1)}, u32[]{:S(2)}, u32[]{:S(2)}) collective-permute-start(bf16[1,112,2048]{2,1,0:T(8,128)(2,1)} %collective-permute-done.6.refs_5_), channel_id=1, source_target_pairs={{0,16},{16,0},{1,17},{17,1},{2,18},{18,2},{3,19},{19,3},{4,20},{20... | collective-permute-start | bytes 1376264 | tf_op jit(solution)/shard_map/ppermute | solution.py:220
  103.1 8.3 %collective-permute-start.22 = (bf16[2,48,1280]{2,1,0:T(8,128)(2,1)S(1)}, bf16[2,48,1280]{2,1,0:T(8,128)(2,1)S(1)}, u32[]{:S(2)}, u32[]{:S(2)}) collective-permute-start(bf16[2,48,1280]{2,1,0:T(8,128)(2,1)S(1)} %get-tuple-element.25), channel_id=1, source_target_pairs={{0,128},{128,1},{1,129},{129,0},{2,130},{130,3},{3,131},{131,2},{4... | collective-permute-start | bytes 737288 | tf_op jit(solution)/shard_map/ppermute | solution.py:225
  103.6 9.1 %collective-permute-start.24 = (bf16[2,48,1280]{2,1,0:T(8,128)(2,1)S(1)}, bf16[2,48,1280]{2,1,0:T(8,128)(2,1)S(1)}, u32[]{:S(2)}, u32[]{:S(2)}) collective-permute-start(bf16[2,48,1280]{2,1,0:T(8,128)(2,1)S(1)} %get-tuple-element.26), channel_id=1, source_target_pairs={{0,129},{128,0},{1,128},{129,1},{2,131},{130,2},{3,130},{131,3},{4... | collective-permute-start | bytes 737288 | tf_op jit(solution)/shard_map/ppermute | solution.py:225
  105.3 11.5 %collective-permute-start.16 = (bf16[4,48,768]{2,1,0:T(8,128)(2,1)S(1)}, bf16[4,48,768]{2,1,0:T(8,128)(2,1)S(1)}, u32[]{:S(2)}, u32[]{:S(2)}) collective-permute-start(bf16[4,48,768]{2,1,0:T(8,128)(2,1)S(1)} %get-tuple-element.29), channel_id=1, source_target_pairs={{0,64},{32,96},{64,0},{96,32},{1,65},{33,97},{65,1},{97,33},{2,66}... | collective-permute-start | bytes 884744 | tf_op jit(solution)/shard_map/ppermute | solution.py:231
  106.5 12.9 %collective-permute-start.17 = (bf16[4,48,768]{2,1,0:T(8,128)(2,1)S(1)}, bf16[4,48,768]{2,1,0:T(8,128)(2,1)S(1)}, u32[]{:S(2)}, u32[]{:S(2)}) collective-permute-start(bf16[4,48,768]{2,1,0:T(8,128)(2,1)S(1)} %get-tuple-element.31), channel_id=1, source_target_pairs={{0,32},{32,64},{64,96},{96,0},{1,33},{33,65},{65,97},{97,1},{2,34}... | collective-permute-start | bytes 884744 | tf_op jit(solution)/shard_map/ppermute | solution.py:231
  108.7 13.1 %collective-permute-start.18 = (bf16[4,48,768]{2,1,0:T(8,128)(2,1)S(1)}, bf16[4,48,768]{2,1,0:T(8,128)(2,1)S(1)}, u32[]{:S(2)}, u32[]{:S(2)}) collective-permute-start(bf16[4,48,768]{2,1,0:T(8,128)(2,1)S(1)} %get-tuple-element.30), channel_id=1, source_target_pairs={{0,96},{32,0},{64,32},{96,64},{1,97},{33,1},{65,33},{97,65},{2,98}... | collective-permute-start | bytes 884744 | tf_op jit(solution)/shard_map/ppermute | solution.py:231
  112.9 13.4 %collective-permute-start.23 = (bf16[4,48,1280]{2,1,0:T(8,128)(2,1)S(1)}, bf16[4,48,1280]{2,1,0:T(8,128)(2,1)S(1)}, u32[]{:S(2)}, u32[]{:S(2)}) collective-permute-start(bf16[4,48,1280]{2,1,0:T(8,128)(2,1)S(1)} %pad_maximum_fusion), channel_id=1, source_target_pairs={{0,128},{128,1},{1,129},{129,0},{2,130},{130,3},{3,131},{131,2},{4... | collective-permute-start | bytes 1474568 | tf_op jit(solution)/shard_map/ppermute | solution.py:225
  113.3 14.7 %collective-permute-start.25 = (bf16[4,48,1280]{2,1,0:T(8,128)(2,1)S(1)}, bf16[4,48,1280]{2,1,0:T(8,128)(2,1)S(1)}, u32[]{:S(2)}, u32[]{:S(2)}) collective-permute-start(bf16[4,48,1280]{2,1,0:T(8,128)(2,1)S(1)} %pad_maximum_fusion.1), channel_id=1, source_target_pairs={{0,129},{128,0},{1,128},{129,1},{2,131},{130,2},{3,130},{131,3},{4... | collective-permute-start | bytes 1474568 | tf_op jit(solution)/shard_map/ppermute | solution.py:225
  122.0 17.4 %copy-start.5 = (s32[2]{0:T(128)S(1)}, s32[2]{0:T(128)}, u32[]{:S(2)}) copy-start(s32[2]{0:T(128)} %pad_add_fusion.2.at_ref) | copy-start | bytes 28
  122.0 11.3 %collective-permute-start.21 = (bf16[2,48,768]{2,1,0:T(8,128)(2,1)S(1)}, bf16[2,48,768]{2,1,0:T(8,128)(2,1)S(1)}, u32[]{:S(2)}, u32[]{:S(2)}) collective-permute-start(bf16[2,48,768]{2,1,0:T(8,128)(2,1)S(1)} %pad_maximum_fusion.5), channel_id=1, source_target_pairs={{0,129},{128,0},{1,128},{129,1},{2,131},{130,2},{3,130},{131,3},{4... | collective-permute-start | bytes 442376 | tf_op jit(solution)/shard_map/ppermute | solution.py:225
  122.9 11.1 %collective-permute-start.20 = (bf16[2,48,768]{2,1,0:T(8,128)(2,1)S(1)}, bf16[2,48,768]{2,1,0:T(8,128)(2,1)S(1)}, u32[]{:S(2)}, u32[]{:S(2)}) collective-permute-start(bf16[2,48,768]{2,1,0:T(8,128)(2,1)S(1)} %pad_maximum_fusion.4), channel_id=1, source_target_pairs={{0,1},{128,129},{1,0},{129,128},{2,3},{130,131},{3,2},{131,130},{4... | collective-permute-start | bytes 442376 | tf_op jit(solution)/shard_map/ppermute | solution.py:225
  125.3 8.7 %collective-permute-start.19 = (bf16[2,48,768]{2,1,0:T(8,128)(2,1)S(1)}, bf16[2,48,768]{2,1,0:T(8,128)(2,1)S(1)}, u32[]{:S(2)}, u32[]{:S(2)}) collective-permute-start(bf16[2,48,768]{2,1,0:T(8,128)(2,1)S(1)} %pad_maximum_fusion.3), channel_id=1, source_target_pairs={{0,128},{128,1},{1,129},{129,0},{2,130},{130,3},{3,131},{131,2},{4... | collective-permute-start | bytes 442376 | tf_op jit(solution)/shard_map/ppermute | solution.py:225
  128.1 6.6 %collective-permute-start.26 = (bf16[48,1280]{1,0:T(8,128)(2,1)S(1)}, bf16[48,1280]{1,0:T(8,128)(2,1)S(1)}, u32[]{:S(2)}, u32[]{:S(2)}) collective-permute-start(bf16[48,1280]{1,0:T(8,128)(2,1)S(1)} %get-tuple-element.34), channel_id=1, source_target_pairs={{0,64},{32,96},{64,0},{96,32},{1,65},{33,97},{65,1},{97,33},{2,66}... | collective-permute-start | bytes 368648 | tf_op jit(solution)/shard_map/ppermute | solution.py:231
  129.4 6.3 %collective-permute-start.27 = (bf16[48,1280]{1,0:T(8,128)(2,1)S(1)}, bf16[48,1280]{1,0:T(8,128)(2,1)S(1)}, u32[]{:S(2)}, u32[]{:S(2)}) collective-permute-start(bf16[48,1280]{1,0:T(8,128)(2,1)S(1)} %get-tuple-element.33), channel_id=1, source_target_pairs={{0,32},{32,64},{64,96},{96,0},{1,33},{33,65},{65,97},{97,1},{2,34}... | collective-permute-start | bytes 368648 | tf_op jit(solution)/shard_map/ppermute | solution.py:231
  133.3 6.1 %collective-permute-start.28 = (bf16[48,1280]{1,0:T(8,128)(2,1)S(1)}, bf16[48,1280]{1,0:T(8,128)(2,1)S(1)}, u32[]{:S(2)}, u32[]{:S(2)}) collective-permute-start(bf16[48,1280]{1,0:T(8,128)(2,1)S(1)} %get-tuple-element.32), channel_id=1, source_target_pairs={{0,96},{32,0},{64,32},{96,64},{1,97},{33,1},{65,33},{97,65},{2,98}... | collective-permute-start | bytes 368648 | tf_op jit(solution)/shard_map/ppermute | solution.py:231

commit v4 on v3

--- a/solution.py
+++ b/solution.py
@@ -17,6 +17,7 @@
 SIDE = 4
 TILE = 256
 Y_FIRST = 768
+EARLY = 5
 
 
 def role_of(index):
@@ -98,26 +99,6 @@
     )(at, w_gate, w_up, w_down)
 
 
-def join_kernel(core_ref, own_ref, other_ref, out_ref):
-    half = own_ref.shape[2]
-    start = pl.multiple_of(core_ref[0] * half, half)
-    out_ref[:, :, pl.ds(start, half)] = own_ref[...]
-    out_ref[:, :, pl.ds(pl.multiple_of(half - start, half), half)] = other_ref[...]
-
-
-def join(core, own, other):
-    kinds, rows, half = own.shape
-    whole = pl.BlockSpec(memory_space=pltpu.VMEM)
-    return pl.pallas_call(
-        join_kernel,
-        in_specs=[pl.BlockSpec(memory_space=pltpu.SMEM), whole, whole],
-        out_specs=whole,
-        out_shape=jax.ShapeDtypeStruct((kinds, rows, 2 * half), own.dtype),
-        compiler_params=pltpu.CompilerParams(vmem_limit_bytes=GRANT),
-        name="join_halves",
-    )(core, own, other)
-
-
 def cost(flops, *arrays):
     return pl.CostEstimate(
         flops=flops,
@@ -126,88 +107,112 @@
     )
 
 
-def hidden_kernel(*refs):
-    x_ref, pieces, (out_ref, held, sems) = refs[0], refs[1:-3], refs[-3:]
-    _, share, width = held.shape[1:]
+def activate(x, weights, share):
+    both = None
+    for columns, part in weights:
+        product = lax.dot_general(
+            x[:, columns], part, (((1,), (1,)), ((), ())), preferred_element_type=jnp.float32
+        )
+        both = product if both is None else both + product
+    gate, up = both[:, :share], both[:, share:]
+    return (gate / (1.0 + jnp.exp(-gate)) * up).astype(jnp.bfloat16)
+
+
+def hidden_kernel(x_ref, *refs):
+    pieces, out_ref = refs[:-1], refs[-1]
+    _, share, width = pieces[0].shape
+    blank = jnp.zeros((x_ref.shape[0], LANES - share), out_ref.dtype)
+    for k, piece in enumerate(pieces):
+        weights = piece[...].reshape(2 * share, width)
+        units = activate(x_ref, [(slice(None), weights)], share)
+        out_ref[:, k * LANES : k * LANES + share] = units
+        out_ref[:, k * LANES + share : (k + 1) * LANES] = blank
+
+
+def hidden_units(rows, pieces):
+    count, width = rows.shape
+    share = pieces[0].shape[1]
+    whole = pl.BlockSpec(memory_space=pltpu.VMEM)
+    return pl.pallas_call(
+        hidden_kernel,
+        in_specs=[whole] * (1 + len(pieces)),
+        out_specs=whole,
+        out_shape=jax.ShapeDtypeStruct((count, len(pieces) * LANES), rows.dtype),
+        compiler_params=pltpu.CompilerParams(vmem_limit_bytes=GRANT),
+        cost_estimate=cost(4 * count * width * share * len(pieces), rows, *pieces),
+        name="hidden_units",
+    )(rows, *pieces)
+
+
+def finish_kernel(core_ref, spots_ref, x_ref, early_ref, late_ref, own_ref, other_ref, *refs):
+    weights, (below_own, below_other, first_ref, rest_ref, held, sems) = refs[:-6], refs[-6:]
+    pieces, share, width = held.shape
+    half = width // 2
+    near = pl.ds(pl.multiple_of(core_ref[0] * half, half), half)
+    distant = pl.ds(pl.multiple_of(half - core_ref[0] * half, half), half)
     copies = [
-        pltpu.make_async_copy(piece, held.at[k], sems.at[k]) for k, piece in enumerate(pieces)
+        pltpu.make_async_copy(ref.at[0], held.at[k], sems.at[k]) for k, ref in enumerate(weights)
+    ]
+    last = pieces - 1
+    copies += [
+        pltpu.make_async_copy(below_own.at[0], held.at[last, :, near], sems.at[last]),
+        pltpu.make_async_copy(below_other.at[0], held.at[last, :, distant], sems.at[last + 1]),
     ]
     for copy in copies:
         copy.start()
-    x = x_ref[...]
-    for k, copy in enumerate(copies):
+    units = activate(
+        x_ref,
+        [
+            (near, own_ref[...].reshape(2 * share, half)),
+            (distant, other_ref[...].reshape(2 * share, half)),
+        ],
+        share,
+    )
+    blank = jnp.zeros((units.shape[0], LANES - share), units.dtype)
+    hidden = jnp.concatenate([early_ref[...], late_ref[...], units, blank], axis=1)
+    for copy in copies:
         copy.wait()
-        both = lax.dot_general(
-            x,
-            held[k].reshape(2 * share, width),
-            (((1,), (1,)), ((), ())),
-            preferred_element_type=jnp.float32,
-        )
-        gate, up = both[:, :share], both[:, share:]
-        out_ref[k, :, :share] = (gate / (1.0 + jnp.exp(-gate)) * up).astype(out_ref.dtype)
-        out_ref[k, :, share:] = jnp.zeros((x.shape[0], LANES - share), out_ref.dtype)
-
-
-def hidden_units(rows, pieces):
+    gap = jnp.zeros((LANES - share, TILE), units.dtype)
+    cut = first_ref.shape[3]
+    for start in range(0, width, TILE):
+        parts = []
+        for k in range(pieces):
+            parts += [held[k, :, start : start + TILE], gap]
+        total = jnp.dot(
+            hidden, jnp.concatenate(parts, axis=0), preferred_element_type=jnp.float32
+        ).astype(units.dtype)
+        for k in range(SIDE * SIDE):
+            value = total[k * CAP : (k + 1) * CAP]
+            across, along = spots_ref[0, k], spots_ref[1, k]
+            if start < cut:
+                first_ref[along, across, :, start : start + TILE] = value
+            else:
+                rest_ref[across, along, :, start - cut : start - cut + TILE] = value
+
+
+def finish(core, spots, rows, early, late, halves, pieces, below):
     count, width = rows.shape
-    shape = pieces[0].shape
-    return pl.pallas_call(
-        hidden_kernel,
-        in_specs=[pl.BlockSpec(memory_space=pltpu.VMEM)]
-        + [pl.BlockSpec(memory_space=pl.ANY)] * len(pieces),
-        out_specs=pl.BlockSpec(memory_space=pltpu.VMEM),
-        out_shape=jax.ShapeDtypeStruct((len(pieces), count, LANES), rows.dtype),
+    share = pieces[0].shape[1]
+    whole = pl.BlockSpec(memory_space=pltpu.VMEM)
+    scalars = pl.BlockSpec(memory_space=pltpu.SMEM)
+    anywhere = pl.BlockSpec(memory_space=pltpu.HBM)
+    number = len(pieces) + 1
+    return pl.pallas_call(
+        finish_kernel,
+        in_specs=[scalars] * 2 + [whole] * 5 + [anywhere] * (number + 1),
+        out_specs=[whole] * 2,
+        out_shape=[
+            jax.ShapeDtypeStruct((SIDE, SIDE, CAP, columns), rows.dtype)
+            for columns in (Y_FIRST, width - Y_FIRST)
+        ],
         scratch_shapes=[
-            pltpu.VMEM((len(pieces),) + shape, rows.dtype),
-            pltpu.SemaphoreType.DMA((len(pieces),)),
+            pltpu.VMEM((number, share, width), rows.dtype),
+            pltpu.SemaphoreType.DMA((number + 1,)),
         ],
         compiler_params=pltpu.CompilerParams(vmem_limit_bytes=GRANT),
-        cost_estimate=cost(4 * count * width * shape[1] * len(pieces), rows, *pieces),
-        name="hidden_units",
-    )(rows, *pieces)
-
-
-def down_kernel(spots_ref, hidden_ref, last_ref, *refs):
-    weights, out_ref = refs[:-1], refs[-1]
-    share, tile = weights[0].shape[1:]
-    blank = jnp.zeros((LANES - share, tile), out_ref.dtype)
-    hidden = [hidden_ref[k] for k in range(hidden_ref.shape[0])]
-    hidden += [last_ref[k] for k in range(last_ref.shape[0])]
-    total = None
-    for k in range(0, len(weights), 2):
-        part = jnp.dot(
-            jnp.concatenate(hidden[k : k + 2], axis=1),
-            jnp.concatenate([weights[k][0], blank, weights[k + 1][0], blank], axis=0),
-            preferred_element_type=jnp.float32,
-        )
-        total = part if total is None else total + part
-    total = total.astype(out_ref.dtype)
-    for k in range(SIDE * SIDE):
-        out_ref[spots_ref[0, k], spots_ref[1, k]] = total[k * CAP : (k + 1) * CAP]
-
-
-def down(spots, hidden, last, pieces, first, width, name):
-    count = hidden.shape[1]
-    share = pieces[0].shape[1]
-    out_shape = jax.ShapeDtypeStruct((SIDE, SIDE, CAP, width), hidden.dtype)
-    return pl.pallas_call(
-        down_kernel,
-        grid_spec=pltpu.PrefetchScalarGridSpec(
-            num_scalar_prefetch=1,
-            grid=(width // TILE,),
-            in_specs=[
-                pl.BlockSpec(hidden.shape, lambda s, spots: (0, 0, 0)),
-                pl.BlockSpec(last.shape, lambda s, spots: (0, 0, 0)),
-            ]
-            + [pl.BlockSpec((1, share, TILE), lambda s, spots: (0, 0, first // TILE + s))]
-            * len(pieces),
-            out_specs=pl.BlockSpec((SIDE, SIDE, CAP, TILE), lambda s, spots: (0, 0, 0, s)),
-        ),
-        out_shape=out_shape,
-        compiler_params=pltpu.CompilerParams(vmem_limit_bytes=GRANT),
-        cost_estimate=cost(2 * count * width * share * len(pieces), out_shape, out_shape),
-        name=name,
-    )(spots, hidden, last, *pieces)
+        cost_estimate=cost(2 * count * width * share * (number + 2), rows, rows, *pieces),
+        name="finish_terms",
+    )(core, spots, rows, early, late, *halves, *pieces, *below)
 
 
 def along_z(value, depth):
@@ -247,7 +252,7 @@
     sources = jnp.arange(chips, dtype=jnp.int32)
     across = (sources % 2 * 2 + sources // 8 - (xh * 2 + xl)) % SIDE
     along = (sources // 2 % SIDE - y) % SIDE
-    x_spots, y_spots = jnp.stack([across, along]), jnp.stack([along, across])
+    spots = jnp.stack([across, along])
 
     gate_up, below = pack(at, w_gate, w_up, w_down, share)
     picked, place = pick(expert_ids, route_logits, tokens, chips)
@@ -256,6 +261,7 @@
     firsts, lasts = [gate_up], [below]
     for _ in range(depth // 2 - 1):
         gate_up, below = along_z(gate_up, depth), along_z(below, depth)
+        gate_up, below = lax.optimization_barrier((gate_up, below))
         firsts += [gate_up, swapped(gate_up)]
         lasts += [below, swapped(below)]
 
@@ -264,13 +270,19 @@
         return along_z(part, depth)
 
     gate_up, below = far(gate_up), far(below)
-    gate_up, below, rows = lax.optimization_barrier((gate_up, below, rows))
-    hidden = hidden_units(rows, firsts)
-    lasts.append(join(core.reshape(1), below, swapped(below)))
-    last = hidden_units(rows, [join(core.reshape(1), gate_up, swapped(gate_up))])
-    first = down(y_spots, hidden, last, lasts, 0, Y_FIRST, "down_y_first")
-    first, hidden = lax.optimization_barrier((first, hidden))
-    rest = down(x_spots, hidden, last, lasts, Y_FIRST, width - Y_FIRST, "down_x_first")
+    early = hidden_units(rows, firsts[:EARLY])
+    late = hidden_units(rows, firsts[EARLY:])
+    gate_up, below, early = lax.optimization_barrier((gate_up, below, early))
+    first, rest = finish(
+        core.reshape(1),
+        spots,
+        rows,
+        early,
+        late,
+        (gate_up, swapped(gate_up)),
+        lasts,
+        (below, swapped(below)),
+    )
     return mix(at, place, home_y_first(first), home_x_first(rest))
 
 

time: 142 us -> 137 us (0.965)
  the two profiles are of different devices: /device:TPU:30 before, /device:TPU:88 now
where the time goes in v4:
time: 137 us; the launch traced here: 136 us
  waiting for transfers between devices  52.7 us (38%)
  starting transfers between devices  49.9 us (36%)
  Pallas kernels  24.6 us (18%)
  local copies, waits for them, and re-layouts  7.72 us (6%)
    ppermute x8, waiting for transfers between devices, along_z(): return lax.ppermute(value, ('c', 'z'), pairs)  32.5 us
    ppermute x8, starting transfers between devices, along_z(): return lax.ppermute(value, ('c', 'z'), pairs)  22.6 us
    ppermute x6, waiting for transfers between devices, along_y(): lax.ppermute(value, 'y', [(y, (y + step) % SIDE) for y in range(SIDE)])  13 us
    ppermute x7, starting transfers between devices, along_x(): lax.ppermute(value, ('xl', 'xh'), [(places[x], places[(x + step) % SIDE])...  11 us
    pallas_call x2, Pallas kernels, hidden_units(): pl.pallas_call(hidden_kernel, in_specs=[whole] * (1 + len(pieces)), out_s...  10.2 us
    pallas_call x1, Pallas kernels, finish(): pl.pallas_call(finish_kernel, in_specs=[scalars] * 2 + [whole] * 5 + [any...  8.33 us
    ppermute x6, starting transfers between devices, along_y(): lax.ppermute(value, 'y', [(y, (y + step) % SIDE) for y in range(SIDE)])  7.44 us
    all_to_all x1, starting transfers between devices, body(): rows = lax.all_to_all(picked, PLANE, 0, 0).reshape(chips * CAP, width)  7.16 us
  transfers between devices with their start and end apart: 30, of which 9 were waited for; matrix products, arithmetic and copies ran while one was open for 3% of the time, Pallas kernels for 8%

profile of v4, /device:TPU:88, one launch (start us, length us, event | category | flops | bytes accessed | tf_op | source)
XLA Modules:
  0.0 136.3 jit_solution(16781547135464891412)
XLA Ops:
  0.0 0.6 pad_add_fusion.1.at_ref
  0.6 3.2 %pack_weights.1 = (bf16[2,112,2048]{2,1,0:T(8,128)(2,1)}, bf16[1,112,2048]{2,1,0:T(8,128)(2,1)}) custom-call(s32[2]{0:T(128)} %pad_add_fusion.1.at_ref, bf16[2,448,2048]{2,1,0:T(8,128)(2,1)} %gate_ref.1, bf16[2,448,2048]{2,1,0:T(8,128)(2,1)} %up_ref.1, bf16[2,448,2048]{2,1,0:T(8,128)(2,1)} %down_ref.1), custom_call_target="tpu_custom_call" | custom-call | tf_op jit(solution)/shard_map/pack_weights/pallas_call | solution.py:90
  3.8 2.0 %collective-permute-start = (bf16[2,112,2048]{2,1,0:T(8,128)(2,1)}, bf16[2,112,2048]{2,1,0:T(8,128)(2,1)}, u32[]{:S(2)}, u32[]{:S(2)}) collective-permute-start(bf16[2,112,2048]{2,1,0:T(8,128)(2,1)} %get-tuple-element.22.refs_0_), channel_id=1, source_target_pairs={{0,2},{2,4},{4,6},{6,8},{8,10},{10,12},{12,14},{14,0},{16,30},{18,... | collective-permute-start | bytes 2752520 | tf_op jit(solution)/shard_map/ppermute | solution.py:221
  5.8 0.1 copy.7.ids_ref
  5.9 0.1 copy.8.logits_ref
  6.0 0.8 pick_rows.1
  6.9 1.6 %copy-done = bf16[16,48,2048]{2,1,0:T(8,128)(2,1)} copy-done((bf16[16,48,2048]{2,1,0:T(8,128)(2,1)}, bf16[16,48,2048]{2,1,0:T(8,128)(2,1)S(1)}, u32[]{:S(2)}) %copy-start) | copy-done | bytes 3145752
  8.5 7.2 %all-to-all-start = ((bf16[16,48,2048]{2,1,0:T(8,128)(2,1)}), bf16[16,48,2048]{2,1,0:T(8,128)(2,1)S(1)}, u32[]{:S(2)}, u32[]{:S(2)}) async-start(bf16[16,48,2048]{2,1,0:T(8,128)(2,1)} %copy-done), calls=%async_computation | async-start | bytes 6291456 | tf_op jit(solution)/shard_map/all_to_all | solution.py:259
  15.7 3.1 %collective-permute-start.1 = (bf16[1,112,2048]{2,1,0:T(8,128)(2,1)}, bf16[1,112,2048]{2,1,0:T(8,128)(2,1)S(1)}, u32[]{:S(2)}, u32[]{:S(2)}) collective-permute-start(bf16[1,112,2048]{2,1,0:T(8,128)(2,1)} %get-tuple-element.23.refs_0_), channel_id=1, source_target_pairs={{0,2},{2,4},{4,6},{6,8},{8,10},{10,12},{12,14},{14,0},{16,30},{18,... | collective-permute-start | bytes 1376264 | tf_op jit(solution)/shard_map/ppermute | solution.py:221
  18.8 6.3 %collective-permute-done.1.refs_1_ = bf16[1,112,2048]{2,1,0:T(8,128)(2,1)S(1)} collective-permute-done((bf16[1,112,2048]{2,1,0:T(8,128)(2,1)}, bf16[1,112,2048]{2,1,0:T(8,128)(2,1)S(1)}, u32[]{:S(2)}, u32[]{:S(2)}) %collective-permute-start.1) | collective-permute-done | bytes 458784 | tf_op jit(solution)/shard_map/ppermute | solution.py:221
  25.1 0.0 collective-permute-done.refs_1_
  25.1 2.4 %collective-permute-start.2 = (bf16[2,112,2048]{2,1,0:T(8,128)(2,1)}, bf16[2,112,2048]{2,1,0:T(8,128)(2,1)}, u32[]{:S(2)}, u32[]{:S(2)}) collective-permute-start(bf16[2,112,2048]{2,1,0:T(8,128)(2,1)} %collective-permute-done.refs_1_), channel_id=1, source_target_pairs={{0,2},{2,4},{4,6},{6,8},{8,10},{10,12},{12,14},{14,0},{16,30},{18,... | collective-permute-start | bytes 2752520 | tf_op jit(solution)/shard_map/ppermute | solution.py:221
  27.5 2.2 %collective-permute-start.3 = (bf16[1,112,2048]{2,1,0:T(8,128)(2,1)S(1)}, bf16[1,112,2048]{2,1,0:T(8,128)(2,1)S(1)}, u32[]{:S(2)}, u32[]{:S(2)}) collective-permute-start(bf16[1,112,2048]{2,1,0:T(8,128)(2,1)S(1)} %collective-permute-done.1.refs_1_), channel_id=1, source_target_pairs={{0,2},{2,4},{4,6},{6,8},{8,10},{10,12},{12,14},{14,0},{16,30},{18,... | collective-permute-start | bytes 1376264 | tf_op jit(solution)/shard_map/ppermute | solution.py:221
  29.7 13.9 %collective-permute-done.3.refs_3_ = bf16[1,112,2048]{2,1,0:T(8,128)(2,1)S(1)} collective-permute-done((bf16[1,112,2048]{2,1,0:T(8,128)(2,1)S(1)}, bf16[1,112,2048]{2,1,0:T(8,128)(2,1)S(1)}, u32[]{:S(2)}, u32[]{:S(2)}) %collective-permute-start.3) | collective-permute-done | bytes 458784 | tf_op jit(solution)/shard_map/ppermute | solution.py:221
  43.6 0.0 collective-permute-done.2.refs_3_
  43.6 2.4 %collective-permute-start.4 = (bf16[2,112,2048]{2,1,0:T(8,128)(2,1)}, bf16[2,112,2048]{2,1,0:T(8,128)(2,1)}, u32[]{:S(2)}, u32[]{:S(2)}) collective-permute-start(bf16[2,112,2048]{2,1,0:T(8,128)(2,1)} %collective-permute-done.2.refs_3_), channel_id=1, source_target_pairs={{0,2},{2,4},{4,6},{6,8},{8,10},{10,12},{12,14},{14,0},{16,30},{18,... | collective-permute-start | bytes 2752520 | tf_op jit(solution)/shard_map/ppermute | solution.py:221
  46.0 0.0 collective-permute-start.8
  46.0 0.5 collective-permute-start.9
  46.5 3.4 %collective-permute-start.5 = (bf16[1,112,2048]{2,1,0:T(8,128)(2,1)S(1)}, bf16[1,112,2048]{2,1,0:T(8,128)(2,1)}, u32[]{:S(2)}, u32[]{:S(2)}) collective-permute-start(bf16[1,112,2048]{2,1,0:T(8,128)(2,1)S(1)} %collective-permute-done.3.refs_3_), channel_id=1, source_target_pairs={{0,2},{2,4},{4,6},{6,8},{8,10},{10,12},{12,14},{14,0},{16,30},{18,... | collective-permute-start | bytes 1376264 | tf_op jit(solution)/shard_map/ppermute | solution.py:221
  50.0 12.3 %collective-permute-done.5.refs_5_ = bf16[1,112,2048]{2,1,0:T(8,128)(2,1)} collective-permute-done((bf16[1,112,2048]{2,1,0:T(8,128)(2,1)S(1)}, bf16[1,112,2048]{2,1,0:T(8,128)(2,1)}, u32[]{:S(2)}, u32[]{:S(2)}) %collective-permute-start.5) | collective-permute-done | bytes 458784 | tf_op jit(solution)/shard_map/ppermute | solution.py:221
  62.3 1.8 %constant_dynamic-slice_fusion.1 = bf16[2,112,1024]{2,1,0:T(8,128)(2,1)} fusion(bf16[2,112,2048]{2,1,0:T(8,128)(2,1)} %collective-permute-done.4.refs_0_, s32[]{:T(128)S(6)} %select_n.91), kind=kLoop, calls=%fused_computation.48 | loop fusion | bytes 917508 | tf_op jit(solution)/shard_map/dynamic_slice | solution.py:269
  64.1 3.2 %collective-permute-start.6 = (bf16[2,112,1024]{2,1,0:T(8,128)(2,1)}, bf16[2,112,1024]{2,1,0:T(8,128)(2,1)}, u32[]{:S(2)}, u32[]{:S(2)}) collective-permute-start(bf16[2,112,1024]{2,1,0:T(8,128)(2,1)} %constant_dynamic-slice_fusion.1), channel_id=1, source_target_pairs={{0,2},{2,4},{4,6},{6,8},{8,10},{10,12},{12,14},{14,0},{16,30},{18,... | collective-permute-start | bytes 1376264 | tf_op jit(solution)/shard_map/ppermute | solution.py:221
  67.4 0.0 collective-permute-start.12
  67.4 1.6 %constant_dynamic-slice_fusion = bf16[1,112,1024]{2,1,0:T(8,128)(2,1)} fusion(bf16[1,112,2048]{2,1,0:T(8,128)(2,1)} %collective-permute-done.5.refs_5_, s32[]{:T(128)S(6)} %select_n.91), kind=kLoop, calls=%fused_computation.47 | loop fusion | bytes 458756 | tf_op jit(solution)/shard_map/dynamic_slice | solution.py:269
  69.0 0.5 collective-permute-start.13
  69.5 0.0 collective-permute-done.9.refs_4_
  69.5 3.8 %collective-permute-start.7 = (bf16[1,112,1024]{2,1,0:T(8,128)(2,1)}, bf16[1,112,1024]{2,1,0:T(8,128)(2,1)S(1)}, u32[]{:S(2)}, u32[]{:S(2)}) collective-permute-start(bf16[1,112,1024]{2,1,0:T(8,128)(2,1)} %constant_dynamic-slice_fusion), channel_id=1, source_target_pairs={{0,2},{2,4},{4,6},{6,8},{8,10},{10,12},{12,14},{14,0},{16,30},{18,... | collective-permute-start | bytes 688136 | tf_op jit(solution)/shard_map/ppermute | solution.py:221
  73.3 1.2 copy-done.3
  74.5 6.5 %hidden_units.2.early_ref = bf16[768,640]{1,0:T(8,128)(2,1)S(1)} custom-call(bf16[768,2048]{1,0:T(8,128)(2,1)S(1)} %bitcast.36, bf16[2,112,2048]{2,1,0:T(8,128)(2,1)S(1)} %copy-done.3, bf16[2,112,2048]{2,1,0:T(8,128)(2,1)} %collective-permute-done.refs_1_, bf16[2,112,2048]{2,1,0:T(8,128)(2,1)} %collective-permute-done.8.refs_2_, ...), custom_call_target="tpu_custom_call" | custom-call | flops 3523215360 | bytes 7733248 | tf_op jit(solution)/shard_map/hidden_units/pallas_call | solution.py:136
  81.0 1.0 copy-done.9
  82.0 0.0 collective-permute-done.7.refs_7_
  82.0 0.5 collective-permute-start.11
  82.5 0.2 collective-permute-start.15
  82.8 3.7 %hidden_units.3.late_ref = bf16[768,256]{1,0:T(8,128)(2,1)S(1)} custom-call(bf16[768,2048]{1,0:T(8,128)(2,1)S(1)} %bitcast.37, bf16[2,112,2048]{2,1,0:T(8,128)(2,1)} %collective-permute-done.4.refs_0_, bf16[2,112,2048]{2,1,0:T(8,128)(2,1)} %collective-permute-done.10.refs_1_), custom_call_target="tpu_custom_call" | custom-call | flops 1409286144 | bytes 4980736 | tf_op jit(solution)/shard_map/hidden_units/pallas_call | solution.py:136
  86.5 0.0 collective-permute-done.12.refs_2_
  86.5 0.0 collective-permute-done.14.refs_6_
  86.5 0.0 collective-permute-done.15.refs_8_
  86.6 8.3 %finish_terms.1 = (bf16[4,4,48,768]{3,2,1,0:T(8,128)(2,1)S(1)}, bf16[4,4,48,1280]{3,2,1,0:T(8,128)(2,1)S(1)}) custom-call(s32[1]{0:T(128)} %bitcast.2.core_ref, s32[2,16]{1,0:T(2,128)S(1)} %pad_add_fusion.spots_ref, bf16[768,2048]{1,0:T(8,128)(2,1)S(1)} %bitcast.38, bf16[768,640]{1,0:T(8,128)(2,1)S(1)} %copy-done.10, ...), custom_call_target="tpu_custom_call" | custom-call | flops 3523215360 | bytes 9502720 | tf_op jit(solution)/shard_map/finish_terms/pallas_call | solution.py:200
  94.9 0.1 slice_bitcast_fusion.6
  95.0 1.5 %collective-permute-start.22 = (bf16[2,48,1280]{2,1,0:T(8,128)(2,1)S(1)}, bf16[2,48,1280]{2,1,0:T(8,128)(2,1)S(1)}, u32[]{:S(2)}, u32[]{:S(2)}) collective-permute-start(bf16[2,48,1280]{2,1,0:T(8,128)(2,1)S(1)} %get-tuple-element.37), channel_id=1, source_target_pairs={{0,128},{128,1},{1,129},{129,0},{2,130},{130,3},{3,131},{131,2},{4... | collective-permute-start | bytes 737288 | tf_op jit(solution)/shard_map/ppermute | solution.py:230
  96.5 1.8 %collective-permute-start.24 = (bf16[2,48,1280]{2,1,0:T(8,128)(2,1)S(1)}, bf16[2,48,1280]{2,1,0:T(8,128)(2,1)S(1)}, u32[]{:S(2)}, u32[]{:S(2)}) collective-permute-start(bf16[2,48,1280]{2,1,0:T(8,128)(2,1)S(1)} %get-tuple-element.38), channel_id=1, source_target_pairs={{0,129},{128,0},{1,128},{129,1},{2,131},{130,2},{3,130},{131,3},{4... | collective-permute-start | bytes 737288 | tf_op jit(solution)/shard_map/ppermute | solution.py:230
  98.3 0.1 slice_bitcast_fusion.2
  98.3 0.4 collective-permute-start.17
  98.7 1.7 %collective-permute-start.18 = (bf16[4,48,768]{2,1,0:T(8,128)(2,1)S(1)}, bf16[4,48,768]{2,1,0:T(8,128)(2,1)S(1)}, u32[]{:S(2)}, u32[]{:S(2)}) collective-permute-start(bf16[4,48,768]{2,1,0:T(8,128)(2,1)S(1)} %get-tuple-element.42), channel_id=1, source_target_pairs={{0,96},{32,0},{64,32},{96,64},{1,97},{33,1},{65,33},{97,65},{2,98}... | collective-permute-start | bytes 884744 | tf_op jit(solution)/shard_map/ppermute | solution.py:236
  100.5 1.5 %collective-permute-start.16 = (bf16[4,48,768]{2,1,0:T(8,128)(2,1)S(1)}, bf16[4,48,768]{2,1,0:T(8,128)(2,1)S(1)}, u32[]{:S(2)}, u32[]{:S(2)}) collective-permute-start(bf16[4,48,768]{2,1,0:T(8,128)(2,1)S(1)} %get-tuple-element.41), channel_id=1, source_target_pairs={{0,64},{32,96},{64,0},{96,32},{1,65},{33,97},{65,1},{97,33},{2,66}... | collective-permute-start | bytes 884744 | tf_op jit(solution)/shard_map/ppermute | solution.py:236
  101.9 2.6 %collective-permute-done.22 = bf16[2,48,1280]{2,1,0:T(8,128)(2,1)S(1)} collective-permute-done((bf16[2,48,1280]{2,1,0:T(8,128)(2,1)S(1)}, bf16[2,48,1280]{2,1,0:T(8,128)(2,1)S(1)}, u32[]{:S(2)}, u32[]{:S(2)}) %collective-permute-start.22) | collective-permute-done | bytes 245792 | tf_op jit(solution)/shard_map/ppermute | solution.py:230
  104.6 0.0 collective-permute-done.24
  104.6 0.1 bitcast_add_fusion.3
  104.7 3.0 %collective-permute-start.25 = (bf16[4,48,1280]{2,1,0:T(8,128)(2,1)S(1)}, bf16[4,48,1280]{2,1,0:T(8,128)(2,1)S(1)}, u32[]{:S(2)}, u32[]{:S(2)}) collective-permute-start(bf16[4,48,1280]{2,1,0:T(8,128)(2,1)S(1)} %pad_maximum_fusion.1), channel_id=1, source_target_pairs={{0,129},{128,0},{1,128},{129,1},{2,131},{130,2},{3,130},{131,3},{4... | collective-permute-start | bytes 1474568 | tf_op jit(solution)/shard_map/ppermute | solution.py:230
  107.8 0.1 collective-permute-start.23
  107.9 0.5 collective-permute-done.17
  108.3 6.7 %collective-permute-done.18 = bf16[4,48,768]{2,1,0:T(8,128)(2,1)S(1)} collective-permute-done((bf16[4,48,768]{2,1,0:T(8,128)(2,1)S(1)}, bf16[4,48,768]{2,1,0:T(8,128)(2,1)S(1)}, u32[]{:S(2)}, u32[]{:S(2)}) %collective-permute-start.18) | collective-permute-done | bytes 294944 | tf_op jit(solution)/shard_map/ppermute | solution.py:236
  115.1 0.1 add.115
  115.3 0.3 collective-permute-start.19
  115.6 2.8 %collective-permute-start.20 = (bf16[2,48,768]{2,1,0:T(8,128)(2,1)S(1)}, bf16[2,48,768]{2,1,0:T(8,128)(2,1)S(1)}, u32[]{:S(2)}, u32[]{:S(2)}) collective-permute-start(bf16[2,48,768]{2,1,0:T(8,128)(2,1)S(1)} %pad_maximum_fusion.4), channel_id=1, source_target_pairs={{0,1},{128,129},{1,0},{129,128},{2,3},{130,131},{3,2},{131,130},{4... | collective-permute-start | bytes 442376 | tf_op jit(solution)/shard_map/ppermute | solution.py:230
  118.4 1.5 %collective-permute-start.21 = (bf16[2,48,768]{2,1,0:T(8,128)(2,1)S(1)}, bf16[2,48,768]{2,1,0:T(8,128)(2,1)S(1)}, u32[]{:S(2)}, u32[]{:S(2)}) collective-permute-start(bf16[2,48,768]{2,1,0:T(8,128)(2,1)S(1)} %pad_maximum_fusion.5), channel_id=1, source_target_pairs={{0,129},{128,0},{1,128},{129,1},{2,131},{130,2},{3,130},{131,3},{4... | collective-permute-start | bytes 442376 | tf_op jit(solution)/shard_map/ppermute | solution.py:230
  119.9 4.5 %collective-permute-done.23 = bf16[4,48,1280]{2,1,0:T(8,128)(2,1)S(1)} collective-permute-done((bf16[4,48,1280]{2,1,0:T(8,128)(2,1)S(1)}, bf16[4,48,1280]{2,1,0:T(8,128)(2,1)S(1)}, u32[]{:S(2)}, u32[]{:S(2)}) %collective-permute-start.23) | collective-permute-done | bytes 491552 | tf_op jit(solution)/shard_map/ppermute | solution.py:230
  124.4 0.1 fusion
  124.5 1.5 %collective-permute-start.26 = (bf16[48,1280]{1,0:T(8,128)(2,1)S(1)}, bf16[48,1280]{1,0:T(8,128)(2,1)S(1)}, u32[]{:S(2)}, u32[]{:S(2)}) collective-permute-start(bf16[48,1280]{1,0:T(8,128)(2,1)S(1)} %get-tuple-element.46), channel_id=1, source_target_pairs={{0,64},{32,96},{64,0},{96,32},{1,65},{33,97},{65,1},{97,33},{2,66}... | collective-permute-start | bytes 368648 | tf_op jit(solution)/shard_map/ppermute | solution.py:236
  126.1 2.1 %collective-permute-start.27 = (bf16[48,1280]{1,0:T(8,128)(2,1)S(1)}, bf16[48,1280]{1,0:T(8,128)(2,1)S(1)}, u32[]{:S(2)}, u32[]{:S(2)}) collective-permute-start(bf16[48,1280]{1,0:T(8,128)(2,1)S(1)} %get-tuple-element.45), channel_id=1, source_target_pairs={{0,32},{32,64},{64,96},{96,0},{1,33},{33,65},{65,97},{97,1},{2,34}... | collective-permute-start | bytes 368648 | tf_op jit(solution)/shard_map/ppermute | solution.py:236
  128.1 0.3 collective-permute-start.28
  128.4 2.5 %collective-permute-done.26.refs_5_ = bf16[48,1280]{1,0:T(8,128)(2,1)S(1)} collective-permute-done((bf16[48,1280]{1,0:T(8,128)(2,1)S(1)}, bf16[48,1280]{1,0:T(8,128)(2,1)S(1)}, u32[]{:S(2)}, u32[]{:S(2)}) %collective-permute-start.26) | collective-permute-done | bytes 122912 | tf_op jit(solution)/shard_map/ppermute | solution.py:236
  131.0 3.2 %collective-permute-done.28.refs_7_ = bf16[48,1280]{1,0:T(8,128)(2,1)S(1)} collective-permute-done((bf16[48,1280]{1,0:T(8,128)(2,1)S(1)}, bf16[48,1280]{1,0:T(8,128)(2,1)S(1)}, u32[]{:S(2)}, u32[]{:S(2)}) %collective-permute-start.28) | collective-permute-done | bytes 122912 | tf_op jit(solution)/shard_map/ppermute | solution.py:236
  134.2 2.1 %mix_terms.1 = bf16[128,2048]{1,0:T(8,128)(2,1)} custom-call(s32[2]{0:T(128)S(1)} %copy-done.2, bf16[2,128,48]{2,1,0:T(8,128)(2,1)S(1)} %get-tuple-element.20.place_ref, bf16[2,48,768]{2,1,0:T(8,128)(2,1)S(1)} %pad_maximum_fusion.2.refs_0_, bf16[2,48,768]{2,1,0:T(8,128)(2,1)S(1)} %collective-permute-done.19.refs_1_, ...), custom_call_target="tpu_custom_call" | custom-call | tf_op jit(solution)/shard_map/mix_terms/pallas_call | solution.py:337
  (50 shorter events, 0.4 us)
Async XLA Ops:
  0.6 5.2 %copy-start.11 = (s32[128,2]{0,1:T(2,128)S(1)}, s32[128,2]{0,1:T(2,128)}, u32[]{:S(2)}) copy-start(s32[128,2]{0,1:T(2,128)} %param.7) | copy-start | bytes 3076
  0.6 5.3 %copy-start.12 = (f32[128,2]{0,1:T(2,128)S(1)}, f32[128,2]{0,1:T(2,128)}, u32[]{:S(2)}) copy-start(f32[128,2]{0,1:T(2,128)} %param.8) | copy-start | bytes 3076
  0.6 5.4 %copy-start.1 = (bf16[128,2048]{1,0:T(8,128)(2,1)S(1)}, bf16[128,2048]{1,0:T(8,128)(2,1)}, u32[]{:S(2)}) copy-start(bf16[128,2048]{1,0:T(8,128)(2,1)} %tokens_ref.1) | copy-start | bytes 1572868
  3.8 21.3 %collective-permute-start = (bf16[2,112,2048]{2,1,0:T(8,128)(2,1)}, bf16[2,112,2048]{2,1,0:T(8,128)(2,1)}, u32[]{:S(2)}, u32[]{:S(2)}) collective-permute-start(bf16[2,112,2048]{2,1,0:T(8,128)(2,1)} %get-tuple-element.22.refs_0_), channel_id=1, source_target_pairs={{0,2},{2,4},{4,6},{6,8},{8,10},{10,12},{12,14},{14,0},{16,30},{18,... | collective-permute-start | bytes 2752520 | tf_op jit(solution)/shard_map/ppermute | solution.py:221
  6.9 1.6 %copy-start = (bf16[16,48,2048]{2,1,0:T(8,128)(2,1)}, bf16[16,48,2048]{2,1,0:T(8,128)(2,1)S(1)}, u32[]{:S(2)}) copy-start(bf16[16,48,2048]{2,1,0:T(8,128)(2,1)S(1)} %get-tuple-element.21) | copy-start | bytes 9437188
  8.5 64.8 %all-to-all-start = ((bf16[16,48,2048]{2,1,0:T(8,128)(2,1)}), bf16[16,48,2048]{2,1,0:T(8,128)(2,1)S(1)}, u32[]{:S(2)}, u32[]{:S(2)}) async-start(bf16[16,48,2048]{2,1,0:T(8,128)(2,1)} %copy-done), calls=%async_computation | async-start | bytes 6291456 | tf_op jit(solution)/shard_map/all_to_all | solution.py:259
  15.7 9.4 %collective-permute-start.1 = (bf16[1,112,2048]{2,1,0:T(8,128)(2,1)}, bf16[1,112,2048]{2,1,0:T(8,128)(2,1)S(1)}, u32[]{:S(2)}, u32[]{:S(2)}) collective-permute-start(bf16[1,112,2048]{2,1,0:T(8,128)(2,1)} %get-tuple-element.23.refs_0_), channel_id=1, source_target_pairs={{0,2},{2,4},{4,6},{6,8},{8,10},{10,12},{12,14},{14,0},{16,30},{18,... | collective-permute-start | bytes 1376264 | tf_op jit(solution)/shard_map/ppermute | solution.py:221
  25.1 2.4 %copy-start.5 = (bf16[1,112,2048]{2,1,0:T(8,128)(2,1)}, bf16[1,112,2048]{2,1,0:T(8,128)(2,1)S(1)}, u32[]{:S(2)}) copy-start(bf16[1,112,2048]{2,1,0:T(8,128)(2,1)S(1)} %collective-permute-done.1.refs_1_) | copy-start | bytes 1376260
  25.1 18.5 %collective-permute-start.2 = (bf16[2,112,2048]{2,1,0:T(8,128)(2,1)}, bf16[2,112,2048]{2,1,0:T(8,128)(2,1)}, u32[]{:S(2)}, u32[]{:S(2)}) collective-permute-start(bf16[2,112,2048]{2,1,0:T(8,128)(2,1)} %collective-permute-done.refs_1_), channel_id=1, source_target_pairs={{0,2},{2,4},{4,6},{6,8},{8,10},{10,12},{12,14},{14,0},{16,30},{18,... | collective-permute-start | bytes 2752520 | tf_op jit(solution)/shard_map/ppermute | solution.py:221
  27.5 16.1 %collective-permute-start.3 = (bf16[1,112,2048]{2,1,0:T(8,128)(2,1)S(1)}, bf16[1,112,2048]{2,1,0:T(8,128)(2,1)S(1)}, u32[]{:S(2)}, u32[]{:S(2)}) collective-permute-start(bf16[1,112,2048]{2,1,0:T(8,128)(2,1)S(1)} %collective-permute-done.1.refs_1_), channel_id=1, source_target_pairs={{0,2},{2,4},{4,6},{6,8},{8,10},{10,12},{12,14},{14,0},{16,30},{18,... | collective-permute-start | bytes 1376264 | tf_op jit(solution)/shard_map/ppermute | solution.py:221
  43.6 2.9 %copy-start.7 = (bf16[1,112,2048]{2,1,0:T(8,128)(2,1)}, bf16[1,112,2048]{2,1,0:T(8,128)(2,1)S(1)}, u32[]{:S(2)}) copy-start(bf16[1,112,2048]{2,1,0:T(8,128)(2,1)S(1)} %collective-permute-done.3.refs_3_) | copy-start | bytes 1376260
  43.6 18.6 %collective-permute-start.4 = (bf16[2,112,2048]{2,1,0:T(8,128)(2,1)}, bf16[2,112,2048]{2,1,0:T(8,128)(2,1)}, u32[]{:S(2)}, u32[]{:S(2)}) collective-permute-start(bf16[2,112,2048]{2,1,0:T(8,128)(2,1)} %collective-permute-done.2.refs_3_), channel_id=1, source_target_pairs={{0,2},{2,4},{4,6},{6,8},{8,10},{10,12},{12,14},{14,0},{16,30},{18,... | collective-permute-start | bytes 2752520 | tf_op jit(solution)/shard_map/ppermute | solution.py:221
  46.0 23.0 %collective-permute-start.8 = (bf16[2,112,2048]{2,1,0:T(8,128)(2,1)}, bf16[2,112,2048]{2,1,0:T(8,128)(2,1)}, u32[]{:S(2)}, u32[]{:S(2)}) collective-permute-start(bf16[2,112,2048]{2,1,0:T(8,128)(2,1)} %collective-permute-done.refs_1_), channel_id=1, source_target_pairs={{0,16},{16,0},{1,17},{17,1},{2,18},{18,2},{3,19},{19,3},{4,20},{20... | collective-permute-start | bytes 2752520 | tf_op jit(solution)/shard_map/ppermute | solution.py:225
  46.0 23.5 %collective-permute-start.9 = (bf16[2,112,2048]{2,1,0:T(8,128)(2,1)}, bf16[2,112,2048]{2,1,0:T(8,128)(2,1)}, u32[]{:S(2)}, u32[]{:S(2)}) collective-permute-start(bf16[2,112,2048]{2,1,0:T(8,128)(2,1)} %collective-permute-done.2.refs_3_), channel_id=1, source_target_pairs={{0,16},{16,0},{1,17},{17,1},{2,18},{18,2},{3,19},{19,3},{4,20},{20... | collective-permute-start | bytes 2752520 | tf_op jit(solution)/shard_map/ppermute | solution.py:225
  46.5 15.7 %collective-permute-start.5 = (bf16[1,112,2048]{2,1,0:T(8,128)(2,1)S(1)}, bf16[1,112,2048]{2,1,0:T(8,128)(2,1)}, u32[]{:S(2)}, u32[]{:S(2)}) collective-permute-start(bf16[1,112,2048]{2,1,0:T(8,128)(2,1)S(1)} %collective-permute-done.3.refs_3_), channel_id=1, source_target_pairs={{0,2},{2,4},{4,6},{6,8},{8,10},{10,12},{12,14},{14,0},{16,30},{18,... | collective-permute-start | bytes 1376264 | tf_op jit(solution)/shard_map/ppermute | solution.py:221
  62.3 20.3 %collective-permute-start.10 = (bf16[2,112,2048]{2,1,0:T(8,128)(2,1)}, bf16[2,112,2048]{2,1,0:T(8,128)(2,1)}, u32[]{:S(2)}, u32[]{:S(2)}) collective-permute-start(bf16[2,112,2048]{2,1,0:T(8,128)(2,1)} %collective-permute-done.4.refs_0_), channel_id=1, source_target_pairs={{0,16},{16,0},{1,17},{17,1},{2,18},{18,2},{3,19},{19,3},{4,20},{20... | collective-permute-start | bytes 2752520 | tf_op jit(solution)/shard_map/ppermute | solution.py:225
  64.1 17.9 %collective-permute-start.6 = (bf16[2,112,1024]{2,1,0:T(8,128)(2,1)}, bf16[2,112,1024]{2,1,0:T(8,128)(2,1)}, u32[]{:S(2)}, u32[]{:S(2)}) collective-permute-start(bf16[2,112,1024]{2,1,0:T(8,128)(2,1)} %constant_dynamic-slice_fusion.1), channel_id=1, source_target_pairs={{0,2},{2,4},{4,6},{6,8},{8,10},{10,12},{12,14},{14,0},{16,30},{18,... | collective-permute-start | bytes 1376264 | tf_op jit(solution)/shard_map/ppermute | solution.py:221
  67.4 19.1 %collective-permute-start.12 = (bf16[1,112,2048]{2,1,0:T(8,128)(2,1)}, bf16[1,112,2048]{2,1,0:T(8,128)(2,1)}, u32[]{:S(2)}, u32[]{:S(2)}) collective-permute-start(bf16[1,112,2048]{2,1,0:T(8,128)(2,1)} %copy-done.5), channel_id=1, source_target_pairs={{0,16},{16,0},{1,17},{17,1},{2,18},{18,2},{3,19},{19,3},{4,20},{20... | collective-permute-start | bytes 1376264 | tf_op jit(solution)/shard_map/ppermute | solution.py:225
  69.0 17.5 %collective-permute-start.13 = (bf16[1,112,2048]{2,1,0:T(8,128)(2,1)}, bf16[1,112,2048]{2,1,0:T(8,128)(2,1)}, u32[]{:S(2)}, u32[]{:S(2)}) collective-permute-start(bf16[1,112,2048]{2,1,0:T(8,128)(2,1)} %copy-done.7), channel_id=1, source_target_pairs={{0,16},{16,0},{1,17},{17,1},{2,18},{18,2},{3,19},{19,3},{4,20},{20... | collective-permute-start | bytes 1376264 | tf_op jit(solution)/shard_map/ppermute | solution.py:225
  69.5 12.5 %collective-permute-start.7 = (bf16[1,112,1024]{2,1,0:T(8,128)(2,1)}, bf16[1,112,1024]{2,1,0:T(8,128)(2,1)S(1)}, u32[]{:S(2)}, u32[]{:S(2)}) collective-permute-start(bf16[1,112,1024]{2,1,0:T(8,128)(2,1)} %constant_dynamic-slice_fusion), channel_id=1, source_target_pairs={{0,2},{2,4},{4,6},{6,8},{8,10},{10,12},{12,14},{14,0},{16,30},{18,... | collective-permute-start | bytes 688136 | tf_op jit(solution)/shard_map/ppermute | solution.py:221
  73.3 1.2 copy-start.3
  81.0 1.0 copy-start.9
  82.0 4.5 %collective-permute-start.14 = (bf16[1,112,2048]{2,1,0:T(8,128)(2,1)}, bf16[1,112,2048]{2,1,0:T(8,128)(2,1)}, u32[]{:S(2)}, u32[]{:S(2)}) collective-permute-start(bf16[1,112,2048]{2,1,0:T(8,128)(2,1)} %collective-permute-done.5.refs_5_), channel_id=1, source_target_pairs={{0,16},{16,0},{1,17},{17,1},{2,18},{18,2},{3,19},{19,3},{4,20},{20... | collective-permute-start | bytes 1376264 | tf_op jit(solution)/shard_map/ppermute | solution.py:225
  82.0 4.5 %collective-permute-start.11 = (bf16[2,112,1024]{2,1,0:T(8,128)(2,1)}, bf16[2,112,1024]{2,1,0:T(8,128)(2,1)}, u32[]{:S(2)}, u32[]{:S(2)}) collective-permute-start(bf16[2,112,1024]{2,1,0:T(8,128)(2,1)} %collective-permute-done.6.own_ref), channel_id=1, source_target_pairs={{0,16},{16,0},{1,17},{17,1},{2,18},{18,2},{3,19},{19,3},{4,20},{20... | collective-permute-start | bytes 1376264 | tf_op jit(solution)/shard_map/ppermute | solution.py:225
  82.5 4.0 %collective-permute-start.15 = (bf16[1,112,1024]{2,1,0:T(8,128)(2,1)S(1)}, bf16[1,112,1024]{2,1,0:T(8,128)(2,1)S(1)}, u32[]{:S(2)}, u32[]{:S(2)}) collective-permute-start(bf16[1,112,1024]{2,1,0:T(8,128)(2,1)S(1)} %collective-permute-done.7.refs_7_), channel_id=1, source_target_pairs={{0,16},{16,0},{1,17},{17,1},{2,18},{18,2},{3,19},{19,3},{4,20},{20... | collective-permute-start | bytes 688136 | tf_op jit(solution)/shard_map/ppermute | solution.py:225
  82.7 3.8 %copy-start.4 = (bf16[1,112,2048]{2,1,0:T(8,128)(2,1)S(1)}, bf16[1,112,2048]{2,1,0:T(8,128)(2,1)}, u32[]{:S(2)}) copy-start(bf16[1,112,2048]{2,1,0:T(8,128)(2,1)} %get-tuple-element.23.refs_0_) | copy-start | bytes 1376260
  82.7 3.8 %copy-start.6 = (bf16[1,112,2048]{2,1,0:T(8,128)(2,1)S(1)}, bf16[1,112,2048]{2,1,0:T(8,128)(2,1)}, u32[]{:S(2)}) copy-start(bf16[1,112,2048]{2,1,0:T(8,128)(2,1)} %copy-done.5) | copy-start | bytes 1376260
  82.8 3.8 %copy-start.8 = (bf16[1,112,2048]{2,1,0:T(8,128)(2,1)S(1)}, bf16[1,112,2048]{2,1,0:T(8,128)(2,1)}, u32[]{:S(2)}) copy-start(bf16[1,112,2048]{2,1,0:T(8,128)(2,1)} %copy-done.7) | copy-start | bytes 1376260
  82.8 3.8 %copy-start.10 = (bf16[768,640]{1,0:T(8,128)(2,1)S(1)}, bf16[768,640]{1,0:T(8,128)(2,1)}, u32[]{:S(2)}) copy-start(bf16[768,640]{1,0:T(8,128)(2,1)} %copy-done.9) | copy-start | bytes 2949124
  95.0 9.6 %collective-permute-start.22 = (bf16[2,48,1280]{2,1,0:T(8,128)(2,1)S(1)}, bf16[2,48,1280]{2,1,0:T(8,128)(2,1)S(1)}, u32[]{:S(2)}, u32[]{:S(2)}) collective-permute-start(bf16[2,48,1280]{2,1,0:T(8,128)(2,1)S(1)} %get-tuple-element.37), channel_id=1, source_target_pairs={{0,128},{128,1},{1,129},{129,0},{2,130},{130,3},{3,131},{131,2},{4... | collective-permute-start | bytes 737288 | tf_op jit(solution)/shard_map/ppermute | solution.py:230
  96.5 8.0 %collective-permute-start.24 = (bf16[2,48,1280]{2,1,0:T(8,128)(2,1)S(1)}, bf16[2,48,1280]{2,1,0:T(8,128)(2,1)S(1)}, u32[]{:S(2)}, u32[]{:S(2)}) collective-permute-start(bf16[2,48,1280]{2,1,0:T(8,128)(2,1)S(1)} %get-tuple-element.38), channel_id=1, source_target_pairs={{0,129},{128,0},{1,128},{129,1},{2,131},{130,2},{3,130},{131,3},{4... | collective-permute-start | bytes 737288 | tf_op jit(solution)/shard_map/ppermute | solution.py:230
  98.3 10.0 %collective-permute-start.17 = (bf16[4,48,768]{2,1,0:T(8,128)(2,1)S(1)}, bf16[4,48,768]{2,1,0:T(8,128)(2,1)S(1)}, u32[]{:S(2)}, u32[]{:S(2)}) collective-permute-start(bf16[4,48,768]{2,1,0:T(8,128)(2,1)S(1)} %get-tuple-element.43), channel_id=1, source_target_pairs={{0,32},{32,64},{64,96},{96,0},{1,33},{33,65},{65,97},{97,1},{2,34}... | collective-permute-start | bytes 884744 | tf_op jit(solution)/shard_map/ppermute | solution.py:236
  98.7 16.3 %collective-permute-start.18 = (bf16[4,48,768]{2,1,0:T(8,128)(2,1)S(1)}, bf16[4,48,768]{2,1,0:T(8,128)(2,1)S(1)}, u32[]{:S(2)}, u32[]{:S(2)}) collective-permute-start(bf16[4,48,768]{2,1,0:T(8,128)(2,1)S(1)} %get-tuple-element.42), channel_id=1, source_target_pairs={{0,96},{32,0},{64,32},{96,64},{1,97},{33,1},{65,33},{97,65},{2,98}... | collective-permute-start | bytes 884744 | tf_op jit(solution)/shard_map/ppermute | solution.py:236
  100.5 14.7 %collective-permute-start.16 = (bf16[4,48,768]{2,1,0:T(8,128)(2,1)S(1)}, bf16[4,48,768]{2,1,0:T(8,128)(2,1)S(1)}, u32[]{:S(2)}, u32[]{:S(2)}) collective-permute-start(bf16[4,48,768]{2,1,0:T(8,128)(2,1)S(1)} %get-tuple-element.41), channel_id=1, source_target_pairs={{0,64},{32,96},{64,0},{96,32},{1,65},{33,97},{65,1},{97,33},{2,66}... | collective-permute-start | bytes 884744 | tf_op jit(solution)/shard_map/ppermute | solution.py:236
  104.7 15.2 %collective-permute-start.25 = (bf16[4,48,1280]{2,1,0:T(8,128)(2,1)S(1)}, bf16[4,48,1280]{2,1,0:T(8,128)(2,1)S(1)}, u32[]{:S(2)}, u32[]{:S(2)}) collective-permute-start(bf16[4,48,1280]{2,1,0:T(8,128)(2,1)S(1)} %pad_maximum_fusion.1), channel_id=1, source_target_pairs={{0,129},{128,0},{1,128},{129,1},{2,131},{130,2},{3,130},{131,3},{4... | collective-permute-start | bytes 1474568 | tf_op jit(solution)/shard_map/ppermute | solution.py:230
  107.8 16.6 %collective-permute-start.23 = (bf16[4,48,1280]{2,1,0:T(8,128)(2,1)S(1)}, bf16[4,48,1280]{2,1,0:T(8,128)(2,1)S(1)}, u32[]{:S(2)}, u32[]{:S(2)}) collective-permute-start(bf16[4,48,1280]{2,1,0:T(8,128)(2,1)S(1)} %pad_maximum_fusion), channel_id=1, source_target_pairs={{0,128},{128,1},{1,129},{129,0},{2,130},{130,3},{3,131},{131,2},{4... | collective-permute-start | bytes 1474568 | tf_op jit(solution)/shard_map/ppermute | solution.py:230
  115.3 19.0 %copy-start.2 = (s32[2]{0:T(128)S(1)}, s32[2]{0:T(128)}, u32[]{:S(2)}) copy-start(s32[2]{0:T(128)} %pad_add_fusion.1.at_ref) | copy-start | bytes 28
  115.3 12.9 %collective-permute-start.19 = (bf16[2,48,768]{2,1,0:T(8,128)(2,1)S(1)}, bf16[2,48,768]{2,1,0:T(8,128)(2,1)S(1)}, u32[]{:S(2)}, u32[]{:S(2)}) collective-permute-start(bf16[2,48,768]{2,1,0:T(8,128)(2,1)S(1)} %pad_maximum_fusion.3), channel_id=1, source_target_pairs={{0,128},{128,1},{1,129},{129,0},{2,130},{130,3},{3,131},{131,2},{4... | collective-permute-start | bytes 442376 | tf_op jit(solution)/shard_map/ppermute | solution.py:230
  115.6 12.8 %collective-permute-start.20 = (bf16[2,48,768]{2,1,0:T(8,128)(2,1)S(1)}, bf16[2,48,768]{2,1,0:T(8,128)(2,1)S(1)}, u32[]{:S(2)}, u32[]{:S(2)}) collective-permute-start(bf16[2,48,768]{2,1,0:T(8,128)(2,1)S(1)} %pad_maximum_fusion.4), channel_id=1, source_target_pairs={{0,1},{128,129},{1,0},{129,128},{2,3},{130,131},{3,2},{131,130},{4... | collective-permute-start | bytes 442376 | tf_op jit(solution)/shard_map/ppermute | solution.py:230
  118.4 10.1 %collective-permute-start.21 = (bf16[2,48,768]{2,1,0:T(8,128)(2,1)S(1)}, bf16[2,48,768]{2,1,0:T(8,128)(2,1)S(1)}, u32[]{:S(2)}, u32[]{:S(2)}) collective-permute-start(bf16[2,48,768]{2,1,0:T(8,128)(2,1)S(1)} %pad_maximum_fusion.5), channel_id=1, source_target_pairs={{0,129},{128,0},{1,128},{129,1},{2,131},{130,2},{3,130},{131,3},{4... | collective-permute-start | bytes 442376 | tf_op jit(solution)/shard_map/ppermute | solution.py:230
  124.5 6.5 %collective-permute-start.26 = (bf16[48,1280]{1,0:T(8,128)(2,1)S(1)}, bf16[48,1280]{1,0:T(8,128)(2,1)S(1)}, u32[]{:S(2)}, u32[]{:S(2)}) collective-permute-start(bf16[48,1280]{1,0:T(8,128)(2,1)S(1)} %get-tuple-element.46), channel_id=1, source_target_pairs={{0,64},{32,96},{64,0},{96,32},{1,65},{33,97},{65,1},{97,33},{2,66}... | collective-permute-start | bytes 368648 | tf_op jit(solution)/shard_map/ppermute | solution.py:236
  126.1 4.9 %collective-permute-start.27 = (bf16[48,1280]{1,0:T(8,128)(2,1)S(1)}, bf16[48,1280]{1,0:T(8,128)(2,1)S(1)}, u32[]{:S(2)}, u32[]{:S(2)}) collective-permute-start(bf16[48,1280]{1,0:T(8,128)(2,1)S(1)} %get-tuple-element.45), channel_id=1, source_target_pairs={{0,32},{32,64},{64,96},{96,0},{1,33},{33,65},{65,97},{97,1},{2,34}... | collective-permute-start | bytes 368648 | tf_op jit(solution)/shard_map/ppermute | solution.py:236
  128.1 6.1 %collective-permute-start.28 = (bf16[48,1280]{1,0:T(8,128)(2,1)S(1)}, bf16[48,1280]{1,0:T(8,128)(2,1)S(1)}, u32[]{:S(2)}, u32[]{:S(2)}) collective-permute-start(bf16[48,1280]{1,0:T(8,128)(2,1)S(1)} %get-tuple-element.44), channel_id=1, source_target_pairs={{0,96},{32,0},{64,32},{96,64},{1,97},{33,1},{65,33},{97,65},{2,98}... | collective-permute-start | bytes 368648 | tf_op jit(solution)/shard_map/ppermute | solution.py:236

commit v5 on v4

--- a/solution.py
+++ b/solution.py
@@ -99,6 +99,27 @@
     )(at, w_gate, w_up, w_down)
 
 
+def halve_kernel(core_ref, *refs):
+    number = len(refs) // 2
+    for source, target in zip(refs[:number], refs[number:]):
+        half = target.shape[2]
+        target[...] = source[:, :, pl.ds(pl.multiple_of(core_ref[0] * half, half), half)]
+
+
+def halve(core, *arrays):
+    whole = pl.BlockSpec(memory_space=pltpu.VMEM)
+    return pl.pallas_call(
+        halve_kernel,
+        in_specs=[pl.BlockSpec(memory_space=pltpu.SMEM)] + [whole] * len(arrays),
+        out_specs=[whole] * len(arrays),
+        out_shape=[
+            jax.ShapeDtypeStruct(a.shape[:2] + (a.shape[2] // 2,), a.dtype) for a in arrays
+        ],
+        compiler_params=pltpu.CompilerParams(vmem_limit_bytes=GRANT),
+        name="halve_pieces",
+    )(core, *arrays)
+
+
 def cost(flops, *arrays):
     return pl.CostEstimate(
         flops=flops,
@@ -245,7 +266,6 @@
     chips = lax.axis_size(PLANE)
     depth = lax.axis_size("z")
     share = w_gate.shape[1] // 4
-    half = width // 2
     xl, xh, y = lax.axis_index("xl"), lax.axis_index("xh"), lax.axis_index("y")
     core = lax.axis_index("c").astype(jnp.int32)
     at = jnp.stack([y % 2, xl * 2 + y // 2]).astype(jnp.int32)
@@ -265,11 +285,8 @@
         firsts += [gate_up, swapped(gate_up)]
         lasts += [below, swapped(below)]
 
-    def far(value):
-        part = lax.dynamic_slice(value, (0, 0, core * half), value.shape[:2] + (half,))
-        return along_z(part, depth)
-
-    gate_up, below = far(gate_up), far(below)
+    gate_up, below = halve(core.reshape(1), gate_up, below)
+    gate_up, below = along_z(gate_up, depth), along_z(below, depth)
     early = hidden_units(rows, firsts[:EARLY])
     late = hidden_units(rows, firsts[EARLY:])
     gate_up, below, early = lax.optimization_barrier((gate_up, below, early))

time: 137 us -> 135 us (0.985)
  the two profiles are of different devices: /device:TPU:88 before, /device:TPU:30 now
where the time goes in v5:
time: 135 us; the launch traced here: 133 us
  waiting for transfers between devices  64.6 us (48%)
  starting transfers between devices  35.5 us (26%)
  Pallas kernels  26.9 us (20%)
  local copies, waits for them, and re-layouts  5.04 us (4%)
    ppermute x8, waiting for transfers between devices, along_z(): return lax.ppermute(value, ('c', 'z'), pairs)  44.8 us
    ppermute x6, waiting for transfers between devices, along_y(): lax.ppermute(value, 'y', [(y, (y + step) % SIDE) for y in range(SIDE)])  11.5 us
    pallas_call x2, Pallas kernels, hidden_units(): pl.pallas_call(hidden_kernel, in_specs=[whole] * (1 + len(pieces)), out_s...  10.2 us
    ppermute x6, starting transfers between devices, along_y(): lax.ppermute(value, 'y', [(y, (y + step) % SIDE) for y in range(SIDE)])  8.85 us
    ppermute x7, starting transfers between devices, along_x(): lax.ppermute(value, ('xl', 'xh'), [(places[x], places[(x + step) % SIDE])...  8.66 us
    ppermute x8, starting transfers between devices, along_z(): return lax.ppermute(value, ('c', 'z'), pairs)  8.41 us
    pallas_call x1, Pallas kernels, finish(): pl.pallas_call(finish_kernel, in_specs=[scalars] * 2 + [whole] * 5 + [any...  8.33 us
    ppermute x7, waiting for transfers between devices, along_x(): lax.ppermute(value, ('xl', 'xh'), [(places[x], places[(x + step) % SIDE])...  8.27 us
  transfers between devices with their start and end apart: 30, of which 12 were waited for; matrix products, arithmetic and copies ran while one was open for 1% of the time, Pallas kernels for 10%

profile of v5, /device:TPU:30, one launch (start us, length us, event | category | flops | bytes accessed | tf_op | source)
XLA Modules:
  0.0 133.3 jit_solution(10327730594947512111)
XLA Ops:
  0.0 0.6 pad_add_fusion.1.at_ref
  0.6 3.2 %pack_weights.1 = (bf16[2,112,2048]{2,1,0:T(8,128)(2,1)}, bf16[1,112,2048]{2,1,0:T(8,128)(2,1)}) custom-call(s32[2]{0:T(128)} %pad_add_fusion.1.at_ref, bf16[2,448,2048]{2,1,0:T(8,128)(2,1)} %gate_ref.1, bf16[2,448,2048]{2,1,0:T(8,128)(2,1)} %up_ref.1, bf16[2,448,2048]{2,1,0:T(8,128)(2,1)} %down_ref.1), custom_call_target="tpu_custom_call" | custom-call | tf_op jit(solution)/shard_map/pack_weights/pallas_call | solution.py:90
  3.8 2.0 %collective-permute-start = (bf16[2,112,2048]{2,1,0:T(8,128)(2,1)}, bf16[2,112,2048]{2,1,0:T(8,128)(2,1)}, u32[]{:S(2)}, u32[]{:S(2)}) collective-permute-start(bf16[2,112,2048]{2,1,0:T(8,128)(2,1)} %get-tuple-element.24.refs_0_), channel_id=1, source_target_pairs={{0,2},{2,4},{4,6},{6,8},{8,10},{10,12},{12,14},{14,0},{16,30},{18,... | collective-permute-start | bytes 2752520 | tf_op jit(solution)/shard_map/ppermute | solution.py:242
  5.8 0.1 copy.7.ids_ref
  5.9 0.1 copy.8.logits_ref
  6.0 0.8 pick_rows.1
  6.9 1.6 %copy-done = bf16[16,48,2048]{2,1,0:T(8,128)(2,1)} copy-done((bf16[16,48,2048]{2,1,0:T(8,128)(2,1)}, bf16[16,48,2048]{2,1,0:T(8,128)(2,1)S(1)}, u32[]{:S(2)}) %copy-start) | copy-done | bytes 3145752
  8.5 7.1 %all-to-all-start = ((bf16[16,48,2048]{2,1,0:T(8,128)(2,1)}), bf16[16,48,2048]{2,1,0:T(8,128)(2,1)S(1)}, u32[]{:S(2)}, u32[]{:S(2)}) async-start(bf16[16,48,2048]{2,1,0:T(8,128)(2,1)} %copy-done), calls=%async_computation | async-start | bytes 6291456 | tf_op jit(solution)/shard_map/all_to_all | solution.py:279
  15.6 1.9 %collective-permute-start.1 = (bf16[1,112,2048]{2,1,0:T(8,128)(2,1)}, bf16[1,112,2048]{2,1,0:T(8,128)(2,1)S(1)}, u32[]{:S(2)}, u32[]{:S(2)}) collective-permute-start(bf16[1,112,2048]{2,1,0:T(8,128)(2,1)} %get-tuple-element.25.refs_0_), channel_id=1, source_target_pairs={{0,2},{2,4},{4,6},{6,8},{8,10},{10,12},{12,14},{14,0},{16,30},{18,... | collective-permute-start | bytes 1376264 | tf_op jit(solution)/shard_map/ppermute | solution.py:242
  17.5 8.7 %collective-permute-done.1.refs_1_ = bf16[1,112,2048]{2,1,0:T(8,128)(2,1)S(1)} collective-permute-done((bf16[1,112,2048]{2,1,0:T(8,128)(2,1)}, bf16[1,112,2048]{2,1,0:T(8,128)(2,1)S(1)}, u32[]{:S(2)}, u32[]{:S(2)}) %collective-permute-start.1) | collective-permute-done | bytes 458784 | tf_op jit(solution)/shard_map/ppermute | solution.py:242
  26.2 0.8 copy-done.5
  27.0 1.9 %collective-permute-start.3 = (bf16[1,112,2048]{2,1,0:T(8,128)(2,1)S(1)}, bf16[1,112,2048]{2,1,0:T(8,128)(2,1)S(1)}, u32[]{:S(2)}, u32[]{:S(2)}) collective-permute-start(bf16[1,112,2048]{2,1,0:T(8,128)(2,1)S(1)} %collective-permute-done.1.refs_1_), channel_id=1, source_target_pairs={{0,2},{2,4},{4,6},{6,8},{8,10},{10,12},{12,14},{14,0},{16,30},{18,... | collective-permute-start | bytes 1376264 | tf_op jit(solution)/shard_map/ppermute | solution.py:242
  28.9 17.1 %collective-permute-done.3.refs_3_ = bf16[1,112,2048]{2,1,0:T(8,128)(2,1)S(1)} collective-permute-done((bf16[1,112,2048]{2,1,0:T(8,128)(2,1)S(1)}, bf16[1,112,2048]{2,1,0:T(8,128)(2,1)S(1)}, u32[]{:S(2)}, u32[]{:S(2)}) %collective-permute-start.3) | collective-permute-done | bytes 458784 | tf_op jit(solution)/shard_map/ppermute | solution.py:242
  45.9 1.2 collective-permute-start.8
  47.2 0.0 collective-permute-start.9
  47.2 0.7 collective-permute-start.5
  47.9 17.9 %collective-permute-done.5.refs_1_.refs_5_ = bf16[1,112,2048]{2,1,0:T(8,128)(2,1)} collective-permute-done((bf16[1,112,2048]{2,1,0:T(8,128)(2,1)S(1)}, bf16[1,112,2048]{2,1,0:T(8,128)(2,1)}, u32[]{:S(2)}, u32[]{:S(2)}) %collective-permute-start.5) | collective-permute-done | bytes 458784 | tf_op jit(solution)/shard_map/ppermute | solution.py:242
  65.8 0.0 collective-permute-done.4.refs_0_
  65.8 0.0 collective-permute-start.10
  65.8 2.2 %halve_pieces.1 = (bf16[2,112,1024]{2,1,0:T(8,128)(2,1)}, bf16[1,112,1024]{2,1,0:T(8,128)(2,1)}) custom-call(s32[1]{0:T(128)} %bitcast.2.core_ref, bf16[2,112,2048]{2,1,0:T(8,128)(2,1)} %collective-permute-done.4.refs_0_, bf16[1,112,2048]{2,1,0:T(8,128)(2,1)} %collective-permute-done.5.refs_1_.refs_5_), custom_call_target="tpu_custom_call" | custom-call | tf_op jit(solution)/shard_map/halve_pieces/pallas_call | solution.py:111
  68.0 0.0 collective-permute-start.6
  68.0 0.5 collective-permute-start.12
  68.5 0.0 collective-permute-done.8.refs_2_
  68.5 0.1 collective-permute-start.13
  68.6 0.0 collective-permute-done.9.refs_4_
  68.6 1.9 %collective-permute-start.7 = (bf16[1,112,1024]{2,1,0:T(8,128)(2,1)}, bf16[1,112,1024]{2,1,0:T(8,128)(2,1)S(1)}, u32[]{:S(2)}, u32[]{:S(2)}) collective-permute-start(bf16[1,112,1024]{2,1,0:T(8,128)(2,1)} %get-tuple-element.33), channel_id=1, source_target_pairs={{0,2},{2,4},{4,6},{6,8},{8,10},{10,12},{12,14},{14,0},{16,30},{18,... | collective-permute-start | bytes 688136 | tf_op jit(solution)/shard_map/ppermute | solution.py:242
  70.5 1.2 copy-done.3
  71.7 6.5 %hidden_units.2.early_ref = bf16[768,640]{1,0:T(8,128)(2,1)S(1)} custom-call(bf16[768,2048]{1,0:T(8,128)(2,1)S(1)} %bitcast.36, bf16[2,112,2048]{2,1,0:T(8,128)(2,1)S(1)} %copy-done.3, bf16[2,112,2048]{2,1,0:T(8,128)(2,1)} %collective-permute-done.refs_1_, bf16[2,112,2048]{2,1,0:T(8,128)(2,1)} %collective-permute-done.8.refs_2_, ...), custom_call_target="tpu_custom_call" | custom-call | flops 3523215360 | bytes 7733248 | tf_op jit(solution)/shard_map/hidden_units/pallas_call | solution.py:157
  78.2 1.0 copy-done.9
  79.2 1.2 collective-permute-done.7.refs_7_
  80.4 0.1 collective-permute-start.14
  80.4 0.0 collective-permute-done.6.own_ref
  80.4 0.4 collective-permute-start.11
  80.9 0.0 collective-permute-done.10.refs_1_
  80.9 0.2 collective-permute-start.15
  81.1 3.7 %hidden_units.3.late_ref = bf16[768,256]{1,0:T(8,128)(2,1)S(1)} custom-call(bf16[768,2048]{1,0:T(8,128)(2,1)S(1)} %bitcast.37, bf16[2,112,2048]{2,1,0:T(8,128)(2,1)} %collective-permute-done.4.refs_0_, bf16[2,112,2048]{2,1,0:T(8,128)(2,1)} %collective-permute-done.10.refs_1_), custom_call_target="tpu_custom_call" | custom-call | flops 1409286144 | bytes 4980736 | tf_op jit(solution)/shard_map/hidden_units/pallas_call | solution.py:157
  84.8 0.0 collective-permute-done.13.refs_4_
  84.9 8.3 %finish_terms.1 = (bf16[4,4,48,768]{3,2,1,0:T(8,128)(2,1)S(1)}, bf16[4,4,48,1280]{3,2,1,0:T(8,128)(2,1)S(1)}) custom-call(s32[1]{0:T(128)} %bitcast.2.core_ref, s32[2,16]{1,0:T(2,128)S(1)} %pad_add_fusion.spots_ref, bf16[768,2048]{1,0:T(8,128)(2,1)S(1)} %bitcast.38, bf16[768,640]{1,0:T(8,128)(2,1)S(1)} %copy-done.10, ...), custom_call_target="tpu_custom_call" | custom-call | flops 3523215360 | bytes 9502720 | tf_op jit(solution)/shard_map/finish_terms/pallas_call | solution.py:221
  93.2 0.1 slice_bitcast_fusion.6
  93.3 0.6 collective-permute-start.22
  93.9 1.5 %collective-permute-start.24 = (bf16[2,48,1280]{2,1,0:T(8,128)(2,1)S(1)}, bf16[2,48,1280]{2,1,0:T(8,128)(2,1)S(1)}, u32[]{:S(2)}, u32[]{:S(2)}) collective-permute-start(bf16[2,48,1280]{2,1,0:T(8,128)(2,1)S(1)} %get-tuple-element.42), channel_id=1, source_target_pairs={{0,129},{128,0},{1,128},{129,1},{2,131},{130,2},{3,130},{131,3},{4... | collective-permute-start | bytes 737288 | tf_op jit(solution)/shard_map/ppermute | solution.py:251
  95.4 0.1 slice_bitcast_fusion.2
  95.5 0.6 collective-permute-start.17
  96.1 1.5 %collective-permute-start.18 = (bf16[4,48,768]{2,1,0:T(8,128)(2,1)S(1)}, bf16[4,48,768]{2,1,0:T(8,128)(2,1)S(1)}, u32[]{:S(2)}, u32[]{:S(2)}) collective-permute-start(bf16[4,48,768]{2,1,0:T(8,128)(2,1)S(1)} %get-tuple-element.46), channel_id=1, source_target_pairs={{0,96},{32,0},{64,32},{96,64},{1,97},{33,1},{65,33},{97,65},{2,98}... | collective-permute-start | bytes 884744 | tf_op jit(solution)/shard_map/ppermute | solution.py:257
  97.6 1.5 %collective-permute-start.16 = (bf16[4,48,768]{2,1,0:T(8,128)(2,1)S(1)}, bf16[4,48,768]{2,1,0:T(8,128)(2,1)S(1)}, u32[]{:S(2)}, u32[]{:S(2)}) collective-permute-start(bf16[4,48,768]{2,1,0:T(8,128)(2,1)S(1)} %get-tuple-element.45), channel_id=1, source_target_pairs={{0,64},{32,96},{64,0},{96,32},{1,65},{33,97},{65,1},{97,33},{2,66}... | collective-permute-start | bytes 884744 | tf_op jit(solution)/shard_map/ppermute | solution.py:257
  99.0 2.6 %collective-permute-done.22 = bf16[2,48,1280]{2,1,0:T(8,128)(2,1)S(1)} collective-permute-done((bf16[2,48,1280]{2,1,0:T(8,128)(2,1)S(1)}, bf16[2,48,1280]{2,1,0:T(8,128)(2,1)S(1)}, u32[]{:S(2)}, u32[]{:S(2)}) %collective-permute-start.22) | collective-permute-done | bytes 245792 | tf_op jit(solution)/shard_map/ppermute | solution.py:251
  101.7 1.5 %collective-permute-done.24 = bf16[2,48,1280]{2,1,0:T(8,128)(2,1)S(1)} collective-permute-done((bf16[2,48,1280]{2,1,0:T(8,128)(2,1)S(1)}, bf16[2,48,1280]{2,1,0:T(8,128)(2,1)S(1)}, u32[]{:S(2)}, u32[]{:S(2)}) %collective-permute-start.24) | collective-permute-done | bytes 245792 | tf_op jit(solution)/shard_map/ppermute | solution.py:251
  103.2 0.1 bitcast_add_fusion.3
  103.3 0.3 collective-permute-start.25
  103.7 3.1 %collective-permute-start.23 = (bf16[4,48,1280]{2,1,0:T(8,128)(2,1)S(1)}, bf16[4,48,1280]{2,1,0:T(8,128)(2,1)S(1)}, u32[]{:S(2)}, u32[]{:S(2)}) collective-permute-start(bf16[4,48,1280]{2,1,0:T(8,128)(2,1)S(1)} %pad_maximum_fusion), channel_id=1, source_target_pairs={{0,128},{128,1},{1,129},{129,0},{2,130},{130,3},{3,131},{131,2},{4... | collective-permute-start | bytes 1474568 | tf_op jit(solution)/shard_map/ppermute | solution.py:251
  106.8 5.4 %collective-permute-done.18 = bf16[4,48,768]{2,1,0:T(8,128)(2,1)S(1)} collective-permute-done((bf16[4,48,768]{2,1,0:T(8,128)(2,1)S(1)}, bf16[4,48,768]{2,1,0:T(8,128)(2,1)S(1)}, u32[]{:S(2)}, u32[]{:S(2)}) %collective-permute-start.18) | collective-permute-done | bytes 294944 | tf_op jit(solution)/shard_map/ppermute | solution.py:257
  112.2 0.1 add.110
  112.4 1.9 %collective-permute-start.19 = (bf16[2,48,768]{2,1,0:T(8,128)(2,1)S(1)}, bf16[2,48,768]{2,1,0:T(8,128)(2,1)S(1)}, u32[]{:S(2)}, u32[]{:S(2)}) collective-permute-start(bf16[2,48,768]{2,1,0:T(8,128)(2,1)S(1)} %pad_maximum_fusion.3), channel_id=1, source_target_pairs={{0,128},{128,1},{1,129},{129,0},{2,130},{130,3},{3,131},{131,2},{4... | collective-permute-start | bytes 442376 | tf_op jit(solution)/shard_map/ppermute | solution.py:251
  114.3 1.2 collective-permute-start.20
  115.5 0.1 collective-permute-start.21
  115.6 3.5 %collective-permute-done.25 = bf16[4,48,1280]{2,1,0:T(8,128)(2,1)S(1)} collective-permute-done((bf16[4,48,1280]{2,1,0:T(8,128)(2,1)S(1)}, bf16[4,48,1280]{2,1,0:T(8,128)(2,1)S(1)}, u32[]{:S(2)}, u32[]{:S(2)}) %collective-permute-start.25) | collective-permute-done | bytes 491552 | tf_op jit(solution)/shard_map/ppermute | solution.py:251
  119.1 0.6 collective-permute-done.23
  119.7 0.1 fusion
  119.8 1.5 %collective-permute-start.26 = (bf16[48,1280]{1,0:T(8,128)(2,1)S(1)}, bf16[48,1280]{1,0:T(8,128)(2,1)S(1)}, u32[]{:S(2)}, u32[]{:S(2)}) collective-permute-start(bf16[48,1280]{1,0:T(8,128)(2,1)S(1)} %get-tuple-element.50), channel_id=1, source_target_pairs={{0,64},{32,96},{64,0},{96,32},{1,65},{33,97},{65,1},{97,33},{2,66}... | collective-permute-start | bytes 368648 | tf_op jit(solution)/shard_map/ppermute | solution.py:257
  121.4 3.7 %collective-permute-start.27 = (bf16[48,1280]{1,0:T(8,128)(2,1)S(1)}, bf16[48,1280]{1,0:T(8,128)(2,1)S(1)}, u32[]{:S(2)}, u32[]{:S(2)}) collective-permute-start(bf16[48,1280]{1,0:T(8,128)(2,1)S(1)} %get-tuple-element.49), channel_id=1, source_target_pairs={{0,32},{32,64},{64,96},{96,0},{1,33},{33,65},{65,97},{97,1},{2,34}... | collective-permute-start | bytes 368648 | tf_op jit(solution)/shard_map/ppermute | solution.py:257
  125.1 1.1 collective-permute-done.26.refs_5_
  126.3 1.3 collective-permute-done.27.refs_6_
  127.5 3.6 %collective-permute-done.28.refs_7_ = bf16[48,1280]{1,0:T(8,128)(2,1)S(1)} collective-permute-done((bf16[48,1280]{1,0:T(8,128)(2,1)S(1)}, bf16[48,1280]{1,0:T(8,128)(2,1)S(1)}, u32[]{:S(2)}, u32[]{:S(2)}) %collective-permute-start.28) | collective-permute-done | bytes 122912 | tf_op jit(solution)/shard_map/ppermute | solution.py:257
  131.2 2.1 %mix_terms.1 = bf16[128,2048]{1,0:T(8,128)(2,1)} custom-call(s32[2]{0:T(128)S(1)} %copy-done.2, bf16[2,128,48]{2,1,0:T(8,128)(2,1)S(1)} %get-tuple-element.22.place_ref, bf16[2,48,768]{2,1,0:T(8,128)(2,1)S(1)} %pad_maximum_fusion.2.refs_0_, bf16[2,48,768]{2,1,0:T(8,128)(2,1)S(1)} %collective-permute-done.19.refs_1_, ...), custom_call_target="tpu_custom_call" | custom-call | tf_op jit(solution)/shard_map/mix_terms/pallas_call | solution.py:354
  (49 shorter events, 0.4 us)
Async XLA Ops:
  0.6 5.2 %copy-start.11 = (s32[128,2]{0,1:T(2,128)S(1)}, s32[128,2]{0,1:T(2,128)}, u32[]{:S(2)}) copy-start(s32[128,2]{0,1:T(2,128)} %param.7) | copy-start | bytes 3076
  0.6 5.3 %copy-start.12 = (f32[128,2]{0,1:T(2,128)S(1)}, f32[128,2]{0,1:T(2,128)}, u32[]{:S(2)}) copy-start(f32[128,2]{0,1:T(2,128)} %param.8) | copy-start | bytes 3076
  0.6 5.4 %copy-start.1 = (bf16[128,2048]{1,0:T(8,128)(2,1)S(1)}, bf16[128,2048]{1,0:T(8,128)(2,1)}, u32[]{:S(2)}) copy-start(bf16[128,2048]{1,0:T(8,128)(2,1)} %tokens_ref.1) | copy-start | bytes 1572868
  3.8 22.4 %collective-permute-start = (bf16[2,112,2048]{2,1,0:T(8,128)(2,1)}, bf16[2,112,2048]{2,1,0:T(8,128)(2,1)}, u32[]{:S(2)}, u32[]{:S(2)}) collective-permute-start(bf16[2,112,2048]{2,1,0:T(8,128)(2,1)} %get-tuple-element.24.refs_0_), channel_id=1, source_target_pairs={{0,2},{2,4},{4,6},{6,8},{8,10},{10,12},{12,14},{14,0},{16,30},{18,... | collective-permute-start | bytes 2752520 | tf_op jit(solution)/shard_map/ppermute | solution.py:242
  6.8 1.6 %copy-start = (bf16[16,48,2048]{2,1,0:T(8,128)(2,1)}, bf16[16,48,2048]{2,1,0:T(8,128)(2,1)S(1)}, u32[]{:S(2)}) copy-start(bf16[16,48,2048]{2,1,0:T(8,128)(2,1)S(1)} %get-tuple-element.23) | copy-start | bytes 9437188
  8.5 62.0 %all-to-all-start = ((bf16[16,48,2048]{2,1,0:T(8,128)(2,1)}), bf16[16,48,2048]{2,1,0:T(8,128)(2,1)S(1)}, u32[]{:S(2)}, u32[]{:S(2)}) async-start(bf16[16,48,2048]{2,1,0:T(8,128)(2,1)} %copy-done), calls=%async_computation | async-start | bytes 6291456 | tf_op jit(solution)/shard_map/all_to_all | solution.py:279
  15.6 10.6 %collective-permute-start.1 = (bf16[1,112,2048]{2,1,0:T(8,128)(2,1)}, bf16[1,112,2048]{2,1,0:T(8,128)(2,1)S(1)}, u32[]{:S(2)}, u32[]{:S(2)}) collective-permute-start(bf16[1,112,2048]{2,1,0:T(8,128)(2,1)} %get-tuple-element.25.refs_0_), channel_id=1, source_target_pairs={{0,2},{2,4},{4,6},{6,8},{8,10},{10,12},{12,14},{14,0},{16,30},{18,... | collective-permute-start | bytes 1376264 | tf_op jit(solution)/shard_map/ppermute | solution.py:242
  26.2 0.8 copy-start.5
  26.2 19.7 %collective-permute-start.2 = (bf16[2,112,2048]{2,1,0:T(8,128)(2,1)}, bf16[2,112,2048]{2,1,0:T(8,128)(2,1)}, u32[]{:S(2)}, u32[]{:S(2)}) collective-permute-start(bf16[2,112,2048]{2,1,0:T(8,128)(2,1)} %collective-permute-done.refs_1_), channel_id=1, source_target_pairs={{0,2},{2,4},{4,6},{6,8},{8,10},{10,12},{12,14},{14,0},{16,30},{18,... | collective-permute-start | bytes 2752520 | tf_op jit(solution)/shard_map/ppermute | solution.py:242
  27.0 18.9 %collective-permute-start.3 = (bf16[1,112,2048]{2,1,0:T(8,128)(2,1)S(1)}, bf16[1,112,2048]{2,1,0:T(8,128)(2,1)S(1)}, u32[]{:S(2)}, u32[]{:S(2)}) collective-permute-start(bf16[1,112,2048]{2,1,0:T(8,128)(2,1)S(1)} %collective-permute-done.1.refs_1_), channel_id=1, source_target_pairs={{0,2},{2,4},{4,6},{6,8},{8,10},{10,12},{12,14},{14,0},{16,30},{18,... | collective-permute-start | bytes 1376264 | tf_op jit(solution)/shard_map/ppermute | solution.py:242
  45.9 1.2 copy-start.7
  45.9 19.8 %collective-permute-start.4 = (bf16[2,112,2048]{2,1,0:T(8,128)(2,1)}, bf16[2,112,2048]{2,1,0:T(8,128)(2,1)}, u32[]{:S(2)}, u32[]{:S(2)}) collective-permute-start(bf16[2,112,2048]{2,1,0:T(8,128)(2,1)} %collective-permute-done.2.refs_3_), channel_id=1, source_target_pairs={{0,2},{2,4},{4,6},{6,8},{8,10},{10,12},{12,14},{14,0},{16,30},{18,... | collective-permute-start | bytes 2752520 | tf_op jit(solution)/shard_map/ppermute | solution.py:242
  45.9 22.6 %collective-permute-start.8 = (bf16[2,112,2048]{2,1,0:T(8,128)(2,1)}, bf16[2,112,2048]{2,1,0:T(8,128)(2,1)}, u32[]{:S(2)}, u32[]{:S(2)}) collective-permute-start(bf16[2,112,2048]{2,1,0:T(8,128)(2,1)} %collective-permute-done.refs_1_), channel_id=1, source_target_pairs={{0,16},{16,0},{1,17},{17,1},{2,18},{18,2},{3,19},{19,3},{4,20},{20... | collective-permute-start | bytes 2752520 | tf_op jit(solution)/shard_map/ppermute | solution.py:246
  47.2 21.4 %collective-permute-start.9 = (bf16[2,112,2048]{2,1,0:T(8,128)(2,1)}, bf16[2,112,2048]{2,1,0:T(8,128)(2,1)}, u32[]{:S(2)}, u32[]{:S(2)}) collective-permute-start(bf16[2,112,2048]{2,1,0:T(8,128)(2,1)} %collective-permute-done.2.refs_3_), channel_id=1, source_target_pairs={{0,16},{16,0},{1,17},{17,1},{2,18},{18,2},{3,19},{19,3},{4,20},{20... | collective-permute-start | bytes 2752520 | tf_op jit(solution)/shard_map/ppermute | solution.py:246
  47.2 18.6 %collective-permute-start.5 = (bf16[1,112,2048]{2,1,0:T(8,128)(2,1)S(1)}, bf16[1,112,2048]{2,1,0:T(8,128)(2,1)}, u32[]{:S(2)}, u32[]{:S(2)}) collective-permute-start(bf16[1,112,2048]{2,1,0:T(8,128)(2,1)S(1)} %collective-permute-done.3.refs_3_), channel_id=1, source_target_pairs={{0,2},{2,4},{4,6},{6,8},{8,10},{10,12},{12,14},{14,0},{16,30},{18,... | collective-permute-start | bytes 1376264 | tf_op jit(solution)/shard_map/ppermute | solution.py:242
  65.8 15.1 %collective-permute-start.10 = (bf16[2,112,2048]{2,1,0:T(8,128)(2,1)}, bf16[2,112,2048]{2,1,0:T(8,128)(2,1)}, u32[]{:S(2)}, u32[]{:S(2)}) collective-permute-start(bf16[2,112,2048]{2,1,0:T(8,128)(2,1)} %collective-permute-done.4.refs_0_), channel_id=1, source_target_pairs={{0,16},{16,0},{1,17},{17,1},{2,18},{18,2},{3,19},{19,3},{4,20},{20... | collective-permute-start | bytes 2752520 | tf_op jit(solution)/shard_map/ppermute | solution.py:246
  68.0 12.4 %collective-permute-start.6 = (bf16[2,112,1024]{2,1,0:T(8,128)(2,1)}, bf16[2,112,1024]{2,1,0:T(8,128)(2,1)}, u32[]{:S(2)}, u32[]{:S(2)}) collective-permute-start(bf16[2,112,1024]{2,1,0:T(8,128)(2,1)} %get-tuple-element.32), channel_id=1, source_target_pairs={{0,2},{2,4},{4,6},{6,8},{8,10},{10,12},{12,14},{14,0},{16,30},{18,... | collective-permute-start | bytes 1376264 | tf_op jit(solution)/shard_map/ppermute | solution.py:242
  68.0 16.8 %collective-permute-start.12 = (bf16[1,112,2048]{2,1,0:T(8,128)(2,1)}, bf16[1,112,2048]{2,1,0:T(8,128)(2,1)}, u32[]{:S(2)}, u32[]{:S(2)}) collective-permute-start(bf16[1,112,2048]{2,1,0:T(8,128)(2,1)} %copy-done.5), channel_id=1, source_target_pairs={{0,16},{16,0},{1,17},{17,1},{2,18},{18,2},{3,19},{19,3},{4,20},{20... | collective-permute-start | bytes 1376264 | tf_op jit(solution)/shard_map/ppermute | solution.py:246
  68.5 16.3 %collective-permute-start.13 = (bf16[1,112,2048]{2,1,0:T(8,128)(2,1)}, bf16[1,112,2048]{2,1,0:T(8,128)(2,1)}, u32[]{:S(2)}, u32[]{:S(2)}) collective-permute-start(bf16[1,112,2048]{2,1,0:T(8,128)(2,1)} %copy-done.7), channel_id=1, source_target_pairs={{0,16},{16,0},{1,17},{17,1},{2,18},{18,2},{3,19},{19,3},{4,20},{20... | collective-permute-start | bytes 1376264 | tf_op jit(solution)/shard_map/ppermute | solution.py:246
  68.6 11.7 %collective-permute-start.7 = (bf16[1,112,1024]{2,1,0:T(8,128)(2,1)}, bf16[1,112,1024]{2,1,0:T(8,128)(2,1)S(1)}, u32[]{:S(2)}, u32[]{:S(2)}) collective-permute-start(bf16[1,112,1024]{2,1,0:T(8,128)(2,1)} %get-tuple-element.33), channel_id=1, source_target_pairs={{0,2},{2,4},{4,6},{6,8},{8,10},{10,12},{12,14},{14,0},{16,30},{18,... | collective-permute-start | bytes 688136 | tf_op jit(solution)/shard_map/ppermute | solution.py:242
  70.5 1.2 copy-start.3
  78.2 1.0 copy-start.9
  80.4 4.5 %collective-permute-start.14 = (bf16[1,112,2048]{2,1,0:T(8,128)(2,1)}, bf16[1,112,2048]{2,1,0:T(8,128)(2,1)}, u32[]{:S(2)}, u32[]{:S(2)}) collective-permute-start(bf16[1,112,2048]{2,1,0:T(8,128)(2,1)} %collective-permute-done.5.refs_1_.refs_5_), channel_id=1, source_target_pairs={{0,16},{16,0},{1,17},{17,1},{2,18},{18,2},{3,19},{19,3},{4,20},{20... | collective-permute-start | bytes 1376264 | tf_op jit(solution)/shard_map/ppermute | solution.py:246
  80.4 4.4 %collective-permute-start.11 = (bf16[2,112,1024]{2,1,0:T(8,128)(2,1)}, bf16[2,112,1024]{2,1,0:T(8,128)(2,1)}, u32[]{:S(2)}, u32[]{:S(2)}) collective-permute-start(bf16[2,112,1024]{2,1,0:T(8,128)(2,1)} %collective-permute-done.6.own_ref), channel_id=1, source_target_pairs={{0,16},{16,0},{1,17},{17,1},{2,18},{18,2},{3,19},{19,3},{4,20},{20... | collective-permute-start | bytes 1376264 | tf_op jit(solution)/shard_map/ppermute | solution.py:246
  80.9 3.9 %collective-permute-start.15 = (bf16[1,112,1024]{2,1,0:T(8,128)(2,1)S(1)}, bf16[1,112,1024]{2,1,0:T(8,128)(2,1)S(1)}, u32[]{:S(2)}, u32[]{:S(2)}) collective-permute-start(bf16[1,112,1024]{2,1,0:T(8,128)(2,1)S(1)} %collective-permute-done.7.refs_7_), channel_id=1, source_target_pairs={{0,16},{16,0},{1,17},{17,1},{2,18},{18,2},{3,19},{19,3},{4,20},{20... | collective-permute-start | bytes 688136 | tf_op jit(solution)/shard_map/ppermute | solution.py:246
  81.1 3.8 %copy-start.4 = (bf16[1,112,2048]{2,1,0:T(8,128)(2,1)S(1)}, bf16[1,112,2048]{2,1,0:T(8,128)(2,1)}, u32[]{:S(2)}) copy-start(bf16[1,112,2048]{2,1,0:T(8,128)(2,1)} %get-tuple-element.25.refs_0_) | copy-start | bytes 1376260
  81.1 3.8 %copy-start.6 = (bf16[1,112,2048]{2,1,0:T(8,128)(2,1)S(1)}, bf16[1,112,2048]{2,1,0:T(8,128)(2,1)}, u32[]{:S(2)}) copy-start(bf16[1,112,2048]{2,1,0:T(8,128)(2,1)} %copy-done.5) | copy-start | bytes 1376260
  81.1 3.8 %copy-start.8 = (bf16[1,112,2048]{2,1,0:T(8,128)(2,1)S(1)}, bf16[1,112,2048]{2,1,0:T(8,128)(2,1)}, u32[]{:S(2)}) copy-start(bf16[1,112,2048]{2,1,0:T(8,128)(2,1)} %copy-done.7) | copy-start | bytes 1376260
  81.1 3.8 %copy-start.10 = (bf16[768,640]{1,0:T(8,128)(2,1)S(1)}, bf16[768,640]{1,0:T(8,128)(2,1)}, u32[]{:S(2)}) copy-start(bf16[768,640]{1,0:T(8,128)(2,1)} %copy-done.9) | copy-start | bytes 2949124
  93.3 8.4 %collective-permute-start.22 = (bf16[2,48,1280]{2,1,0:T(8,128)(2,1)S(1)}, bf16[2,48,1280]{2,1,0:T(8,128)(2,1)S(1)}, u32[]{:S(2)}, u32[]{:S(2)}) collective-permute-start(bf16[2,48,1280]{2,1,0:T(8,128)(2,1)S(1)} %get-tuple-element.41), channel_id=1, source_target_pairs={{0,128},{128,1},{1,129},{129,0},{2,130},{130,3},{3,131},{131,2},{4... | collective-permute-start | bytes 737288 | tf_op jit(solution)/shard_map/ppermute | solution.py:251
  93.9 9.3 %collective-permute-start.24 = (bf16[2,48,1280]{2,1,0:T(8,128)(2,1)S(1)}, bf16[2,48,1280]{2,1,0:T(8,128)(2,1)S(1)}, u32[]{:S(2)}, u32[]{:S(2)}) collective-permute-start(bf16[2,48,1280]{2,1,0:T(8,128)(2,1)S(1)} %get-tuple-element.42), channel_id=1, source_target_pairs={{0,129},{128,0},{1,128},{129,1},{2,131},{130,2},{3,130},{131,3},{4... | collective-permute-start | bytes 737288 | tf_op jit(solution)/shard_map/ppermute | solution.py:251
  95.5 11.3 %collective-permute-start.17 = (bf16[4,48,768]{2,1,0:T(8,128)(2,1)S(1)}, bf16[4,48,768]{2,1,0:T(8,128)(2,1)S(1)}, u32[]{:S(2)}, u32[]{:S(2)}) collective-permute-start(bf16[4,48,768]{2,1,0:T(8,128)(2,1)S(1)} %get-tuple-element.47), channel_id=1, source_target_pairs={{0,32},{32,64},{64,96},{96,0},{1,33},{33,65},{65,97},{97,1},{2,34}... | collective-permute-start | bytes 884744 | tf_op jit(solution)/shard_map/ppermute | solution.py:257
  96.1 16.1 %collective-permute-start.18 = (bf16[4,48,768]{2,1,0:T(8,128)(2,1)S(1)}, bf16[4,48,768]{2,1,0:T(8,128)(2,1)S(1)}, u32[]{:S(2)}, u32[]{:S(2)}) collective-permute-start(bf16[4,48,768]{2,1,0:T(8,128)(2,1)S(1)} %get-tuple-element.46), channel_id=1, source_target_pairs={{0,96},{32,0},{64,32},{96,64},{1,97},{33,1},{65,33},{97,65},{2,98}... | collective-permute-start | bytes 884744 | tf_op jit(solution)/shard_map/ppermute | solution.py:257
  97.6 14.7 %collective-permute-start.16 = (bf16[4,48,768]{2,1,0:T(8,128)(2,1)S(1)}, bf16[4,48,768]{2,1,0:T(8,128)(2,1)S(1)}, u32[]{:S(2)}, u32[]{:S(2)}) collective-permute-start(bf16[4,48,768]{2,1,0:T(8,128)(2,1)S(1)} %get-tuple-element.45), channel_id=1, source_target_pairs={{0,64},{32,96},{64,0},{96,32},{1,65},{33,97},{65,1},{97,33},{2,66}... | collective-permute-start | bytes 884744 | tf_op jit(solution)/shard_map/ppermute | solution.py:257
  103.3 15.8 %collective-permute-start.25 = (bf16[4,48,1280]{2,1,0:T(8,128)(2,1)S(1)}, bf16[4,48,1280]{2,1,0:T(8,128)(2,1)S(1)}, u32[]{:S(2)}, u32[]{:S(2)}) collective-permute-start(bf16[4,48,1280]{2,1,0:T(8,128)(2,1)S(1)} %pad_maximum_fusion.1), channel_id=1, source_target_pairs={{0,129},{128,0},{1,128},{129,1},{2,131},{130,2},{3,130},{131,3},{4... | collective-permute-start | bytes 1474568 | tf_op jit(solution)/shard_map/ppermute | solution.py:251
  103.7 16.0 %collective-permute-start.23 = (bf16[4,48,1280]{2,1,0:T(8,128)(2,1)S(1)}, bf16[4,48,1280]{2,1,0:T(8,128)(2,1)S(1)}, u32[]{:S(2)}, u32[]{:S(2)}) collective-permute-start(bf16[4,48,1280]{2,1,0:T(8,128)(2,1)S(1)} %pad_maximum_fusion), channel_id=1, source_target_pairs={{0,128},{128,1},{1,129},{129,0},{2,130},{130,3},{3,131},{131,2},{4... | collective-permute-start | bytes 1474568 | tf_op jit(solution)/shard_map/ppermute | solution.py:251
  112.4 18.8 %copy-start.2 = (s32[2]{0:T(128)S(1)}, s32[2]{0:T(128)}, u32[]{:S(2)}) copy-start(s32[2]{0:T(128)} %pad_add_fusion.1.at_ref) | copy-start | bytes 28
  112.4 12.7 %collective-permute-start.19 = (bf16[2,48,768]{2,1,0:T(8,128)(2,1)S(1)}, bf16[2,48,768]{2,1,0:T(8,128)(2,1)S(1)}, u32[]{:S(2)}, u32[]{:S(2)}) collective-permute-start(bf16[2,48,768]{2,1,0:T(8,128)(2,1)S(1)} %pad_maximum_fusion.3), channel_id=1, source_target_pairs={{0,128},{128,1},{1,129},{129,0},{2,130},{130,3},{3,131},{131,2},{4... | collective-permute-start | bytes 442376 | tf_op jit(solution)/shard_map/ppermute | solution.py:251
  114.3 10.8 %collective-permute-start.20 = (bf16[2,48,768]{2,1,0:T(8,128)(2,1)S(1)}, bf16[2,48,768]{2,1,0:T(8,128)(2,1)S(1)}, u32[]{:S(2)}, u32[]{:S(2)}) collective-permute-start(bf16[2,48,768]{2,1,0:T(8,128)(2,1)S(1)} %pad_maximum_fusion.4), channel_id=1, source_target_pairs={{0,1},{128,129},{1,0},{129,128},{2,3},{130,131},{3,2},{131,130},{4... | collective-permute-start | bytes 442376 | tf_op jit(solution)/shard_map/ppermute | solution.py:251
  115.5 9.6 %collective-permute-start.21 = (bf16[2,48,768]{2,1,0:T(8,128)(2,1)S(1)}, bf16[2,48,768]{2,1,0:T(8,128)(2,1)S(1)}, u32[]{:S(2)}, u32[]{:S(2)}) collective-permute-start(bf16[2,48,768]{2,1,0:T(8,128)(2,1)S(1)} %pad_maximum_fusion.5), channel_id=1, source_target_pairs={{0,129},{128,0},{1,128},{129,1},{2,131},{130,2},{3,130},{131,3},{4... | collective-permute-start | bytes 442376 | tf_op jit(solution)/shard_map/ppermute | solution.py:251
  119.8 6.5 %collective-permute-start.26 = (bf16[48,1280]{1,0:T(8,128)(2,1)S(1)}, bf16[48,1280]{1,0:T(8,128)(2,1)S(1)}, u32[]{:S(2)}, u32[]{:S(2)}) collective-permute-start(bf16[48,1280]{1,0:T(8,128)(2,1)S(1)} %get-tuple-element.50), channel_id=1, source_target_pairs={{0,64},{32,96},{64,0},{96,32},{1,65},{33,97},{65,1},{97,33},{2,66}... | collective-permute-start | bytes 368648 | tf_op jit(solution)/shard_map/ppermute | solution.py:257
  121.4 6.2 %collective-permute-start.27 = (bf16[48,1280]{1,0:T(8,128)(2,1)S(1)}, bf16[48,1280]{1,0:T(8,128)(2,1)S(1)}, u32[]{:S(2)}, u32[]{:S(2)}) collective-permute-start(bf16[48,1280]{1,0:T(8,128)(2,1)S(1)} %get-tuple-element.49), channel_id=1, source_target_pairs={{0,32},{32,64},{64,96},{96,0},{1,33},{33,65},{65,97},{97,1},{2,34}... | collective-permute-start | bytes 368648 | tf_op jit(solution)/shard_map/ppermute | solution.py:257
  125.1 6.1 %collective-permute-start.28 = (bf16[48,1280]{1,0:T(8,128)(2,1)S(1)}, bf16[48,1280]{1,0:T(8,128)(2,1)S(1)}, u32[]{:S(2)}, u32[]{:S(2)}) collective-permute-start(bf16[48,1280]{1,0:T(8,128)(2,1)S(1)} %get-tuple-element.48), channel_id=1, source_target_pairs={{0,96},{32,0},{64,32},{96,64},{1,97},{33,1},{65,33},{97,65},{2,98}... | collective-permute-start | bytes 368648 | tf_op jit(solution)/shard_map/ppermute | solution.py:257

commit v6 on v5

--- a/solution.py
+++ b/solution.py
@@ -12,7 +12,7 @@
 CAP = 48
 PLANE = ("xl", "y", "xh")
 VMEM = 20 * 1024 * 1024
-GRANT = 30 * 1024 * 1024
+GRANT = 18 * 1024 * 1024
 LANES = 128
 SIDE = 4
 TILE = 256

time: 135 us -> 135 us (level)
  no operation moved by 1% of the time
where the time goes in v6:
time: 135 us; the launch traced here: 133 us
  waiting for transfers between devices  64.6 us (48%)
  starting transfers between devices  35.5 us (26%)
  Pallas kernels  26.9 us (20%)
  local copies, waits for them, and re-layouts  5.04 us (4%)
    ppermute x8, waiting for transfers between devices, along_z(): return lax.ppermute(value, ('c', 'z'), pairs)  44.8 us
    ppermute x6, waiting for transfers between devices, along_y(): lax.ppermute(value, 'y', [(y, (y + step) % SIDE) for y in range(SIDE)])  11.5 us
    pallas_call x2, Pallas kernels, hidden_units(): pl.pallas_call(hidden_kernel, in_specs=[whole] * (1 + len(pieces)), out_s...  10.2 us
    ppermute x6, starting transfers between devices, along_y(): lax.ppermute(value, 'y', [(y, (y + step) % SIDE) for y in range(SIDE)])  8.85 us
    ppermute x7, starting transfers between devices, along_x(): lax.ppermute(value, ('xl', 'xh'), [(places[x], places[(x + step) % SIDE])...  8.66 us
    ppermute x8, starting transfers between devices, along_z(): return lax.ppermute(value, ('c', 'z'), pairs)  8.41 us
    pallas_call x1, Pallas kernels, finish(): pl.pallas_call(finish_kernel, in_specs=[scalars] * 2 + [whole] * 5 + [any...  8.33 us
    ppermute x7, waiting for transfers between devices, along_x(): lax.ppermute(value, ('xl', 'xh'), [(places[x], places[(x + step) % SIDE])...  8.27 us
  transfers between devices with their start and end apart: 30, of which 12 were waited for; matrix products, arithmetic and copies ran while one was open for 1% of the time, Pallas kernels for 10%

profile of v6, /device:TPU:30, one launch (start us, length us, event | category | flops | bytes accessed | tf_op | source)
XLA Modules:
  0.0 133.3 jit_solution(602200833009856505)
XLA Ops:
  0.0 0.6 pad_add_fusion.1.at_ref
  0.6 3.2 %pack_weights.1 = (bf16[2,112,2048]{2,1,0:T(8,128)(2,1)}, bf16[1,112,2048]{2,1,0:T(8,128)(2,1)}) custom-call(s32[2]{0:T(128)} %pad_add_fusion.1.at_ref, bf16[2,448,2048]{2,1,0:T(8,128)(2,1)} %gate_ref.1, bf16[2,448,2048]{2,1,0:T(8,128)(2,1)} %up_ref.1, bf16[2,448,2048]{2,1,0:T(8,128)(2,1)} %down_ref.1), custom_call_target="tpu_custom_call" | custom-call | tf_op jit(solution)/shard_map/pack_weights/pallas_call | solution.py:90
  3.8 2.0 %collective-permute-start = (bf16[2,112,2048]{2,1,0:T(8,128)(2,1)}, bf16[2,112,2048]{2,1,0:T(8,128)(2,1)}, u32[]{:S(2)}, u32[]{:S(2)}) collective-permute-start(bf16[2,112,2048]{2,1,0:T(8,128)(2,1)} %get-tuple-element.24.refs_0_), channel_id=1, source_target_pairs={{0,2},{2,4},{4,6},{6,8},{8,10},{10,12},{12,14},{14,0},{16,30},{18,... | collective-permute-start | bytes 2752520 | tf_op jit(solution)/shard_map/ppermute | solution.py:242
  5.8 0.1 copy.7.ids_ref
  5.9 0.1 copy.8.logits_ref
  6.0 0.8 pick_rows.1
  6.9 1.6 %copy-done = bf16[16,48,2048]{2,1,0:T(8,128)(2,1)} copy-done((bf16[16,48,2048]{2,1,0:T(8,128)(2,1)}, bf16[16,48,2048]{2,1,0:T(8,128)(2,1)S(1)}, u32[]{:S(2)}) %copy-start) | copy-done | bytes 3145752
  8.5 7.1 %all-to-all-start = ((bf16[16,48,2048]{2,1,0:T(8,128)(2,1)}), bf16[16,48,2048]{2,1,0:T(8,128)(2,1)S(1)}, u32[]{:S(2)}, u32[]{:S(2)}) async-start(bf16[16,48,2048]{2,1,0:T(8,128)(2,1)} %copy-done), calls=%async_computation | async-start | bytes 6291456 | tf_op jit(solution)/shard_map/all_to_all | solution.py:279
  15.6 1.9 %collective-permute-start.1 = (bf16[1,112,2048]{2,1,0:T(8,128)(2,1)}, bf16[1,112,2048]{2,1,0:T(8,128)(2,1)S(1)}, u32[]{:S(2)}, u32[]{:S(2)}) collective-permute-start(bf16[1,112,2048]{2,1,0:T(8,128)(2,1)} %get-tuple-element.25.refs_0_), channel_id=1, source_target_pairs={{0,2},{2,4},{4,6},{6,8},{8,10},{10,12},{12,14},{14,0},{16,30},{18,... | collective-permute-start | bytes 1376264 | tf_op jit(solution)/shard_map/ppermute | solution.py:242
  17.5 8.7 %collective-permute-done.1.refs_1_ = bf16[1,112,2048]{2,1,0:T(8,128)(2,1)S(1)} collective-permute-done((bf16[1,112,2048]{2,1,0:T(8,128)(2,1)}, bf16[1,112,2048]{2,1,0:T(8,128)(2,1)S(1)}, u32[]{:S(2)}, u32[]{:S(2)}) %collective-permute-start.1) | collective-permute-done | bytes 458784 | tf_op jit(solution)/shard_map/ppermute | solution.py:242
  26.2 0.8 copy-done.5
  27.0 1.9 %collective-permute-start.3 = (bf16[1,112,2048]{2,1,0:T(8,128)(2,1)S(1)}, bf16[1,112,2048]{2,1,0:T(8,128)(2,1)S(1)}, u32[]{:S(2)}, u32[]{:S(2)}) collective-permute-start(bf16[1,112,2048]{2,1,0:T(8,128)(2,1)S(1)} %collective-permute-done.1.refs_1_), channel_id=1, source_target_pairs={{0,2},{2,4},{4,6},{6,8},{8,10},{10,12},{12,14},{14,0},{16,30},{18,... | collective-permute-start | bytes 1376264 | tf_op jit(solution)/shard_map/ppermute | solution.py:242
  28.9 17.1 %collective-permute-done.3.refs_3_ = bf16[1,112,2048]{2,1,0:T(8,128)(2,1)S(1)} collective-permute-done((bf16[1,112,2048]{2,1,0:T(8,128)(2,1)S(1)}, bf16[1,112,2048]{2,1,0:T(8,128)(2,1)S(1)}, u32[]{:S(2)}, u32[]{:S(2)}) %collective-permute-start.3) | collective-permute-done | bytes 458784 | tf_op jit(solution)/shard_map/ppermute | solution.py:242
  45.9 1.2 collective-permute-start.8
  47.2 0.0 collective-permute-start.9
  47.2 0.7 collective-permute-start.5
  47.9 17.9 %collective-permute-done.5.refs_1_.refs_5_ = bf16[1,112,2048]{2,1,0:T(8,128)(2,1)} collective-permute-done((bf16[1,112,2048]{2,1,0:T(8,128)(2,1)S(1)}, bf16[1,112,2048]{2,1,0:T(8,128)(2,1)}, u32[]{:S(2)}, u32[]{:S(2)}) %collective-permute-start.5) | collective-permute-done | bytes 458784 | tf_op jit(solution)/shard_map/ppermute | solution.py:242
  65.8 0.0 collective-permute-done.4.refs_0_
  65.8 0.0 collective-permute-start.10
  65.8 2.2 %halve_pieces.1 = (bf16[2,112,1024]{2,1,0:T(8,128)(2,1)}, bf16[1,112,1024]{2,1,0:T(8,128)(2,1)}) custom-call(s32[1]{0:T(128)} %bitcast.2.core_ref, bf16[2,112,2048]{2,1,0:T(8,128)(2,1)} %collective-permute-done.4.refs_0_, bf16[1,112,2048]{2,1,0:T(8,128)(2,1)} %collective-permute-done.5.refs_1_.refs_5_), custom_call_target="tpu_custom_call" | custom-call | tf_op jit(solution)/shard_map/halve_pieces/pallas_call | solution.py:111
  68.0 0.0 collective-permute-start.6
  68.0 0.5 collective-permute-start.12
  68.5 0.0 collective-permute-done.8.refs_2_
  68.5 0.1 collective-permute-start.13
  68.6 0.0 collective-permute-done.9.refs_4_
  68.6 1.9 %collective-permute-start.7 = (bf16[1,112,1024]{2,1,0:T(8,128)(2,1)}, bf16[1,112,1024]{2,1,0:T(8,128)(2,1)S(1)}, u32[]{:S(2)}, u32[]{:S(2)}) collective-permute-start(bf16[1,112,1024]{2,1,0:T(8,128)(2,1)} %get-tuple-element.33), channel_id=1, source_target_pairs={{0,2},{2,4},{4,6},{6,8},{8,10},{10,12},{12,14},{14,0},{16,30},{18,... | collective-permute-start | bytes 688136 | tf_op jit(solution)/shard_map/ppermute | solution.py:242
  70.5 1.2 copy-done.3
  71.7 6.5 %hidden_units.2.early_ref = bf16[768,640]{1,0:T(8,128)(2,1)S(1)} custom-call(bf16[768,2048]{1,0:T(8,128)(2,1)S(1)} %bitcast.36, bf16[2,112,2048]{2,1,0:T(8,128)(2,1)S(1)} %copy-done.3, bf16[2,112,2048]{2,1,0:T(8,128)(2,1)} %collective-permute-done.refs_1_, bf16[2,112,2048]{2,1,0:T(8,128)(2,1)} %collective-permute-done.8.refs_2_, ...), custom_call_target="tpu_custom_call" | custom-call | flops 3523215360 | bytes 7733248 | tf_op jit(solution)/shard_map/hidden_units/pallas_call | solution.py:157
  78.2 1.0 copy-done.9
  79.2 1.2 collective-permute-done.7.refs_7_
  80.4 0.1 collective-permute-start.14
  80.4 0.0 collective-permute-done.6.own_ref
  80.4 0.4 collective-permute-start.11
  80.9 0.0 collective-permute-done.10.refs_1_
  80.9 0.2 collective-permute-start.15
  81.1 3.7 %hidden_units.3.late_ref = bf16[768,256]{1,0:T(8,128)(2,1)S(1)} custom-call(bf16[768,2048]{1,0:T(8,128)(2,1)S(1)} %bitcast.37, bf16[2,112,2048]{2,1,0:T(8,128)(2,1)} %collective-permute-done.4.refs_0_, bf16[2,112,2048]{2,1,0:T(8,128)(2,1)} %collective-permute-done.10.refs_1_), custom_call_target="tpu_custom_call" | custom-call | flops 1409286144 | bytes 4980736 | tf_op jit(solution)/shard_map/hidden_units/pallas_call | solution.py:157
  84.8 0.0 collective-permute-done.13.refs_4_
  84.9 8.3 %finish_terms.1 = (bf16[4,4,48,768]{3,2,1,0:T(8,128)(2,1)S(1)}, bf16[4,4,48,1280]{3,2,1,0:T(8,128)(2,1)S(1)}) custom-call(s32[1]{0:T(128)} %bitcast.2.core_ref, s32[2,16]{1,0:T(2,128)S(1)} %pad_add_fusion.spots_ref, bf16[768,2048]{1,0:T(8,128)(2,1)S(1)} %bitcast.38, bf16[768,640]{1,0:T(8,128)(2,1)S(1)} %copy-done.10, ...), custom_call_target="tpu_custom_call" | custom-call | flops 3523215360 | bytes 9502720 | tf_op jit(solution)/shard_map/finish_terms/pallas_call | solution.py:221
  93.2 0.1 slice_bitcast_fusion.6
  93.3 0.6 collective-permute-start.22
  93.9 1.5 %collective-permute-start.24 = (bf16[2,48,1280]{2,1,0:T(8,128)(2,1)S(1)}, bf16[2,48,1280]{2,1,0:T(8,128)(2,1)S(1)}, u32[]{:S(2)}, u32[]{:S(2)}) collective-permute-start(bf16[2,48,1280]{2,1,0:T(8,128)(2,1)S(1)} %get-tuple-element.42), channel_id=1, source_target_pairs={{0,129},{128,0},{1,128},{129,1},{2,131},{130,2},{3,130},{131,3},{4... | collective-permute-start | bytes 737288 | tf_op jit(solution)/shard_map/ppermute | solution.py:251
  95.4 0.1 slice_bitcast_fusion.2
  95.5 0.6 collective-permute-start.17
  96.1 1.5 %collective-permute-start.18 = (bf16[4,48,768]{2,1,0:T(8,128)(2,1)S(1)}, bf16[4,48,768]{2,1,0:T(8,128)(2,1)S(1)}, u32[]{:S(2)}, u32[]{:S(2)}) collective-permute-start(bf16[4,48,768]{2,1,0:T(8,128)(2,1)S(1)} %get-tuple-element.46), channel_id=1, source_target_pairs={{0,96},{32,0},{64,32},{96,64},{1,97},{33,1},{65,33},{97,65},{2,98}... | collective-permute-start | bytes 884744 | tf_op jit(solution)/shard_map/ppermute | solution.py:257
  97.6 1.5 %collective-permute-start.16 = (bf16[4,48,768]{2,1,0:T(8,128)(2,1)S(1)}, bf16[4,48,768]{2,1,0:T(8,128)(2,1)S(1)}, u32[]{:S(2)}, u32[]{:S(2)}) collective-permute-start(bf16[4,48,768]{2,1,0:T(8,128)(2,1)S(1)} %get-tuple-element.45), channel_id=1, source_target_pairs={{0,64},{32,96},{64,0},{96,32},{1,65},{33,97},{65,1},{97,33},{2,66}... | collective-permute-start | bytes 884744 | tf_op jit(solution)/shard_map/ppermute | solution.py:257
  99.0 2.6 %collective-permute-done.22 = bf16[2,48,1280]{2,1,0:T(8,128)(2,1)S(1)} collective-permute-done((bf16[2,48,1280]{2,1,0:T(8,128)(2,1)S(1)}, bf16[2,48,1280]{2,1,0:T(8,128)(2,1)S(1)}, u32[]{:S(2)}, u32[]{:S(2)}) %collective-permute-start.22) | collective-permute-done | bytes 245792 | tf_op jit(solution)/shard_map/ppermute | solution.py:251
  101.7 1.5 %collective-permute-done.24 = bf16[2,48,1280]{2,1,0:T(8,128)(2,1)S(1)} collective-permute-done((bf16[2,48,1280]{2,1,0:T(8,128)(2,1)S(1)}, bf16[2,48,1280]{2,1,0:T(8,128)(2,1)S(1)}, u32[]{:S(2)}, u32[]{:S(2)}) %collective-permute-start.24) | collective-permute-done | bytes 245792 | tf_op jit(solution)/shard_map/ppermute | solution.py:251
  103.2 0.1 bitcast_add_fusion.3
  103.3 0.3 collective-permute-start.25
  103.7 3.1 %collective-permute-start.23 = (bf16[4,48,1280]{2,1,0:T(8,128)(2,1)S(1)}, bf16[4,48,1280]{2,1,0:T(8,128)(2,1)S(1)}, u32[]{:S(2)}, u32[]{:S(2)}) collective-permute-start(bf16[4,48,1280]{2,1,0:T(8,128)(2,1)S(1)} %pad_maximum_fusion), channel_id=1, source_target_pairs={{0,128},{128,1},{1,129},{129,0},{2,130},{130,3},{3,131},{131,2},{4... | collective-permute-start | bytes 1474568 | tf_op jit(solution)/shard_map/ppermute | solution.py:251
  106.8 5.4 %collective-permute-done.18 = bf16[4,48,768]{2,1,0:T(8,128)(2,1)S(1)} collective-permute-done((bf16[4,48,768]{2,1,0:T(8,128)(2,1)S(1)}, bf16[4,48,768]{2,1,0:T(8,128)(2,1)S(1)}, u32[]{:S(2)}, u32[]{:S(2)}) %collective-permute-start.18) | collective-permute-done | bytes 294944 | tf_op jit(solution)/shard_map/ppermute | solution.py:257
  112.2 0.1 add.110
  112.4 1.9 %collective-permute-start.19 = (bf16[2,48,768]{2,1,0:T(8,128)(2,1)S(1)}, bf16[2,48,768]{2,1,0:T(8,128)(2,1)S(1)}, u32[]{:S(2)}, u32[]{:S(2)}) collective-permute-start(bf16[2,48,768]{2,1,0:T(8,128)(2,1)S(1)} %pad_maximum_fusion.3), channel_id=1, source_target_pairs={{0,128},{128,1},{1,129},{129,0},{2,130},{130,3},{3,131},{131,2},{4... | collective-permute-start | bytes 442376 | tf_op jit(solution)/shard_map/ppermute | solution.py:251
  114.3 1.2 collective-permute-start.20
  115.5 0.1 collective-permute-start.21
  115.6 3.5 %collective-permute-done.25 = bf16[4,48,1280]{2,1,0:T(8,128)(2,1)S(1)} collective-permute-done((bf16[4,48,1280]{2,1,0:T(8,128)(2,1)S(1)}, bf16[4,48,1280]{2,1,0:T(8,128)(2,1)S(1)}, u32[]{:S(2)}, u32[]{:S(2)}) %collective-permute-start.25) | collective-permute-done | bytes 491552 | tf_op jit(solution)/shard_map/ppermute | solution.py:251
  119.1 0.6 collective-permute-done.23
  119.7 0.1 fusion
  119.8 1.5 %collective-permute-start.26 = (bf16[48,1280]{1,0:T(8,128)(2,1)S(1)}, bf16[48,1280]{1,0:T(8,128)(2,1)S(1)}, u32[]{:S(2)}, u32[]{:S(2)}) collective-permute-start(bf16[48,1280]{1,0:T(8,128)(2,1)S(1)} %get-tuple-element.50), channel_id=1, source_target_pairs={{0,64},{32,96},{64,0},{96,32},{1,65},{33,97},{65,1},{97,33},{2,66}... | collective-permute-start | bytes 368648 | tf_op jit(solution)/shard_map/ppermute | solution.py:257
  121.4 3.7 %collective-permute-start.27 = (bf16[48,1280]{1,0:T(8,128)(2,1)S(1)}, bf16[48,1280]{1,0:T(8,128)(2,1)S(1)}, u32[]{:S(2)}, u32[]{:S(2)}) collective-permute-start(bf16[48,1280]{1,0:T(8,128)(2,1)S(1)} %get-tuple-element.49), channel_id=1, source_target_pairs={{0,32},{32,64},{64,96},{96,0},{1,33},{33,65},{65,97},{97,1},{2,34}... | collective-permute-start | bytes 368648 | tf_op jit(solution)/shard_map/ppermute | solution.py:257
  125.1 1.1 collective-permute-done.26.refs_5_
  126.3 1.3 collective-permute-done.27.refs_6_
  127.5 3.6 %collective-permute-done.28.refs_7_ = bf16[48,1280]{1,0:T(8,128)(2,1)S(1)} collective-permute-done((bf16[48,1280]{1,0:T(8,128)(2,1)S(1)}, bf16[48,1280]{1,0:T(8,128)(2,1)S(1)}, u32[]{:S(2)}, u32[]{:S(2)}) %collective-permute-start.28) | collective-permute-done | bytes 122912 | tf_op jit(solution)/shard_map/ppermute | solution.py:257
  131.2 2.1 %mix_terms.1 = bf16[128,2048]{1,0:T(8,128)(2,1)} custom-call(s32[2]{0:T(128)S(1)} %copy-done.2, bf16[2,128,48]{2,1,0:T(8,128)(2,1)S(1)} %get-tuple-element.22.place_ref, bf16[2,48,768]{2,1,0:T(8,128)(2,1)S(1)} %pad_maximum_fusion.2.refs_0_, bf16[2,48,768]{2,1,0:T(8,128)(2,1)S(1)} %collective-permute-done.19.refs_1_, ...), custom_call_target="tpu_custom_call" | custom-call | tf_op jit(solution)/shard_map/mix_terms/pallas_call | solution.py:354
  (49 shorter events, 0.4 us)
Async XLA Ops:
  0.6 5.2 %copy-start.11 = (s32[128,2]{0,1:T(2,128)S(1)}, s32[128,2]{0,1:T(2,128)}, u32[]{:S(2)}) copy-start(s32[128,2]{0,1:T(2,128)} %param.7) | copy-start | bytes 3076
  0.6 5.3 %copy-start.12 = (f32[128,2]{0,1:T(2,128)S(1)}, f32[128,2]{0,1:T(2,128)}, u32[]{:S(2)}) copy-start(f32[128,2]{0,1:T(2,128)} %param.8) | copy-start | bytes 3076
  0.6 5.4 %copy-start.1 = (bf16[128,2048]{1,0:T(8,128)(2,1)S(1)}, bf16[128,2048]{1,0:T(8,128)(2,1)}, u32[]{:S(2)}) copy-start(bf16[128,2048]{1,0:T(8,128)(2,1)} %tokens_ref.1) | copy-start | bytes 1572868
  3.8 22.4 %collective-permute-start = (bf16[2,112,2048]{2,1,0:T(8,128)(2,1)}, bf16[2,112,2048]{2,1,0:T(8,128)(2,1)}, u32[]{:S(2)}, u32[]{:S(2)}) collective-permute-start(bf16[2,112,2048]{2,1,0:T(8,128)(2,1)} %get-tuple-element.24.refs_0_), channel_id=1, source_target_pairs={{0,2},{2,4},{4,6},{6,8},{8,10},{10,12},{12,14},{14,0},{16,30},{18,... | collective-permute-start | bytes 2752520 | tf_op jit(solution)/shard_map/ppermute | solution.py:242
  6.8 1.6 %copy-start = (bf16[16,48,2048]{2,1,0:T(8,128)(2,1)}, bf16[16,48,2048]{2,1,0:T(8,128)(2,1)S(1)}, u32[]{:S(2)}) copy-start(bf16[16,48,2048]{2,1,0:T(8,128)(2,1)S(1)} %get-tuple-element.23) | copy-start | bytes 9437188
  8.5 62.0 %all-to-all-start = ((bf16[16,48,2048]{2,1,0:T(8,128)(2,1)}), bf16[16,48,2048]{2,1,0:T(8,128)(2,1)S(1)}, u32[]{:S(2)}, u32[]{:S(2)}) async-start(bf16[16,48,2048]{2,1,0:T(8,128)(2,1)} %copy-done), calls=%async_computation | async-start | bytes 6291456 | tf_op jit(solution)/shard_map/all_to_all | solution.py:279
  15.6 10.6 %collective-permute-start.1 = (bf16[1,112,2048]{2,1,0:T(8,128)(2,1)}, bf16[1,112,2048]{2,1,0:T(8,128)(2,1)S(1)}, u32[]{:S(2)}, u32[]{:S(2)}) collective-permute-start(bf16[1,112,2048]{2,1,0:T(8,128)(2,1)} %get-tuple-element.25.refs_0_), channel_id=1, source_target_pairs={{0,2},{2,4},{4,6},{6,8},{8,10},{10,12},{12,14},{14,0},{16,30},{18,... | collective-permute-start | bytes 1376264 | tf_op jit(solution)/shard_map/ppermute | solution.py:242
  26.2 0.8 copy-start.5
  26.2 19.7 %collective-permute-start.2 = (bf16[2,112,2048]{2,1,0:T(8,128)(2,1)}, bf16[2,112,2048]{2,1,0:T(8,128)(2,1)}, u32[]{:S(2)}, u32[]{:S(2)}) collective-permute-start(bf16[2,112,2048]{2,1,0:T(8,128)(2,1)} %collective-permute-done.refs_1_), channel_id=1, source_target_pairs={{0,2},{2,4},{4,6},{6,8},{8,10},{10,12},{12,14},{14,0},{16,30},{18,... | collective-permute-start | bytes 2752520 | tf_op jit(solution)/shard_map/ppermute | solution.py:242
  27.0 18.9 %collective-permute-start.3 = (bf16[1,112,2048]{2,1,0:T(8,128)(2,1)S(1)}, bf16[1,112,2048]{2,1,0:T(8,128)(2,1)S(1)}, u32[]{:S(2)}, u32[]{:S(2)}) collective-permute-start(bf16[1,112,2048]{2,1,0:T(8,128)(2,1)S(1)} %collective-permute-done.1.refs_1_), channel_id=1, source_target_pairs={{0,2},{2,4},{4,6},{6,8},{8,10},{10,12},{12,14},{14,0},{16,30},{18,... | collective-permute-start | bytes 1376264 | tf_op jit(solution)/shard_map/ppermute | solution.py:242
  45.9 1.2 copy-start.7
  45.9 19.8 %collective-permute-start.4 = (bf16[2,112,2048]{2,1,0:T(8,128)(2,1)}, bf16[2,112,2048]{2,1,0:T(8,128)(2,1)}, u32[]{:S(2)}, u32[]{:S(2)}) collective-permute-start(bf16[2,112,2048]{2,1,0:T(8,128)(2,1)} %collective-permute-done.2.refs_3_), channel_id=1, source_target_pairs={{0,2},{2,4},{4,6},{6,8},{8,10},{10,12},{12,14},{14,0},{16,30},{18,... | collective-permute-start | bytes 2752520 | tf_op jit(solution)/shard_map/ppermute | solution.py:242
  45.9 22.6 %collective-permute-start.8 = (bf16[2,112,2048]{2,1,0:T(8,128)(2,1)}, bf16[2,112,2048]{2,1,0:T(8,128)(2,1)}, u32[]{:S(2)}, u32[]{:S(2)}) collective-permute-start(bf16[2,112,2048]{2,1,0:T(8,128)(2,1)} %collective-permute-done.refs_1_), channel_id=1, source_target_pairs={{0,16},{16,0},{1,17},{17,1},{2,18},{18,2},{3,19},{19,3},{4,20},{20... | collective-permute-start | bytes 2752520 | tf_op jit(solution)/shard_map/ppermute | solution.py:246
  47.2 21.4 %collective-permute-start.9 = (bf16[2,112,2048]{2,1,0:T(8,128)(2,1)}, bf16[2,112,2048]{2,1,0:T(8,128)(2,1)}, u32[]{:S(2)}, u32[]{:S(2)}) collective-permute-start(bf16[2,112,2048]{2,1,0:T(8,128)(2,1)} %collective-permute-done.2.refs_3_), channel_id=1, source_target_pairs={{0,16},{16,0},{1,17},{17,1},{2,18},{18,2},{3,19},{19,3},{4,20},{20... | collective-permute-start | bytes 2752520 | tf_op jit(solution)/shard_map/ppermute | solution.py:246
  47.2 18.6 %collective-permute-start.5 = (bf16[1,112,2048]{2,1,0:T(8,128)(2,1)S(1)}, bf16[1,112,2048]{2,1,0:T(8,128)(2,1)}, u32[]{:S(2)}, u32[]{:S(2)}) collective-permute-start(bf16[1,112,2048]{2,1,0:T(8,128)(2,1)S(1)} %collective-permute-done.3.refs_3_), channel_id=1, source_target_pairs={{0,2},{2,4},{4,6},{6,8},{8,10},{10,12},{12,14},{14,0},{16,30},{18,... | collective-permute-start | bytes 1376264 | tf_op jit(solution)/shard_map/ppermute | solution.py:242
  65.8 15.1 %collective-permute-start.10 = (bf16[2,112,2048]{2,1,0:T(8,128)(2,1)}, bf16[2,112,2048]{2,1,0:T(8,128)(2,1)}, u32[]{:S(2)}, u32[]{:S(2)}) collective-permute-start(bf16[2,112,2048]{2,1,0:T(8,128)(2,1)} %collective-permute-done.4.refs_0_), channel_id=1, source_target_pairs={{0,16},{16,0},{1,17},{17,1},{2,18},{18,2},{3,19},{19,3},{4,20},{20... | collective-permute-start | bytes 2752520 | tf_op jit(solution)/shard_map/ppermute | solution.py:246
  68.0 12.4 %collective-permute-start.6 = (bf16[2,112,1024]{2,1,0:T(8,128)(2,1)}, bf16[2,112,1024]{2,1,0:T(8,128)(2,1)}, u32[]{:S(2)}, u32[]{:S(2)}) collective-permute-start(bf16[2,112,1024]{2,1,0:T(8,128)(2,1)} %get-tuple-element.32), channel_id=1, source_target_pairs={{0,2},{2,4},{4,6},{6,8},{8,10},{10,12},{12,14},{14,0},{16,30},{18,... | collective-permute-start | bytes 1376264 | tf_op jit(solution)/shard_map/ppermute | solution.py:242
  68.0 16.8 %collective-permute-start.12 = (bf16[1,112,2048]{2,1,0:T(8,128)(2,1)}, bf16[1,112,2048]{2,1,0:T(8,128)(2,1)}, u32[]{:S(2)}, u32[]{:S(2)}) collective-permute-start(bf16[1,112,2048]{2,1,0:T(8,128)(2,1)} %copy-done.5), channel_id=1, source_target_pairs={{0,16},{16,0},{1,17},{17,1},{2,18},{18,2},{3,19},{19,3},{4,20},{20... | collective-permute-start | bytes 1376264 | tf_op jit(solution)/shard_map/ppermute | solution.py:246
  68.5 16.3 %collective-permute-start.13 = (bf16[1,112,2048]{2,1,0:T(8,128)(2,1)}, bf16[1,112,2048]{2,1,0:T(8,128)(2,1)}, u32[]{:S(2)}, u32[]{:S(2)}) collective-permute-start(bf16[1,112,2048]{2,1,0:T(8,128)(2,1)} %copy-done.7), channel_id=1, source_target_pairs={{0,16},{16,0},{1,17},{17,1},{2,18},{18,2},{3,19},{19,3},{4,20},{20... | collective-permute-start | bytes 1376264 | tf_op jit(solution)/shard_map/ppermute | solution.py:246
  68.6 11.7 %collective-permute-start.7 = (bf16[1,112,1024]{2,1,0:T(8,128)(2,1)}, bf16[1,112,1024]{2,1,0:T(8,128)(2,1)S(1)}, u32[]{:S(2)}, u32[]{:S(2)}) collective-permute-start(bf16[1,112,1024]{2,1,0:T(8,128)(2,1)} %get-tuple-element.33), channel_id=1, source_target_pairs={{0,2},{2,4},{4,6},{6,8},{8,10},{10,12},{12,14},{14,0},{16,30},{18,... | collective-permute-start | bytes 688136 | tf_op jit(solution)/shard_map/ppermute | solution.py:242
  70.5 1.2 copy-start.3
  78.2 1.0 copy-start.9
  80.4 4.5 %collective-permute-start.14 = (bf16[1,112,2048]{2,1,0:T(8,128)(2,1)}, bf16[1,112,2048]{2,1,0:T(8,128)(2,1)}, u32[]{:S(2)}, u32[]{:S(2)}) collective-permute-start(bf16[1,112,2048]{2,1,0:T(8,128)(2,1)} %collective-permute-done.5.refs_1_.refs_5_), channel_id=1, source_target_pairs={{0,16},{16,0},{1,17},{17,1},{2,18},{18,2},{3,19},{19,3},{4,20},{20... | collective-permute-start | bytes 1376264 | tf_op jit(solution)/shard_map/ppermute | solution.py:246
  80.4 4.4 %collective-permute-start.11 = (bf16[2,112,1024]{2,1,0:T(8,128)(2,1)}, bf16[2,112,1024]{2,1,0:T(8,128)(2,1)}, u32[]{:S(2)}, u32[]{:S(2)}) collective-permute-start(bf16[2,112,1024]{2,1,0:T(8,128)(2,1)} %collective-permute-done.6.own_ref), channel_id=1, source_target_pairs={{0,16},{16,0},{1,17},{17,1},{2,18},{18,2},{3,19},{19,3},{4,20},{20... | collective-permute-start | bytes 1376264 | tf_op jit(solution)/shard_map/ppermute | solution.py:246
  80.9 3.9 %collective-permute-start.15 = (bf16[1,112,1024]{2,1,0:T(8,128)(2,1)S(1)}, bf16[1,112,1024]{2,1,0:T(8,128)(2,1)S(1)}, u32[]{:S(2)}, u32[]{:S(2)}) collective-permute-start(bf16[1,112,1024]{2,1,0:T(8,128)(2,1)S(1)} %collective-permute-done.7.refs_7_), channel_id=1, source_target_pairs={{0,16},{16,0},{1,17},{17,1},{2,18},{18,2},{3,19},{19,3},{4,20},{20... | collective-permute-start | bytes 688136 | tf_op jit(solution)/shard_map/ppermute | solution.py:246
  81.1 3.8 %copy-start.4 = (bf16[1,112,2048]{2,1,0:T(8,128)(2,1)S(1)}, bf16[1,112,2048]{2,1,0:T(8,128)(2,1)}, u32[]{:S(2)}) copy-start(bf16[1,112,2048]{2,1,0:T(8,128)(2,1)} %get-tuple-element.25.refs_0_) | copy-start | bytes 1376260
  81.1 3.8 %copy-start.6 = (bf16[1,112,2048]{2,1,0:T(8,128)(2,1)S(1)}, bf16[1,112,2048]{2,1,0:T(8,128)(2,1)}, u32[]{:S(2)}) copy-start(bf16[1,112,2048]{2,1,0:T(8,128)(2,1)} %copy-done.5) | copy-start | bytes 1376260
  81.1 3.8 %copy-start.8 = (bf16[1,112,2048]{2,1,0:T(8,128)(2,1)S(1)}, bf16[1,112,2048]{2,1,0:T(8,128)(2,1)}, u32[]{:S(2)}) copy-start(bf16[1,112,2048]{2,1,0:T(8,128)(2,1)} %copy-done.7) | copy-start | bytes 1376260
  81.1 3.8 %copy-start.10 = (bf16[768,640]{1,0:T(8,128)(2,1)S(1)}, bf16[768,640]{1,0:T(8,128)(2,1)}, u32[]{:S(2)}) copy-start(bf16[768,640]{1,0:T(8,128)(2,1)} %copy-done.9) | copy-start | bytes 2949124
  93.3 8.4 %collective-permute-start.22 = (bf16[2,48,1280]{2,1,0:T(8,128)(2,1)S(1)}, bf16[2,48,1280]{2,1,0:T(8,128)(2,1)S(1)}, u32[]{:S(2)}, u32[]{:S(2)}) collective-permute-start(bf16[2,48,1280]{2,1,0:T(8,128)(2,1)S(1)} %get-tuple-element.41), channel_id=1, source_target_pairs={{0,128},{128,1},{1,129},{129,0},{2,130},{130,3},{3,131},{131,2},{4... | collective-permute-start | bytes 737288 | tf_op jit(solution)/shard_map/ppermute | solution.py:251
  93.9 9.3 %collective-permute-start.24 = (bf16[2,48,1280]{2,1,0:T(8,128)(2,1)S(1)}, bf16[2,48,1280]{2,1,0:T(8,128)(2,1)S(1)}, u32[]{:S(2)}, u32[]{:S(2)}) collective-permute-start(bf16[2,48,1280]{2,1,0:T(8,128)(2,1)S(1)} %get-tuple-element.42), channel_id=1, source_target_pairs={{0,129},{128,0},{1,128},{129,1},{2,131},{130,2},{3,130},{131,3},{4... | collective-permute-start | bytes 737288 | tf_op jit(solution)/shard_map/ppermute | solution.py:251
  95.5 11.3 %collective-permute-start.17 = (bf16[4,48,768]{2,1,0:T(8,128)(2,1)S(1)}, bf16[4,48,768]{2,1,0:T(8,128)(2,1)S(1)}, u32[]{:S(2)}, u32[]{:S(2)}) collective-permute-start(bf16[4,48,768]{2,1,0:T(8,128)(2,1)S(1)} %get-tuple-element.47), channel_id=1, source_target_pairs={{0,32},{32,64},{64,96},{96,0},{1,33},{33,65},{65,97},{97,1},{2,34}... | collective-permute-start | bytes 884744 | tf_op jit(solution)/shard_map/ppermute | solution.py:257
  96.1 16.1 %collective-permute-start.18 = (bf16[4,48,768]{2,1,0:T(8,128)(2,1)S(1)}, bf16[4,48,768]{2,1,0:T(8,128)(2,1)S(1)}, u32[]{:S(2)}, u32[]{:S(2)}) collective-permute-start(bf16[4,48,768]{2,1,0:T(8,128)(2,1)S(1)} %get-tuple-element.46), channel_id=1, source_target_pairs={{0,96},{32,0},{64,32},{96,64},{1,97},{33,1},{65,33},{97,65},{2,98}... | collective-permute-start | bytes 884744 | tf_op jit(solution)/shard_map/ppermute | solution.py:257
  97.6 14.7 %collective-permute-start.16 = (bf16[4,48,768]{2,1,0:T(8,128)(2,1)S(1)}, bf16[4,48,768]{2,1,0:T(8,128)(2,1)S(1)}, u32[]{:S(2)}, u32[]{:S(2)}) collective-permute-start(bf16[4,48,768]{2,1,0:T(8,128)(2,1)S(1)} %get-tuple-element.45), channel_id=1, source_target_pairs={{0,64},{32,96},{64,0},{96,32},{1,65},{33,97},{65,1},{97,33},{2,66}... | collective-permute-start | bytes 884744 | tf_op jit(solution)/shard_map/ppermute | solution.py:257
  103.3 15.8 %collective-permute-start.25 = (bf16[4,48,1280]{2,1,0:T(8,128)(2,1)S(1)}, bf16[4,48,1280]{2,1,0:T(8,128)(2,1)S(1)}, u32[]{:S(2)}, u32[]{:S(2)}) collective-permute-start(bf16[4,48,1280]{2,1,0:T(8,128)(2,1)S(1)} %pad_maximum_fusion.1), channel_id=1, source_target_pairs={{0,129},{128,0},{1,128},{129,1},{2,131},{130,2},{3,130},{131,3},{4... | collective-permute-start | bytes 1474568 | tf_op jit(solution)/shard_map/ppermute | solution.py:251
  103.7 16.0 %collective-permute-start.23 = (bf16[4,48,1280]{2,1,0:T(8,128)(2,1)S(1)}, bf16[4,48,1280]{2,1,0:T(8,128)(2,1)S(1)}, u32[]{:S(2)}, u32[]{:S(2)}) collective-permute-start(bf16[4,48,1280]{2,1,0:T(8,128)(2,1)S(1)} %pad_maximum_fusion), channel_id=1, source_target_pairs={{0,128},{128,1},{1,129},{129,0},{2,130},{130,3},{3,131},{131,2},{4... | collective-permute-start | bytes 1474568 | tf_op jit(solution)/shard_map/ppermute | solution.py:251
  112.4 18.8 %copy-start.2 = (s32[2]{0:T(128)S(1)}, s32[2]{0:T(128)}, u32[]{:S(2)}) copy-start(s32[2]{0:T(128)} %pad_add_fusion.1.at_ref) | copy-start | bytes 28
  112.4 12.7 %collective-permute-start.19 = (bf16[2,48,768]{2,1,0:T(8,128)(2,1)S(1)}, bf16[2,48,768]{2,1,0:T(8,128)(2,1)S(1)}, u32[]{:S(2)}, u32[]{:S(2)}) collective-permute-start(bf16[2,48,768]{2,1,0:T(8,128)(2,1)S(1)} %pad_maximum_fusion.3), channel_id=1, source_target_pairs={{0,128},{128,1},{1,129},{129,0},{2,130},{130,3},{3,131},{131,2},{4... | collective-permute-start | bytes 442376 | tf_op jit(solution)/shard_map/ppermute | solution.py:251
  114.3 10.8 %collective-permute-start.20 = (bf16[2,48,768]{2,1,0:T(8,128)(2,1)S(1)}, bf16[2,48,768]{2,1,0:T(8,128)(2,1)S(1)}, u32[]{:S(2)}, u32[]{:S(2)}) collective-permute-start(bf16[2,48,768]{2,1,0:T(8,128)(2,1)S(1)} %pad_maximum_fusion.4), channel_id=1, source_target_pairs={{0,1},{128,129},{1,0},{129,128},{2,3},{130,131},{3,2},{131,130},{4... | collective-permute-start | bytes 442376 | tf_op jit(solution)/shard_map/ppermute | solution.py:251
  115.5 9.6 %collective-permute-start.21 = (bf16[2,48,768]{2,1,0:T(8,128)(2,1)S(1)}, bf16[2,48,768]{2,1,0:T(8,128)(2,1)S(1)}, u32[]{:S(2)}, u32[]{:S(2)}) collective-permute-start(bf16[2,48,768]{2,1,0:T(8,128)(2,1)S(1)} %pad_maximum_fusion.5), channel_id=1, source_target_pairs={{0,129},{128,0},{1,128},{129,1},{2,131},{130,2},{3,130},{131,3},{4... | collective-permute-start | bytes 442376 | tf_op jit(solution)/shard_map/ppermute | solution.py:251
  119.8 6.5 %collective-permute-start.26 = (bf16[48,1280]{1,0:T(8,128)(2,1)S(1)}, bf16[48,1280]{1,0:T(8,128)(2,1)S(1)}, u32[]{:S(2)}, u32[]{:S(2)}) collective-permute-start(bf16[48,1280]{1,0:T(8,128)(2,1)S(1)} %get-tuple-element.50), channel_id=1, source_target_pairs={{0,64},{32,96},{64,0},{96,32},{1,65},{33,97},{65,1},{97,33},{2,66}... | collective-permute-start | bytes 368648 | tf_op jit(solution)/shard_map/ppermute | solution.py:257
  121.4 6.2 %collective-permute-start.27 = (bf16[48,1280]{1,0:T(8,128)(2,1)S(1)}, bf16[48,1280]{1,0:T(8,128)(2,1)S(1)}, u32[]{:S(2)}, u32[]{:S(2)}) collective-permute-start(bf16[48,1280]{1,0:T(8,128)(2,1)S(1)} %get-tuple-element.49), channel_id=1, source_target_pairs={{0,32},{32,64},{64,96},{96,0},{1,33},{33,65},{65,97},{97,1},{2,34}... | collective-permute-start | bytes 368648 | tf_op jit(solution)/shard_map/ppermute | solution.py:257
  125.1 6.1 %collective-permute-start.28 = (bf16[48,1280]{1,0:T(8,128)(2,1)S(1)}, bf16[48,1280]{1,0:T(8,128)(2,1)S(1)}, u32[]{:S(2)}, u32[]{:S(2)}) collective-permute-start(bf16[48,1280]{1,0:T(8,128)(2,1)S(1)} %get-tuple-element.48), channel_id=1, source_target_pairs={{0,96},{32,0},{64,32},{96,64},{1,97},{33,1},{65,33},{97,65},{2,98}... | collective-permute-start | bytes 368648 | tf_op jit(solution)/shard_map/ppermute | solution.py:257
